TPU v7x, 32 devices: a whole 2x2x4 slice. The times are simulated.
32 devices in a mesh: parts: 2 (over y), wide: 8 (over z, core), narrow: 2 (over x), sub: 1.
Axes of the slice: x: 2, y: 2, z: 4, core: 2. Of those that a mesh axis runs over, the one named last changes fastest.
Arguments:
- modes: float32 [128, 256, 512], P(('parts', 'wide'), None, ('narrow', 'sub')), parts along dimension 0, may hold values from -0.375 to 0.375
- eigvals: float32 [128, 512], P(('parts', 'wide'), ('narrow', 'sub')), parts along dimension 0, may hold values from 1 to 16
- stiff_tiles: float32 [128, 4, 2, 128, 256], P(('parts', 'wide'), 'narrow'), parts along dimension 0, may hold values from -0.18 to 0.18
- mass_tiles: float32 [128, 4, 2, 128, 256], P(('parts', 'wide'), 'narrow'), parts along dimension 0, may hold values from -0.18 to 0.18
- row_blocks: int32 [128, 4, 2], P(('parts', 'wide'), 'narrow'), parts along dimension 0, may hold values from 0 to 1
- adjacency: int32 [128, 4], P(('parts', 'wide')), parts along dimension 0, may hold values from 0 to 7, all different within a row; in each aligned block of 8 rows (0 to 7, 8 to 15, ...) at most 4 rows name the same one
- iface_stiff: float32 [16, 256, 256], P(('parts', 'wide'), ('narrow', 'sub')), parts along dimension 0, may hold values from -6 to 6
- iface_mass: float32 [16, 256, 256], P(('parts', 'wide'), ('narrow', 'sub')), parts along dimension 0, may hold values from -6 to 6
Outputs:
- reduced_stiff: float32 [16, 256, 256], P(('parts', 'wide'), ('narrow', 'sub')), parts along dimension 0
- reduced_mass: float32 [16, 256, 256], P(('parts', 'wide'), ('narrow', 'sub')), parts along dimension 0
There are 2 independent parts, one for each index of `parts`. A program takes and returns all parts, laid end to end along the dimension named above; each array names one. Nothing has to cross between parts.
Inputs may be any that keep to these rules, and one draw needn't show every extreme that they name: `adjacency`: each row names 4 different interfaces. Within the rows of one index of wide (8 substructures in a row), no interface is named more than 4 times, a bound that some block reaches.
All inputs are finite; a program needn't handle non-finite values.
Results may differ from a plain program's by a relative error of at most 0.0001.
Values sent between devices are 32-bit elements; how exact they have to be, the bound alone decides.
No kernel may reach another device: no remote copies, remote signals or barrier semaphores. Data moves between devices by JAX's collectives and lax.ppermute only.
A program may use at most 128 MiB of HBM per device.

v0:
```python
import jax
import jax.numpy as jnp
from jax import lax
from jax.sharding import PartitionSpec as P

ROWT = 128


highest = lax.Precision.HIGHEST


def chosen_rows(modal, blocks):
    subs = modal.shape[0]
    tiled = modal.reshape(subs, -1, ROWT, modal.shape[2])
    which = jnp.arange(subs)[:, None, None]
    return tiled[which, blocks]


def project(modal, stiff, mass, blocks):
    chosen = chosen_rows(modal, blocks)
    proj_stiff = jnp.einsum(
        "sjtrm,sjtrc->sjmc", chosen, stiff, precision=highest, preferred_element_type=jnp.float32
    )
    proj_mass = jnp.einsum(
        "sjtrm,sjtrc->sjmc", chosen, mass, precision=highest, preferred_element_type=jnp.float32
    )
    return jnp.stack([proj_stiff, proj_mass], 0)


def per_device(
    modes, eigvals, stiff_tiles, mass_tiles, row_blocks, adjacency, iface_stiff, iface_mass
):
    inverse = 1.0 / eigvals
    subs = modes.shape[0]
    mode_part = modes.shape[2]
    width = stiff_tiles.shape[4]
    adj_total = adjacency.shape[1]
    partial_blocks = project(
        lax.all_gather(modes, "narrow", axis=2, tiled=True), stiff_tiles, mass_tiles, row_blocks
    )
    projected = lax.all_to_all(partial_blocks, "narrow", split_axis=3, concat_axis=2, tiled=True)
    n_wide = lax.axis_size("wide")
    block_count = subs * adj_total
    capacity = max(2, (block_count + n_wide - 1) // n_wide)
    owners = adjacency.reshape(block_count)
    positions = jnp.arange(block_count)
    earlier = (owners[:, None] == owners[None, :]) & (positions[:, None] > positions[None, :])
    ranking = jnp.sum(earlier.astype(jnp.int32), axis=1)
    slot_index = owners * capacity + ranking
    placing = (slot_index[None, :] == jnp.arange(n_wide * capacity)[:, None]).astype(jnp.float32)
    flat_blocks = projected.reshape(2, block_count, mode_part * width)
    send_blocks = jnp.einsum(
        "pb,kbx->kpx", placing, flat_blocks, precision=highest, preferred_element_type=jnp.float32
    )
    send_blocks = send_blocks.reshape(2, n_wide, capacity, mode_part, width)
    block_inverse = jnp.broadcast_to(inverse[:, None, :], (subs, adj_total, mode_part)).reshape(
        block_count, mode_part
    )
    send_inverse = jnp.dot(
        placing, block_inverse, precision=highest, preferred_element_type=jnp.float32
    )
    send_inverse = send_inverse.reshape(1, n_wide, capacity, mode_part)
    got_blocks, got_inverse = (
        lax.all_to_all(send_blocks, "wide", split_axis=1, concat_axis=1, tiled=True),
        lax.all_to_all(send_inverse, "wide", split_axis=1, concat_axis=1, tiled=True),
    )
    recv_stiff = got_blocks[0].reshape(-1, width)
    recv_mass = got_blocks[1].reshape(-1, width)
    weight_one = got_inverse.reshape(-1)[:, None]
    part_stiff = jnp.einsum(
        "rc,rd->cd",
        recv_stiff,
        weight_one * recv_stiff,
        precision=highest,
        preferred_element_type=jnp.float32,
    )
    cross = jnp.einsum(
        "rc,rd->cd",
        recv_stiff,
        weight_one * recv_mass,
        precision=highest,
        preferred_element_type=jnp.float32,
    )
    second = jnp.einsum(
        "rc,rd->cd",
        recv_stiff,
        weight_one * weight_one * recv_stiff,
        precision=highest,
        preferred_element_type=jnp.float32,
    )
    part_mass = second - cross - cross.T
    sum_stiff, sum_mass = (
        lax.psum_scatter(part_stiff, ("narrow", "sub"), scatter_dimension=0, tiled=True),
        lax.psum_scatter(part_mass, ("narrow", "sub"), scatter_dimension=0, tiled=True),
    )
    return (iface_stiff - sum_stiff[None], iface_mass + sum_mass[None])


def solution(mesh):
    return jax.shard_map(
        per_device,
        mesh=mesh,
        in_specs=(
            P(("parts", "wide"), None, ("narrow", "sub")),
            P(("parts", "wide"), ("narrow", "sub")),
            P(("parts", "wide"), "narrow", None, None, None),
            P(("parts", "wide"), "narrow", None, None, None),
            P(("parts", "wide"), "narrow", None),
            P(("parts", "wide"), None),
            P(("parts", "wide"), ("narrow", "sub"), None),
            P(("parts", "wide"), ("narrow", "sub"), None),
        ),
        out_specs=(
            P(("parts", "wide"), ("narrow", "sub"), None),
            P(("parts", "wide"), ("narrow", "sub"), None),
        ),
        check_vma=False,
    )
```

profile of v0, /device:TPU:0, one launch (start us, length us, event | category | flops | bytes accessed | tf_op | source)
XLA Modules:
  0.0 866.5 jit_solution(17411420882966839069)
XLA Ops:
  7.2 0.0 all-gather.2.cloned.1.call-start
  7.2 0.7 all-gather.2.cloned.1.call-update
  7.9 0.7 fusion.55
  8.6 0.1 copy.45
  8.7 0.1 reshape.109
  8.8 60.2 %all-gather.2.cloned.1.call-done = f32[8,256,512]{2,1,0:T(8,128)} async-done(((f32[8,256,256]{2,1,0:T(8,128)}), f32[8,256,512]{2,1,0:T(8,128)}) %all-gather.2.cloned.1.call-update) | async-done | bytes 4194320 | tf_op jit(solution)/shard_map/all_gather | solution.py:39
  69.0 6.5 gather_fusion
  75.5 0.0 copy-start
  75.5 19.6 %convolution_bitcast_fusion = f32[1,8,2,512,256]{4,3,2,1,0:T(8,128)} fusion(f32[8,2,2,128,512]{4,3,2,1,0:T(8,128)} %bitcast.127, f32[8,2,2,128,256]{4,3,2,1,0:T(8,128)} %param.11), kind=kOutput, calls=%fused_computation.22 | convolution fusion | flops 6442450944 | bytes 20971520 | tf_op jit(solution)/shard_map/sjtrm,sjtrc->sjmc/dot_general | solution.py:24
  95.1 0.0 copy-done
  95.1 0.0 copy-done.1
  95.1 15.7 %convolution_bitcast_fusion.1 = f32[1,8,2,512,256]{4,3,2,1,0:T(8,128)} fusion(f32[8,2,2,128,512]{4,3,2,1,0:T(8,128)S(1)} %bitcast.128, f32[8,2,2,128,256]{4,3,2,1,0:T(8,128)S(1)} %copy-done.1), kind=kOutput, calls=%fused_computation.23 | convolution fusion | flops 6442450944 | bytes 20971520 | tf_op jit(solution)/shard_map/sjtrm,sjtrc->sjmc/dot_general | solution.py:21
  110.8 6.9 pad_maximum_fusion
  117.7 19.4 %copy.47 = f32[2,8,2,512,256]{4,2,1,0,3:T(2,128)} copy(f32[2,8,2,512,256]{4,3,2,1,0:T(8,128)S(1)} %pad_maximum_fusion) | data formatting | bytes 33554432 | tf_op jit(solution)/shard_map/stack | solution.py:27
  137.2 9.8 %all-to-all-start = ((f32[2,8,2,512,256]{4,2,1,0,3:T(2,128)}), f32[2,8,2,512,256]{4,2,1,0,3:T(2,128)}, u32[]{:S(2)}, u32[]{:S(2)}) async-start(f32[2,8,2,512,256]{4,2,1,0,3:T(2,128)} %copy.47), calls=%async_computation | async-start | bytes 33554432 | tf_op jit(solution)/shard_map/all_to_all | solution.py:41
  147.0 0.0 copy-done.5
  147.0 0.1 copy.49
  147.1 0.1 reshape.102
  147.2 0.0 copy-done.4
  147.2 0.2 convert_reduce_fusion
  147.4 0.2 convolution_bitcast_fusion.2
  147.6 0.6 copy.52
  148.2 181.2 %all-to-all-done = f32[2,8,2,512,256]{4,2,1,0,3:T(2,128)} async-done(((f32[2,8,2,512,256]{4,2,1,0,3:T(2,128)}), f32[2,8,2,512,256]{4,2,1,0,3:T(2,128)}, u32[]{:S(2)}, u32[]{:S(2)}) %all-to-all-start) | async-done | bytes 16777248 | tf_op jit(solution)/shard_map/all_to_all | solution.py:41
  329.5 4.9 all-to-all-start.2
  334.4 15.9 %copy.70 = f32[2,8,2,2,256,256]{5,4,2,3,1,0:T(8,128)} copy(f32[2,8,2,2,256,256]{5,2,1,0,4,3:T(2,128)} %bitcast.9) | data formatting | bytes 33554432 | tf_op jit(solution)/shard_map/all_to_all | solution.py:41
  350.3 14.5 %reshape.101 = f32[2,32,65536]{2,1,0:T(8,128)} reshape(f32[2,8,2,2,256,256]{5,4,3,2,1,0:T(8,128)} %bitcast.130) | data formatting | bytes 33554432 | tf_op jit(solution)/shard_map/reshape | solution.py:51
  364.8 14.9 %fusion.46 = f32[2,65536,32]{1,2,0:T(8,128)} fusion(f32[2,32,65536]{2,1,0:T(8,128)} %reshape.101, s32[32]{0:T(128)S(1)} %multiply_add_fusion.1), kind=kOutput, calls=%fused_computation.37 | convolution fusion | flops 1610613760 | bytes 33554560 | tf_op jit(solution)/shard_map/pb,kbx->kpx/dot_general | solution.py:52
  379.7 15.8 %copy.68 = f32[8,8,256,256]{3,2,1,0:T(8,128)} copy(f32[8,8,256,256]{3,1,2,0:T(8,128)} %bitcast.129) | data formatting | bytes 33554432
  395.4 17.4 %copy.50 = f32[2,8,4,256,256]{3,4,2,0,1:T(8,128)} copy(f32[2,8,4,256,256]{4,3,2,1,0:T(8,128)} %bitcast.131) | data formatting | bytes 33554432 | tf_op jit(solution)/shard_map/reshape | solution.py:55
  412.8 0.0 all-to-all-done.2
  412.8 5.7 all-to-all-start.1
  418.6 0.0 reduce-scatter.5.cloned.1.call-start
  418.6 363.6 %all-to-all-done.1 = f32[2,8,4,256,256]{3,4,2,0,1:T(8,128)} async-done(((f32[2,8,4,256,256]{3,4,2,0,1:T(8,128)}), f32[2,8,4,256,256]{3,4,2,0,1:T(8,128)}, u32[]{:S(2)}, u32[]{:S(2)}) %all-to-all-start.1) | async-done | bytes 16777248 | tf_op jit(solution)/shard_map/all_to_all | solution.py:64
  782.2 21.7 %fusion.29 = f32[256,256]{1,0:T(8,128)S(1)} fusion(f32[2,8,4,256,256]{3,4,2,0,1:T(8,128)} %all-to-all-done.1, f32[8,4,256]{2,1,0:T(4,128)S(1)} %bitcast.133), kind=kOutput, calls=%fused_computation.26 | convolution fusion | flops 6444548096 | bytes 17072128 | tf_op jit(solution)/shard_map/rc,rd->cd/dot_general | solution.py:77
  803.9 0.1 copy.57
  804.1 22.1 %fusion.39 = f32[256,256]{1,0:T(8,128)} fusion(f32[256,256]{1,0:T(8,128)S(1)} %fusion.29, f32[2,8,4,256,256]{3,4,2,0,1:T(8,128)} %all-to-all-done.1, f32[8,4,256]{2,1,0:T(4,128)S(1)} %bitcast_multiply_fusion.2, f32[256,256]{0,1:T(8,128)S(1)} %copy.57), kind=kOutput, calls=%fused_computation.28 | convolution fusion | flops 6444679168 | bytes 17596416 | tf_op jit(solution)/shard_map/rc,rd->cd/dot_general | solution.py:84
  826.2 0.0 reduce-scatter.5.cloned.1.call-update
  826.2 0.0 copy-start.2
  826.2 0.0 copy-start.3
  826.2 0.0 reduce-scatter.3.cloned.1.call-start
  826.3 22.2 %fusion.19 = f32[256,256]{1,0:T(8,128)} fusion(f32[2,8,4,256,256]{3,4,2,0,1:T(8,128)} %all-to-all-done.1, f32[8,4,256]{2,1,0:T(4,128)S(1)} %bitcast.134), kind=kOutput, calls=%fused_computation.24 | convolution fusion | flops 6444548096 | bytes 17072128 | tf_op jit(solution)/shard_map/rc,rd->cd/dot_general | solution.py:70
  848.5 0.0 reduce-scatter.3.cloned.1.call-update
  848.5 0.0 reduce-scatter.5.cloned.1.call-done
  848.5 0.0 copy-done.2
  848.5 1.6 bitcast_add_fusion
  850.1 8.0 reduce-scatter.3.cloned.1.call-done
  858.1 0.0 copy-done.3
  858.1 1.6 bitcast_subtract_fusion
  (9 shorter events, 0.1 us)
Async XLA Ops:
  7.2 61.9 %all-gather.2.cloned.1.call-start = ((), (), s32[]{:S(2)}) async-start(), calls=%async_computation.5 | async-start | bytes 6291456 | tf_op jit(solution)/shard_map/all_gather | solution.py:39
  75.5 19.6 %copy-start = (f32[32,128,512]{2,1,0:T(8,128)S(1)}, f32[32,128,512]{2,1,0:T(8,128)}, u32[]{:S(2)}) copy-start(f32[32,128,512]{2,1,0:T(8,128)} %gather_fusion) | copy-start | bytes 25165828
  75.5 19.6 %copy-start.1 = (f32[8,2,2,128,256]{4,3,2,1,0:T(8,128)S(1)}, f32[8,2,2,128,256]{4,3,2,1,0:T(8,128)}, u32[]{:S(2)}) copy-start(f32[8,2,2,128,256]{4,3,2,1,0:T(8,128)} %param.10) | copy-start | bytes 12582916
  137.2 9.8 %copy-start.5 = (s32[8,4]{0,1:T(4,128)S(1)}, s32[8,4]{0,1:T(4,128)}, u32[]{:S(2)}) copy-start(s32[8,4]{0,1:T(4,128)} %param.13) | copy-start | bytes 388
  137.2 10.0 %copy-start.4 = (f32[8,256]{1,0:T(8,128)S(1)}, f32[8,256]{1,0:T(8,128)}, u32[]{:S(2)}) copy-start(f32[8,256]{1,0:T(8,128)} %param.9) | copy-start | bytes 24580
  137.2 192.3 %all-to-all-start = ((f32[2,8,2,512,256]{4,2,1,0,3:T(2,128)}), f32[2,8,2,512,256]{4,2,1,0,3:T(2,128)}, u32[]{:S(2)}, u32[]{:S(2)}) async-start(f32[2,8,2,512,256]{4,2,1,0,3:T(2,128)} %copy.47), calls=%async_computation | async-start | bytes 33554432 | tf_op jit(solution)/shard_map/all_to_all | solution.py:41
  329.5 83.4 %all-to-all-start.2 = ((f32[1,8,4,256]{3,2,0,1:T(4,128)}), f32[1,8,4,256]{3,2,0,1:T(4,128)S(1)}, u32[]{:S(2)}, u32[]{:S(2)}) async-start(f32[1,8,4,256]{3,2,0,1:T(4,128)} %copy.52), calls=%async_computation.2 | async-start | bytes 65536 | tf_op jit(solution)/shard_map/all_to_all | solution.py:65
  412.8 369.4 %all-to-all-start.1 = ((f32[2,8,4,256,256]{3,4,2,0,1:T(8,128)}), f32[2,8,4,256,256]{3,4,2,0,1:T(8,128)}, u32[]{:S(2)}, u32[]{:S(2)}) async-start(f32[2,8,4,256,256]{3,4,2,0,1:T(8,128)} %copy.50), calls=%async_computation.1 | async-start | bytes 33554432 | tf_op jit(solution)/shard_map/all_to_all | solution.py:64
  418.6 429.9 %reduce-scatter.5.cloned.1.call-start = ((), (), s32[]{:S(2)}) async-start(), calls=%async_computation.7 | async-start | bytes 393216 | tf_op jit(solution)/shard_map/reduce_scatter | solution.py:94
  826.2 22.3 %copy-start.2 = (f32[1,128,256]{2,1,0:T(8,128)S(1)}, f32[1,128,256]{2,1,0:T(8,128)}, u32[]{:S(2)}) copy-start(f32[1,128,256]{2,1,0:T(8,128)} %param.15) | copy-start | bytes 393220
  826.2 31.9 %copy-start.3 = (f32[1,128,256]{2,1,0:T(8,128)S(1)}, f32[1,128,256]{2,1,0:T(8,128)}, u32[]{:S(2)}) copy-start(f32[1,128,256]{2,1,0:T(8,128)} %param.14) | copy-start | bytes 393220
  826.2 31.9 %reduce-scatter.3.cloned.1.call-start = ((), (), s32[]{:S(2)}) async-start(), calls=%async_computation.6 | async-start | bytes 393216 | tf_op jit(solution)/shard_map/reduce_scatter | solution.py:93
Sparse Core Ops, SparseCore 0:
  9.5 59.4 all-gather.1
  826.3 9.5 reduce-scatter.4
  848.6 9.4 reduce-scatter.2
where the time goes:
time: 874 us; the launch traced here: 866 us
  waiting for transfers between devices  614 us (70%)
  matrix products  116 us (13%)
  local copies, waits for them, and re-layouts  90.7 us (10%)
  starting transfers between devices  20.5 us (2%)
  between operations  14.1 us (2%)
  other arithmetic  11 us (1%)
    all_to_all x1, waiting for transfers between devices, per_device(): lax.all_to_all(send_blocks, 'wide', split_axis=1, concat_axis=1, tiled=True)  364 us
    all_to_all x1, waiting for transfers between devices, per_device(): lax.all_to_all(partial_blocks, 'narrow', split_axis=3, concat_axis=2, til...  181 us
    all_gather x1, waiting for transfers between devices, per_device(): lax.all_gather(modes, 'narrow', axis=2, tiled=True)  60.2 us
    dot_general x1, matrix products, per_device(): jnp.einsum('rc,rd->cd', recv_stiff, weight_one * recv_stiff, precision=hi...  22.2 us
    dot_general x1, matrix products, per_device(): jnp.einsum('rc,rd->cd', recv_stiff, weight_one * weight_one * recv_stiff,...  22.1 us
    dot_general x1, matrix products, per_device(): jnp.einsum('rc,rd->cd', recv_stiff, weight_one * recv_mass, precision=hig...  21.7 us
    dot_general x1, matrix products, project(): jnp.einsum('sjtrm,sjtrc->sjmc', chosen, mass, precision=highest, preferre...  19.6 us
    another operation x1, local copies, waits for them, and re-layouts, project(): return jnp.stack([proj_stiff, proj_mass], 0)  19.4 us
  transfers between devices with their start and end apart: 6, of which 4 were waited for; matrix products, arithmetic and copies ran while one was open for 12% of the time, Pallas kernels for 0%

commit v1 on v0

v1 whole, which is shorter than its diff:
```python
import functools

import jax
import jax.numpy as jnp
from jax import lax
from jax.experimental import pallas as pl
from jax.experimental.pallas import tpu as pltpu
from jax.sharding import PartitionSpec as P

ROWT = 128
LANES = 128
GROUP = 8
FIRST = 4
LAST = 1
VMEM_LIMIT = 56 * 1024 * 1024

f32 = jnp.float32
bf16 = jnp.bfloat16


def split(x):
    high = x.astype(bf16)
    return high, (x - high.astype(f32)).astype(bf16)


def product(a, b, a_dim, b_dim):
    def one(x, y):
        return lax.dot_general(
            x, y, (((a_dim,), (b_dim,)), ((), ())), preferred_element_type=f32
        )

    return one(a[0], b[0]) + (one(a[0], b[1]) + one(a[1], b[0]))


def stacked(a, b, axis):
    return tuple(jnp.concatenate(pair, axis) for pair in zip(a, b, strict=True))


def full_rows(tiles_ref, slot, blocks_ref, sub, row_tiles):
    tiles = tiles_ref.shape[2]
    rows = []
    for r in range(row_tiles):
        total = None
        for t in range(tiles):
            here = (blocks_ref[sub, slot, t] == r).astype(f32)
            term = tiles_ref[0, slot, t] * here
            total = term if total is None else total + term
        rows.append(total)
    return jnp.concatenate(rows, 0)


def add_substructure(
    sub, mode_refs, eig_refs, stiff_ref, mass_ref, blocks_ref, adjacency_ref, first_slot, acc_ref
):
    gram = None
    for modes_ref, eig_ref in zip(mode_refs, eig_refs, strict=True):
        phi = modes_ref[...]
        inverse = 1.0 / eig_ref[pl.ds(sub, 1), :]
        once = phi * inverse
        twice = once * inverse
        term = product(stacked(split(once), split(twice), 0), split(phi), 1, 1)
        gram = term if gram is None else gram + term
    rows = gram.shape[1]
    gram = split(jnp.concatenate([gram[:rows], 0.5 * gram[rows:]], 0))
    gram_one = (gram[0][:rows], gram[1][:rows])
    for slot in range(stiff_ref.shape[1]):
        stiff = split(full_rows(stiff_ref, slot, blocks_ref, sub, rows // ROWT))
        mass = split(full_rows(mass_ref, slot, blocks_ref, sub, rows // ROWT))
        both = product(gram, stiff, 1, 0)
        cross = product(gram_one, mass, 1, 0)
        right = stacked(split(both[:rows]), split(both[rows:] - cross), 1)
        owner = adjacency_ref[sub, first_slot + slot]
        acc_ref[owner] += product(stiff, right, 0, 0)


def sum_kernel(n_parts, start, has_acc, info, blocks, adjacency, *refs):
    mode_refs, eig_refs = refs[:n_parts], refs[n_parts : 2 * n_parts]
    stiff_ref, mass_ref = refs[2 * n_parts : 2 * n_parts + 2]
    acc_in = refs[2 * n_parts + 2] if has_acc else None
    acc_ref = refs[-1]

    @pl.when(pl.program_id(0) == 0)
    def _():
        acc_ref[...] = acc_in[...] if has_acc else jnp.zeros_like(acc_ref)

    add_substructure(
        pl.program_id(0) + start,
        mode_refs,
        eig_refs,
        stiff_ref,
        mass_ref,
        blocks,
        adjacency,
        info[0] * stiff_ref.shape[1],
        acc_ref,
    )


def pack_interface(acc_ref, owner, out_ref, place):
    half = ROWT // 2
    row = lax.broadcasted_iota(jnp.int32, (ROWT, ROWT), 0)
    col = lax.broadcasted_iota(jnp.int32, (ROWT, ROWT), 1)
    low, mid = slice(0, ROWT), slice(ROWT, 2 * ROWT)
    diagonals = []
    for which in range(2):
        base = which * 2 * ROWT
        lanes_low, lanes_mid = slice(base, base + ROWT), slice(base + ROWT, base + 2 * ROWT)
        first, second = acc_ref[owner, low, lanes_low], acc_ref[owner, mid, lanes_mid]
        corner = acc_ref[owner, mid, lanes_low]
        square = jnp.where(row > col, first, second)
        diagonal = jnp.sum(jnp.where(row == col, first, 0.0), axis=0, keepdims=True)
        if which == 1:
            corner = corner + acc_ref[owner, low, lanes_mid].T
            square = square + jnp.where(row < col, first, second).T
            diagonal = diagonal + diagonal
        diagonals.append(diagonal)
        for part in range(2):
            rows = slice(part * half, (part + 1) * half)
            out_ref[part, place, which * half : (which + 1) * half, :LANES] = corner[rows]
            out_ref[part, place, which * half : (which + 1) * half, LANES:] = square[rows]
    extra = jnp.broadcast_to(jnp.concatenate(diagonals, 1), (GROUP, 2 * LANES))
    for part in range(2):
        out_ref[part, place, 2 * half :, :] = extra


def last_kernel(n_parts, start, count, info, blocks, adjacency, *refs):
    mode_refs, eig_refs = refs[:n_parts], refs[n_parts : 2 * n_parts]
    stiff_ref, mass_ref, acc_in, send_ref, keep_ref, acc_ref = refs[2 * n_parts :]

    @pl.when(pl.program_id(0) == 0)
    def _():
        acc_ref[...] = acc_in[...]

    add_substructure(
        pl.program_id(0) + start,
        mode_refs,
        eig_refs,
        stiff_ref,
        mass_ref,
        blocks,
        adjacency,
        info[0] * stiff_ref.shape[1],
        acc_ref,
    )

    @pl.when(pl.program_id(0) == count - 1)
    def _():
        chips = send_ref.shape[1]
        chip, core = info[1], info[2]
        for shift in range(chips):
            target = lax.rem(chip + shift, chips) * 2
            pack_interface(acc_ref, target + 1 - core, send_ref, shift)
            pack_interface(acc_ref, target + core, keep_ref, shift)


def sums_of(info, blocks, adjacency, parts, eigs, stiff, mass, start, count, ifaces, acc=None, chips=0):
    subs, slots, tiles, rowt, width = stiff.shape
    n_parts = len(parts)
    rows = parts[0][2]
    scalars = pl.BlockSpec(memory_space=pltpu.SMEM)
    in_specs = [scalars] * 3
    operands = [info, blocks, adjacency]
    for array, first, height in parts:
        in_specs.append(
            pl.BlockSpec(
                (height, array.shape[1]), functools.partial(lambda o, i: (i + o, 0), start - first)
            )
        )
        operands.append(array)
    for array, place in eigs:
        in_specs.append(
            pl.BlockSpec((subs, array.shape[1]), functools.partial(lambda o, i: (o, 0), place))
        )
        operands.append(array)
    for array in (stiff, mass):
        in_specs.append(
            pl.BlockSpec((1, slots, tiles, rowt, width), lambda i: (i + start, 0, 0, 0, 0))
        )
        operands.append(array)
    acc_shape = (ifaces, width, 2 * width)
    if acc is not None:
        in_specs.append(
            pl.BlockSpec(acc_shape, lambda i: (0, 0, 0), pipeline_mode=pl.Buffered(1))
        )
        operands.append(acc)
    if chips:
        kernel = functools.partial(last_kernel, n_parts, start, count)
        packed = (2, chips, ROWT + GROUP, 2 * LANES)
        out_shape = (jax.ShapeDtypeStruct(packed, f32),) * 2
        out_specs = (pl.BlockSpec(packed, lambda i: (0, 0, 0, 0)),) * 2
        scratch = [pltpu.VMEM(acc_shape, f32)]
    else:
        kernel = functools.partial(sum_kernel, n_parts, start, acc is not None)
        out_shape = jax.ShapeDtypeStruct(acc_shape, f32)
        out_specs = pl.BlockSpec(acc_shape, lambda i: (0, 0, 0))
        scratch = []
    modes_held = sum(array.shape[1] for array, _, _ in parts)
    flops = 6 * count * (2 * rows * rows * modes_held + 5 * slots * rows * rows * width)
    moved = 4 * (count * (rows * modes_held + 2 * slots * tiles * rowt * width))
    moved = moved + 8 * ifaces * width * 2 * width
    return pl.pallas_call(
        kernel,
        grid=(count,),
        in_specs=in_specs,
        out_specs=out_specs,
        out_shape=out_shape,
        scratch_shapes=scratch,
        compiler_params=pltpu.CompilerParams(vmem_limit_bytes=VMEM_LIMIT),
        cost_estimate=pl.CostEstimate(flops=flops, bytes_accessed=moved, transcendentals=0),
    )(*operands)


def unpack_kernel(info, mine, theirs, stiff_ref, mass_ref, out_stiff, out_mass):
    half = ROWT // 2
    side = info[0]
    row = lax.broadcasted_iota(jnp.int32, (ROWT, ROWT), 0)
    col = lax.broadcasted_iota(jnp.int32, (ROWT, ROWT), 1)
    a, b = mine[...], theirs[...]
    upper = jnp.where(side == 0, a, b)
    lower = jnp.where(side == 0, b, a)
    for which, (iface_ref, out_ref) in enumerate(((stiff_ref, out_stiff), (mass_ref, out_mass))):
        sign = -1.0 if which == 0 else 1.0
        rows = slice(which * half, (which + 1) * half)
        packed = jnp.concatenate([upper[rows], lower[rows]], 0)
        corner, square = packed[:, :LANES], packed[:, LANES:]
        diagonal = upper[2 * half : 2 * half + 1, which * LANES : (which + 1) * LANES]
        flipped = square.T

        @pl.when(side == 0)
        def _():
            first = jnp.where(row > col, square, jnp.where(row == col, diagonal, flipped))
            out_ref[0, :, :LANES] = iface_ref[0, :, :LANES] + sign * first
            out_ref[0, :, LANES:] = iface_ref[0, :, LANES:] + sign * corner.T

        @pl.when(side != 0)
        def _():
            second = jnp.where(row <= col, square, flipped)
            out_ref[0, :, :LANES] = iface_ref[0, :, :LANES] + sign * corner
            out_ref[0, :, LANES:] = iface_ref[0, :, LANES:] + sign * second


def unpack(info, mine, theirs, iface_stiff, iface_mass):
    scalars = pl.BlockSpec(memory_space=pltpu.SMEM)
    whole = pl.BlockSpec(memory_space=pltpu.VMEM)
    return pl.pallas_call(
        unpack_kernel,
        in_specs=[scalars] + [whole] * 4,
        out_specs=(whole, whole),
        out_shape=(jax.ShapeDtypeStruct(iface_stiff.shape, f32),) * 2,
        compiler_params=pltpu.CompilerParams(vmem_limit_bytes=VMEM_LIMIT),
    )(info, mine, theirs, iface_stiff, iface_mass)


def paired(modes, eigvals, stiff, mass, blocks, adjacency, iface_stiff, iface_mass):
    subs, rows, held = modes.shape
    n_wide = lax.axis_size("wide")
    chips = n_wide // 2
    side, wide = lax.axis_index("narrow"), lax.axis_index("wide")
    info = jnp.stack([side, wide // 2, wide % 2]).astype(jnp.int32)
    flat = modes.reshape(subs * rows, held)
    swap = [(0, 1), (1, 0)]

    last = min(LAST, subs - 1)
    first = min(FIRST, subs - last)
    cuts = sorted({0, first, subs - last, subs})
    arrived = []
    for begin, end in zip(cuts[:-1], cuts[1:], strict=True):
        piece = flat[begin * rows : end * rows]
        if begin == 0:
            piece = jnp.concatenate([piece, eigvals], 0)
        else:
            piece, _ = lax.optimization_barrier((piece, arrived[-1][0]))
        arrived.append((lax.ppermute(piece, "narrow", swap), begin, end))
    eigs = [(eigvals, 0), (arrived[0][0], first * rows // subs)]
    acc = None
    for piece, begin, end in arrived:
        acc = sums_of(
            info,
            blocks,
            adjacency,
            [(flat, 0, rows), (piece, begin, rows)],
            eigs,
            stiff,
            mass,
            begin,
            end - begin,
            n_wide,
            acc,
            chips if end == subs else 0,
        )
    send, keep = acc

    def other(x, i):
        return lax.dynamic_index_in_dim(x, i, 0, keepdims=False)

    got = lax.ppermute(send, "wide", [(i, i ^ 1) for i in range(n_wide)])
    away = other(keep, 1 - side) + other(got, 1 - side)
    came = lax.ppermute(away, "narrow", swap)
    here = other(keep, side) + other(got, side)
    total = here[0] + came[0]
    for shift in range(1, chips):
        ring = [(i, (i + 2 * shift) % n_wide) for i in range(n_wide)]
        total = total + lax.ppermute(here[shift] + came[shift], "wide", ring)
    return unpack(info, total, lax.ppermute(total, "narrow", swap), iface_stiff, iface_mass)


def grouped(modes, eigvals, stiff, mass, blocks, adjacency, iface_stiff, iface_mass):
    subs, rows, _ = modes.shape
    width = stiff.shape[4]
    n_wide = lax.axis_size("wide")
    info = jnp.stack([lax.axis_index("narrow")] * 3).astype(jnp.int32)
    modes = lax.all_gather(modes, "narrow", axis=2, tiled=True)
    eigvals = lax.all_gather(eigvals, "narrow", axis=1, tiled=True)
    flat = modes.reshape(subs * rows, modes.shape[2])
    acc = sums_of(
        info, blocks, adjacency, [(flat, 0, rows)], [(eigvals, 0)], stiff, mass, 0, subs, n_wide
    )
    half = acc[:, :, width:]
    part = jnp.concatenate([acc[:, :, :width], half + jnp.swapaxes(half, 1, 2)], 2)
    part = lax.psum_scatter(part, "wide", scatter_dimension=0, tiled=True)
    part = lax.psum_scatter(part, ("narrow", "sub"), scatter_dimension=1, tiled=True)
    return iface_stiff - part[:, :, :width], iface_mass + part[:, :, width:]


def solution(mesh):
    pairs = mesh.shape["narrow"] == 2 and mesh.shape["sub"] == 1 and mesh.shape["wide"] % 2 == 0
    return jax.shard_map(
        paired if pairs else grouped,
        mesh=mesh,
        in_specs=(
            P(("parts", "wide"), None, ("narrow", "sub")),
            P(("parts", "wide"), ("narrow", "sub")),
            P(("parts", "wide"), "narrow", None, None, None),
            P(("parts", "wide"), "narrow", None, None, None),
            P(("parts", "wide"), "narrow", None),
            P(("parts", "wide"), None),
            P(("parts", "wide"), ("narrow", "sub"), None),
            P(("parts", "wide"), ("narrow", "sub"), None),
        ),
        out_specs=(
            P(("parts", "wide"), ("narrow", "sub"), None),
            P(("parts", "wide"), ("narrow", "sub"), None),
        ),
        check_vma=False,
    )
```

time: 874 us -> 112 us (0.13)
  waiting for transfers between devices: 614 us -> 53.1 us
  matrix products: 116 us -> 0 us
  local copies, waits for them, and re-layouts: 90.7 us -> 5.02 us
  Pallas kernels: 0 us -> 36.6 us
  between operations: 14.1 us -> 0.72 us
    all_to_all x3 -> x0, waiting for transfers between devices: 545 us -> none  [the longest x1 364 us: per_device(): lax.all_to_all(send_blocks, 'wide', split_axis=1, concat_axis=1, tiled=True)]
    dot_general x7 -> x0, matrix products: 116 us -> none  [the longest x1 22.2 us: per_device(): jnp.einsum('rc,rd->cd', recv_stiff, weight_one * recv_stiff, precision=hi...]
    all_gather x1 -> x0, waiting for transfers between devices: 60.2 us -> none  [per_device(): lax.all_gather(modes, 'narrow', axis=2, tiled=True)]
    ppermute x0 -> x9, waiting for transfers between devices: none -> 53.1 us  [the longest x3 23.8 us: paired(): arrived.append((lax.ppermute(piece, 'narrow', swap), begin, end))]
    pallas_call x0 -> x4, Pallas kernels: none -> 36.6 us  [the longest x3 34.3 us: sums_of(): pl.pallas_call(kernel, grid=(count,), in_specs=in_specs, out_specs=out_sp...]
    reshape x4 -> x0, local copies, waits for them, and re-layouts: 32 us -> none  [the longest x1 17.4 us: per_device(): send_blocks = send_blocks.reshape(2, n_wide, capacity, mode_part, width)]
    all_to_all x3 -> x0, starting transfers between devices: 20.4 us -> none  [the longest x1 9.8 us: per_device(): lax.all_to_all(partial_blocks, 'narrow', split_axis=3, concat_axis=2, til...]
    another operation x1 -> x0, local copies, waits for them, and re-layouts: 19.4 us -> none  [project(): return jnp.stack([proj_stiff, proj_mass], 0)]
  transfers between devices with their start and end apart: 6 -> 9, of which waited for: 4 -> 8; matrix products, arithmetic and copies ran while one was open for 12% -> 3% of each run, Pallas kernels for 0% -> 24%
where the time goes in v1:
time: 112 us; the launch traced here: 111 us
  waiting for transfers between devices  53.1 us (47%)
  Pallas kernels  36.6 us (33%)
  starting transfers between devices  12.9 us (12%)
  local copies, waits for them, and re-layouts  5.02 us (4%)
  other arithmetic  3.12 us (3%)
    pallas_call x3, Pallas kernels, sums_of(): pl.pallas_call(kernel, grid=(count,), in_specs=in_specs, out_specs=out_sp...  34.3 us
    ppermute x3, waiting for transfers between devices, paired(): arrived.append((lax.ppermute(piece, 'narrow', swap), begin, end))  23.8 us
    ppermute x1, waiting for transfers between devices, paired(): came = lax.ppermute(away, 'narrow', swap)  14.1 us
    ppermute x3, waiting for transfers between devices, paired(): total = total + lax.ppermute(here[shift] + came[shift], 'wide', ring)  7.35 us
    ppermute x3, starting transfers between devices, paired(): arrived.append((lax.ppermute(piece, 'narrow', swap), begin, end))  6.11 us
    ppermute x3, starting transfers between devices, paired(): total = total + lax.ppermute(here[shift] + came[shift], 'wide', ring)  5.56 us
    ppermute x1, waiting for transfers between devices, paired(): lax.ppermute(total, 'narrow', swap)  4.91 us
    ppermute x1, waiting for transfers between devices, paired(): got = lax.ppermute(send, 'wide', [(i, i ^ 1) for i in range(n_wide)])  2.96 us
  transfers between devices with their start and end apart: 9, of which 8 were waited for; matrix products, arithmetic and copies ran while one was open for 3% of the time, Pallas kernels for 24%

profile of v1, /device:TPU:0, one launch (start us, length us, event | category | flops | bytes accessed | tf_op | source)
XLA Modules:
  0.0 111.5 jit_solution(3245298734138224644)
XLA Ops:
  0.6 0.0 copy-start.5
  0.6 1.3 %slice.58 = f32[4,256,256]{2,1,0:T(8,128)S(1)} slice(f32[8,256,256]{2,1,0:T(8,128)} %param.8), slice={[0:4], [0:256], [0:256]} | slice | bytes 2097152 | tf_op jit(solution)/shard_map/slice | solution.py:268
  2.0 0.0 copy-start
  2.0 0.0 copy-done.5
  2.0 1.1 pad_maximum_fusion
  3.0 0.0 copy-start.6
  3.1 0.0 copy-start.7
  3.1 2.9 %collective-permute-start = (f32[1032,256]{1,0:T(8,128)}, f32[1032,256]{1,0:T(8,128)S(1)}, u32[]{:S(2)}, u32[]{:S(2)}) collective-permute-start(f32[1032,256]{1,0:T(8,128)} %pad_maximum_fusion), channel_id=1, source_target_pairs={{0,1},{1,0},{2,3},{3,2},{4,5},{5,4},{6,7},{7,6},{8,9},{9,8},{10,11... | collective-permute-start | bytes 3170312 | tf_op jit(solution)/shard_map/ppermute | solution.py:273
  6.0 0.0 copy-done
  6.0 0.9 slice.56
  6.9 22.6 %collective-permute-done.refs_1_.refs_3_ = f32[1032,256]{1,0:T(8,128)S(1)} collective-permute-done((f32[1032,256]{1,0:T(8,128)}, f32[1032,256]{1,0:T(8,128)S(1)}, u32[]{:S(2)}, u32[]{:S(2)}) %collective-permute-start) | collective-permute-done | bytes 1056800 | tf_op jit(solution)/shard_map/ppermute | solution.py:273
  29.5 0.0 copy-start.1
  29.5 1.7 %collective-permute-start.1 = (f32[768,256]{1,0:T(8,128)}, f32[768,256]{1,0:T(8,128)}, u32[]{:S(2)}, u32[]{:S(2)}) collective-permute-start(f32[768,256]{1,0:T(8,128)} %bitcast.44), channel_id=1, source_target_pairs={{0,1},{1,0},{2,3},{3,2},{4,5},{5,4},{6,7},{7,6},{8,9},{9,8},{10,11... | collective-permute-start | bytes 2359304 | tf_op jit(solution)/shard_map/ppermute | solution.py:273
  31.3 0.6 pad_add_fusion.info
  31.9 0.0 copy-done.6
  31.9 0.7 copy.14.blocks
  32.5 0.0 copy-done.7
  32.6 0.7 copy.15.adjacency
  33.2 0.0 copy-done.1
  33.3 14.1 %shard_map.95.refs_6_ = f32[8,256,512]{2,1,0:T(8,128)} custom-call(s32[3]{0:T(128)} %pad_add_fusion.info, s32[8,2,2]{2,1,0:T(2,128)} %copy.14.blocks, s32[8,4]{1,0:T(8,128)} %copy.15.adjacency, f32[2048,256]{1,0:T(8,128)} %bitcast.40, f32[1032,256]{1,0:T(8,128)} %copy-done.1, f32[8,256]{1,0:T(8,128)} %refs_2_.5, f32[1032,256]{1,0:T(8,128)} %copy-done.1, ...), custom_call_target="tpu_custom_call" | custom-call | flops 5637144576 | bytes 14680064 | tf_op jit(solution)/shard_map/pallas_call | solution.py:201
  47.3 1.2 %collective-permute-done.1.refs_1_ = f32[768,256]{1,0:T(8,128)} collective-permute-done((f32[768,256]{1,0:T(8,128)}, f32[768,256]{1,0:T(8,128)}, u32[]{:S(2)}, u32[]{:S(2)}) %collective-permute-start.1) | collective-permute-done | bytes 786464 | tf_op jit(solution)/shard_map/ppermute | solution.py:273
  48.6 1.4 %collective-permute-start.2 = (f32[256,256]{1,0:T(8,128)S(1)}, f32[256,256]{1,0:T(8,128)S(1)}, u32[]{:S(2)}, u32[]{:S(2)}) collective-permute-start(f32[256,256]{1,0:T(8,128)S(1)} %slice_bitcast_fusion), channel_id=1, source_target_pairs={{0,1},{1,0},{2,3},{3,2},{4,5},{5,4},{6,7},{7,6},{8,9},{9,8},{10,11... | collective-permute-start | bytes 786440 | tf_op jit(solution)/shard_map/ppermute | solution.py:273
  50.0 12.9 %shard_map.96.refs_6_ = f32[8,256,512]{2,1,0:T(8,128)} custom-call(s32[3]{0:T(128)} %pad_add_fusion.info, s32[8,2,2]{2,1,0:T(2,128)} %copy.14.blocks, s32[8,4]{1,0:T(8,128)} %copy.15.adjacency, f32[2048,256]{1,0:T(8,128)} %bitcast.41, f32[768,256]{1,0:T(8,128)} %collective-permute-done.1.refs_1_, f32[8,256]{1,0:T(8,128)} %refs_2_.5, f32[1032,256]{1,0:T(8,128)} %copy-done.1, ...), custom_call_target="tpu_custom_call" | custom-call | flops 4227858432 | bytes 13107200 | tf_op jit(solution)/shard_map/pallas_call | solution.py:201
  62.9 0.0 collective-permute-done.2.refs_1_
  62.9 0.0 copy-start.3
  62.9 0.7 copy-done.3
  63.6 7.4 %shard_map.97 = (f32[2,4,136,256]{3,2,1,0:T(8,128)}, f32[2,4,136,256]{3,2,1,0:T(8,128)}) custom-call(s32[3]{0:T(128)} %pad_add_fusion.info, s32[8,2,2]{2,1,0:T(2,128)} %copy.14.blocks, s32[8,4]{1,0:T(8,128)} %copy.15.adjacency, f32[2048,256]{1,0:T(8,128)} %bitcast.42, f32[256,256]{1,0:T(8,128)} %copy-done.3, f32[8,256]{1,0:T(8,128)} %refs_2_.5, ...), custom_call_target="tpu_custom_call" | custom-call | flops 1409286144 | bytes 9961472 | tf_op jit(solution)/shard_map/pallas_call | solution.py:201
  71.0 0.0 collective-permute-start.3
  71.0 3.0 %collective-permute-done.3 = f32[2,4,136,256]{3,2,1,0:T(8,128)S(1)} collective-permute-done((f32[2,4,136,256]{3,2,1,0:T(8,128)}, f32[2,4,136,256]{3,2,1,0:T(8,128)S(1)}, u32[]{:S(2)}, u32[]{:S(2)}) %collective-permute-start.3) | collective-permute-done | bytes 1114144 | tf_op jit(solution)/shard_map/ppermute | solution.py:296
  73.9 1.4 %dynamic-slice_add_fusion = (f32[1,4,136,256]{3,2,1,0:T(8,128)S(1)}, f32[4,136,256]{2,1,0:T(8,128)S(1)}) fusion(f32[2,4,136,256]{3,2,1,0:T(8,128)S(1)} %collective-permute-done.3, s32[]{:T(128)S(6)} %select_n.22, f32[2,4,136,256]{3,2,1,0:T(8,128)} %get-tuple-element.8, s32[]{:T(128)S(6)} %select_n.23), kind=kLoop, calls=%fused_computation.2 | loop fusion | flops 278528 | bytes 3342344 | tf_op jit(solution)/shard_map/add | solution.py:299
  75.3 0.7 collective-permute-start.4
  75.9 14.1 %collective-permute-done.4 = f32[4,136,256]{2,1,0:T(8,128)S(1)} collective-permute-done((f32[4,136,256]{2,1,0:T(8,128)S(1)}, f32[4,136,256]{2,1,0:T(8,128)S(1)}, u32[]{:S(2)}, u32[]{:S(2)}) %collective-permute-start.4) | collective-permute-done | bytes 557088 | tf_op jit(solution)/shard_map/ppermute | solution.py:298
  90.0 0.1 fusion.2
  90.1 1.6 %collective-permute-start.5 = (f32[136,256]{1,0:T(8,128)S(1)}, f32[136,256]{1,0:T(8,128)S(1)}, u32[]{:S(2)}, u32[]{:S(2)}) collective-permute-start(f32[136,256]{1,0:T(8,128)S(1)} %get-tuple-element.12), channel_id=1, source_target_pairs={{0,4},{2,6},{4,8},{6,10},{8,12},{10,14},{12,0},{14,2},{1,5},{3,7},... | collective-permute-start | bytes 417800 | tf_op jit(solution)/shard_map/ppermute | solution.py:303
  91.7 2.6 %collective-permute-start.6 = (f32[136,256]{1,0:T(8,128)S(1)}, f32[136,256]{1,0:T(8,128)S(1)}, u32[]{:S(2)}, u32[]{:S(2)}) collective-permute-start(f32[136,256]{1,0:T(8,128)S(1)} %get-tuple-element.14), channel_id=1, source_target_pairs={{0,8},{2,10},{4,12},{6,14},{8,0},{10,2},{12,4},{14,6},{1,9},{3,11}... | collective-permute-start | bytes 417800 | tf_op jit(solution)/shard_map/ppermute | solution.py:303
  94.3 1.3 %collective-permute-start.7 = (f32[136,256]{1,0:T(8,128)S(1)}, f32[136,256]{1,0:T(8,128)S(1)}, u32[]{:S(2)}, u32[]{:S(2)}) collective-permute-start(f32[136,256]{1,0:T(8,128)S(1)} %get-tuple-element.13), channel_id=1, source_target_pairs={{0,12},{2,14},{4,0},{6,2},{8,4},{10,6},{12,8},{14,10},{1,13},{3,15... | collective-permute-start | bytes 417800 | tf_op jit(solution)/shard_map/ppermute | solution.py:303
  95.6 3.0 %collective-permute-done.5 = f32[136,256]{1,0:T(8,128)S(1)} collective-permute-done((f32[136,256]{1,0:T(8,128)S(1)}, f32[136,256]{1,0:T(8,128)S(1)}, u32[]{:S(2)}, u32[]{:S(2)}) %collective-permute-start.5) | collective-permute-done | bytes 139296 | tf_op jit(solution)/shard_map/ppermute | solution.py:303
  98.7 4.3 %collective-permute-done.6 = f32[136,256]{1,0:T(8,128)S(1)} collective-permute-done((f32[136,256]{1,0:T(8,128)S(1)}, f32[136,256]{1,0:T(8,128)S(1)}, u32[]{:S(2)}, u32[]{:S(2)}) %collective-permute-start.6) | collective-permute-done | bytes 139296 | tf_op jit(solution)/shard_map/ppermute | solution.py:303
  102.9 0.1 collective-permute-done.7
  103.0 0.1 fusion.6.mine
  103.1 0.0 copy-start.2
  103.1 0.6 collective-permute-start.8
  103.7 4.9 %collective-permute-done.8.theirs = f32[136,256]{1,0:T(8,128)S(1)} collective-permute-done((f32[136,256]{1,0:T(8,128)S(1)}, f32[136,256]{1,0:T(8,128)S(1)}, u32[]{:S(2)}, u32[]{:S(2)}) %collective-permute-start.8) | collective-permute-done | bytes 139296 | tf_op jit(solution)/shard_map/ppermute | solution.py:304
  108.6 0.0 copy-done.2
  108.6 0.0 copy-start.4
  108.6 0.7 copy-done.4
  109.2 2.2 %shard_map.98 = (f32[1,128,256]{2,1,0:T(8,128)}, f32[1,128,256]{2,1,0:T(8,128)}) custom-call(s32[3]{0:T(128)} %pad_add_fusion.info, f32[136,256]{1,0:T(8,128)} %copy-done.2, f32[136,256]{1,0:T(8,128)} %copy-done.4, f32[1,128,256]{2,1,0:T(8,128)} %stiff_ref.1, f32[1,128,256]{2,1,0:T(8,128)} %mass_ref.1), custom_call_target="tpu_custom_call" | custom-call | tf_op jit(solution)/shard_map/pallas_call | solution.py:245
  (1 shorter events, 0.0 us)
Async XLA Ops:
  0.6 1.3 %copy-start.5 = (f32[8,256]{1,0:T(8,128)S(1)}, f32[8,256]{1,0:T(8,128)}, u32[]{:S(2)}) copy-start(f32[8,256]{1,0:T(8,128)} %refs_2_.5) | copy-start | bytes 24580
  2.0 4.0 %copy-start = (f32[8,256,256]{2,1,0:T(8,128)S(1)}, f32[8,256,256]{2,1,0:T(8,128)}, u32[]{:S(2)}) copy-start(f32[8,256,256]{2,1,0:T(8,128)} %param.8) | copy-start | bytes 6291460
  3.0 28.8 %copy-start.6 = (s32[8,2,2]{0,2,1:T(2,128)S(1)}, s32[8,2,2]{0,2,1:T(2,128)}, u32[]{:S(2)}) copy-start(s32[8,2,2]{0,2,1:T(2,128)} %param.12) | copy-start | bytes 388
  3.1 29.5 %copy-start.7 = (s32[8,4]{0,1:T(4,128)S(1)}, s32[8,4]{0,1:T(4,128)}, u32[]{:S(2)}) copy-start(s32[8,4]{0,1:T(4,128)} %param.13) | copy-start | bytes 388
  3.1 26.5 %collective-permute-start = (f32[1032,256]{1,0:T(8,128)}, f32[1032,256]{1,0:T(8,128)S(1)}, u32[]{:S(2)}, u32[]{:S(2)}) collective-permute-start(f32[1032,256]{1,0:T(8,128)} %pad_maximum_fusion), channel_id=1, source_target_pairs={{0,1},{1,0},{2,3},{3,2},{4,5},{5,4},{6,7},{7,6},{8,9},{9,8},{10,11... | collective-permute-start | bytes 3170312 | tf_op jit(solution)/shard_map/ppermute | solution.py:273
  29.5 3.7 %copy-start.1 = (f32[1032,256]{1,0:T(8,128)}, f32[1032,256]{1,0:T(8,128)S(1)}, u32[]{:S(2)}) copy-start(f32[1032,256]{1,0:T(8,128)S(1)} %collective-permute-done.refs_1_.refs_3_) | copy-start | bytes 3170308
  29.5 19.0 %collective-permute-start.1 = (f32[768,256]{1,0:T(8,128)}, f32[768,256]{1,0:T(8,128)}, u32[]{:S(2)}, u32[]{:S(2)}) collective-permute-start(f32[768,256]{1,0:T(8,128)} %bitcast.44), channel_id=1, source_target_pairs={{0,1},{1,0},{2,3},{3,2},{4,5},{5,4},{6,7},{7,6},{8,9},{9,8},{10,11... | collective-permute-start | bytes 2359304 | tf_op jit(solution)/shard_map/ppermute | solution.py:273
  48.6 14.3 %collective-permute-start.2 = (f32[256,256]{1,0:T(8,128)S(1)}, f32[256,256]{1,0:T(8,128)S(1)}, u32[]{:S(2)}, u32[]{:S(2)}) collective-permute-start(f32[256,256]{1,0:T(8,128)S(1)} %slice_bitcast_fusion), channel_id=1, source_target_pairs={{0,1},{1,0},{2,3},{3,2},{4,5},{5,4},{6,7},{7,6},{8,9},{9,8},{10,11... | collective-permute-start | bytes 786440 | tf_op jit(solution)/shard_map/ppermute | solution.py:273
  62.9 0.7 copy-start.3
  71.0 3.0 %collective-permute-start.3 = (f32[2,4,136,256]{3,2,1,0:T(8,128)}, f32[2,4,136,256]{3,2,1,0:T(8,128)S(1)}, u32[]{:S(2)}, u32[]{:S(2)}) collective-permute-start(f32[2,4,136,256]{3,2,1,0:T(8,128)} %get-tuple-element.9), channel_id=1, source_target_pairs={{0,2},{2,0},{4,6},{6,4},{8,10},{10,8},{12,14},{14,12},{1,3},{3,1},... | collective-permute-start | bytes 3342344 | tf_op jit(solution)/shard_map/ppermute | solution.py:296
  75.3 14.7 %collective-permute-start.4 = (f32[4,136,256]{2,1,0:T(8,128)S(1)}, f32[4,136,256]{2,1,0:T(8,128)S(1)}, u32[]{:S(2)}, u32[]{:S(2)}) collective-permute-start(f32[4,136,256]{2,1,0:T(8,128)S(1)} %get-tuple-element.11), channel_id=1, source_target_pairs={{0,1},{1,0},{2,3},{3,2},{4,5},{5,4},{6,7},{7,6},{8,9},{9,8},{10,11... | collective-permute-start | bytes 1671176 | tf_op jit(solution)/shard_map/ppermute | solution.py:298
  90.1 8.6 %collective-permute-start.5 = (f32[136,256]{1,0:T(8,128)S(1)}, f32[136,256]{1,0:T(8,128)S(1)}, u32[]{:S(2)}, u32[]{:S(2)}) collective-permute-start(f32[136,256]{1,0:T(8,128)S(1)} %get-tuple-element.12), channel_id=1, source_target_pairs={{0,4},{2,6},{4,8},{6,10},{8,12},{10,14},{12,0},{14,2},{1,5},{3,7},... | collective-permute-start | bytes 417800 | tf_op jit(solution)/shard_map/ppermute | solution.py:303
  91.7 11.2 %collective-permute-start.6 = (f32[136,256]{1,0:T(8,128)S(1)}, f32[136,256]{1,0:T(8,128)S(1)}, u32[]{:S(2)}, u32[]{:S(2)}) collective-permute-start(f32[136,256]{1,0:T(8,128)S(1)} %get-tuple-element.14), channel_id=1, source_target_pairs={{0,8},{2,10},{4,12},{6,14},{8,0},{10,2},{12,4},{14,6},{1,9},{3,11}... | collective-permute-start | bytes 417800 | tf_op jit(solution)/shard_map/ppermute | solution.py:303
  94.3 8.7 %collective-permute-start.7 = (f32[136,256]{1,0:T(8,128)S(1)}, f32[136,256]{1,0:T(8,128)S(1)}, u32[]{:S(2)}, u32[]{:S(2)}) collective-permute-start(f32[136,256]{1,0:T(8,128)S(1)} %get-tuple-element.13), channel_id=1, source_target_pairs={{0,12},{2,14},{4,0},{6,2},{8,4},{10,6},{12,8},{14,10},{1,13},{3,15... | collective-permute-start | bytes 417800 | tf_op jit(solution)/shard_map/ppermute | solution.py:303
  103.1 5.5 %copy-start.2 = (f32[136,256]{1,0:T(8,128)}, f32[136,256]{1,0:T(8,128)S(1)}, u32[]{:S(2)}) copy-start(f32[136,256]{1,0:T(8,128)S(1)} %fusion.6.mine) | copy-start | bytes 417796
  103.1 5.5 %collective-permute-start.8 = (f32[136,256]{1,0:T(8,128)S(1)}, f32[136,256]{1,0:T(8,128)S(1)}, u32[]{:S(2)}, u32[]{:S(2)}) collective-permute-start(f32[136,256]{1,0:T(8,128)S(1)} %fusion.6.mine), channel_id=1, source_target_pairs={{0,1},{1,0},{2,3},{3,2},{4,5},{5,4},{6,7},{7,6},{8,9},{9,8},{10,11... | collective-permute-start | bytes 417800 | tf_op jit(solution)/shard_map/ppermute | solution.py:304
  108.6 0.7 copy-start.4

commit v2 on v0

v2 whole, which is shorter than its diff:
```python
import functools

import jax
import jax.numpy as jnp
from jax import lax
from jax.experimental import pallas as pl
from jax.experimental.pallas import tpu as pltpu
from jax.sharding import PartitionSpec as P

ROWT = 128
LANES = 128
GROUP = 8
PIECE = (2 * ROWT + GROUP) // 3
MIB = 1024 * 1024

f32 = jnp.float32
bf16 = jnp.bfloat16


def split(x):
    high = x.astype(bf16)
    return high, (x - high.astype(f32)).astype(bf16)


def left(pair, axis):
    return jnp.concatenate([pair[0], pair[1], pair[0]], axis)


def right(pair, axis):
    return jnp.concatenate([pair[0], pair[0], pair[1]], axis)


def product(a, b, a_dim, b_dim):
    return lax.dot_general(a, b, (((a_dim,), (b_dim,)), ((), ())), preferred_element_type=f32)


def full_rows(tiles_ref, slot, blocks_ref, sub, row_tiles):
    tiles = tiles_ref.shape[2]
    rows = []
    for r in range(row_tiles):
        total = None
        for t in range(tiles):
            here = (blocks_ref[sub, slot, t] == r).astype(f32)
            term = tiles_ref[0, slot, t] * here
            total = term if total is None else total + term
        rows.append(total)
    return jnp.concatenate(rows, 0)


def contributions(phi, inverse, stiffs, masses):
    held = phi.shape[1]
    width = stiffs[0][0].shape[1]
    sides = [jnp.concatenate(x, 1) for x in zip(*stiffs, *masses, strict=True)]
    projected = product(left(split(phi.T), 1), right(sides, 0), 1, 0)
    scale = jnp.broadcast_to(inverse, (LANES, held)).T
    scale = jnp.concatenate([scale] * (width // LANES), 1)
    slots = len(stiffs)
    for slot in range(slots):
        p = projected[:, slot * width : (slot + 1) * width]
        q = projected[:, (slots + slot) * width : (slots + slot + 1) * width]
        first = scale * p
        second = scale * (0.5 * first - q)
        both = [jnp.concatenate(x, 1) for x in zip(split(first), split(second), strict=True)]
        yield product(left(split(p.T), 1), right(both, 0), 1, 0)


def local_kernel(start, has_acc, info, blocks, adjacency, modes_ref, eig_ref, stiff_ref, mass_ref, *refs):
    acc_in = refs[0] if has_acc else None
    s_ref, m_ref, acc_ref = refs[-3:]

    @pl.when(pl.program_id(0) == 0)
    def _():
        acc_ref[...] = acc_in[...] if has_acc else jnp.zeros_like(acc_ref)

    sub = pl.program_id(0) + start
    row_tiles = modes_ref.shape[0] // ROWT
    slots = stiff_ref.shape[1]
    stiffs, masses = [], []
    for slot in range(slots):
        for pairs, tiles_ref, pair_ref in ((stiffs, stiff_ref, s_ref), (masses, mass_ref, m_ref)):
            pairs.append(split(full_rows(tiles_ref, slot, blocks, sub, row_tiles)))
            pair_ref[0, slot, 0], pair_ref[0, slot, 1] = pairs[-1]
    inverse = 1.0 / eig_ref[pl.ds(sub, 1), :]
    for slot, update in enumerate(contributions(modes_ref[...], inverse, stiffs, masses)):
        acc_ref[adjacency[sub, info[0] * slots + slot]] += update


def whole(shape):
    return pl.BlockSpec(shape, functools.partial(lambda n, i: (0,) * n, len(shape)))


def once(shape):
    return pl.BlockSpec(
        shape, functools.partial(lambda n, i: (0,) * n, len(shape)), pipeline_mode=pl.Buffered(1)
    )


def params(limit):
    return pltpu.CompilerParams(vmem_limit_bytes=limit * MIB)


def cost(count, rows, held, slots, width):
    flops = 6 * count * 4 * slots * rows * held * width
    return pl.CostEstimate(flops=flops, bytes_accessed=count * 3 * MIB, transcendentals=0)


def local_sums(scalars, flat, eigvals, stiff, mass, start, count, limit, ifaces, acc=None):
    subs, slots, tiles, rowt, width = stiff.shape
    held = flat.shape[1]
    rows = flat.shape[0] // subs
    tile_spec = pl.BlockSpec((1, slots, tiles, rowt, width), lambda i: (i + start, 0, 0, 0, 0))
    pair_spec = pl.BlockSpec((1, slots, 2, rows, width), lambda i: (i, 0, 0, 0, 0))
    pair = jax.ShapeDtypeStruct((count, slots, 2, rows, width), bf16)
    shape = (ifaces, width, 2 * width)
    given = [] if acc is None else [acc]
    return pl.pallas_call(
        functools.partial(local_kernel, start, acc is not None),
        grid=(count,),
        in_specs=[pl.BlockSpec(memory_space=pltpu.SMEM)] * 3
        + [pl.BlockSpec((rows, held), lambda i: (i + start, 0)), whole(eigvals.shape), tile_spec, tile_spec]
        + [once(shape)] * len(given),
        out_specs=[pair_spec, pair_spec, whole(shape)],
        out_shape=[pair, pair, jax.ShapeDtypeStruct(shape, f32)],
        compiler_params=params(limit),
        cost_estimate=cost(count, rows, held, slots, width),
    )(*scalars, flat, eigvals, stiff, mass, *given)


def pairs_of(ref, place=0):
    return [(ref[place, slot, 0], ref[place, slot, 1]) for slot in range(ref.shape[1])]


def sum_kernel(start, info, adjacency, modes_ref, eig_ref, s_ref, m_ref, acc_in, acc_ref):
    @pl.when(pl.program_id(0) == 0)
    def _():
        acc_ref[...] = acc_in[...]

    sub = pl.program_id(0) + start
    slots = s_ref.shape[1]
    inverse = 1.0 / eig_ref[pl.ds(sub, 1), :]
    sums = contributions(modes_ref[...], inverse, pairs_of(s_ref), pairs_of(m_ref))
    for slot, update in enumerate(sums):
        acc_ref[adjacency[sub, info[0] * slots + slot]] += update


def pair_specs(pairs, offset):
    return [
        pl.BlockSpec((1, *pair.shape[1:]), lambda i: (i + offset, 0, 0, 0, 0)) for pair in pairs
    ]


def arrived_sums(scalars, modes, eigs, pairs, start, offset, count, acc):
    slots, _, rows, width = pairs[0].shape[1:]
    held = modes.shape[1]
    return pl.pallas_call(
        functools.partial(sum_kernel, start),
        grid=(count,),
        in_specs=[pl.BlockSpec(memory_space=pltpu.SMEM)] * 2
        + [pl.BlockSpec((rows, held), lambda i: (i, 0)), whole(eigs.shape)]
        + pair_specs(pairs, offset)
        + [once(acc.shape)],
        out_specs=whole(acc.shape),
        out_shape=jax.ShapeDtypeStruct(acc.shape, f32),
        compiler_params=params(24),
        cost_estimate=cost(count, rows, held, slots, width),
    )(*scalars, modes, eigs, *pairs, acc)


def pack(sums):
    row = lax.broadcasted_iota(jnp.int32, (ROWT, ROWT), 0)
    col = lax.broadcasted_iota(jnp.int32, (ROWT, ROWT), 1)
    packed, diagonals = [], []
    for which in range(2):
        base = which * 2 * ROWT
        first = sums(slice(0, ROWT), slice(base, base + ROWT))
        second = sums(slice(ROWT, 2 * ROWT), slice(base + ROWT, base + 2 * ROWT))
        corner = sums(slice(ROWT, 2 * ROWT), slice(base, base + ROWT))
        square = jnp.where(row > col, first, second)
        diagonal = jnp.sum(jnp.where(row == col, first, 0.0), axis=0, keepdims=True)
        if which == 1:
            corner = corner + sums(slice(0, ROWT), slice(base + ROWT, base + 2 * ROWT)).T
            square = square + jnp.where(row < col, first, second).T
            diagonal = diagonal + diagonal
        packed.append(jnp.concatenate([corner, square], 1))
        diagonals.append(diagonal)
    packed.append(jnp.broadcast_to(jnp.concatenate(diagonals, 1), (GROUP, 2 * LANES)))
    return jnp.concatenate(packed, 0)


def places(side):
    return ((0, 0), (1, 2 - side), (2, 1 + side))


def pack_kernel(info, acc_ref, send_ref, keep_ref):
    side, chip, core = info[0], info[1], info[2]

    def one(shift, carry):
        target = lax.bitwise_xor(chip, shift) * 2
        for owner, out_ref in ((target + 1 - core, send_ref), (target + core, keep_ref)):
            packed = pack(lambda r, c, o=owner: acc_ref[o, r, c])
            for piece, place in places(side):
                out_ref[place, shift] = packed[piece * PIECE : (piece + 1) * PIECE]
        return carry

    lax.fori_loop(0, send_ref.shape[1], one, 0)


def packed_sums(info, acc, shape):
    return pl.pallas_call(
        pack_kernel,
        in_specs=[pl.BlockSpec(memory_space=pltpu.SMEM), pl.BlockSpec(memory_space=pltpu.VMEM)],
        out_specs=[pl.BlockSpec(memory_space=pltpu.VMEM)] * 2,
        out_shape=[jax.ShapeDtypeStruct(shape, f32)] * 2,
        compiler_params=params(16),
        cost_estimate=pl.CostEstimate(flops=8_000_000, bytes_accessed=MIB, transcendentals=0),
    )(info, acc)


def add_kernel(
    sub, info, adjacency, modes_ref, eig_ref, s_ref, m_ref, send_in, keep_in, send_ref, keep_ref, held, sems
):
    side, chip, core = info[0], info[1], info[2]
    slots = s_ref.shape[1]

    def copies(slot, inward):
        owner = adjacency[sub, side * slots + slot]
        shift = lax.bitwise_xor(owner // 2, chip)
        mine = lax.rem(owner, 2) == core
        for here, ref in ((mine, keep_ref), (jnp.logical_not(mine), send_ref)):
            ends = (ref.at[:, shift], held.at[slot])
            source, target = ends if inward else ends[::-1]
            yield here, pltpu.make_async_copy(source, target, sems.at[slot])

    def run(slot, inward, wait):
        for here, copy in copies(slot, inward):

            @pl.when(here)
            def _(copy=copy):
                if wait:
                    copy.wait()
                else:
                    copy.start()

    for slot in range(slots):
        run(slot, True, False)
    inverse = 1.0 / eig_ref[sub : sub + 1, :]
    sums = contributions(modes_ref[...], inverse, pairs_of(s_ref), pairs_of(m_ref))
    for slot, update in enumerate(sums):
        packed = pack(lambda r, c, u=update: u[r, c])
        run(slot, True, True)
        for piece, place in places(side):
            held[slot, place] += packed[piece * PIECE : (piece + 1) * PIECE]
        run(slot, False, False)
    for slot in range(slots):
        run(slot, False, True)


def added_sums(scalars, modes, eigs, pairs, sub, offset, sums):
    slots, _, rows, width = pairs[0].shape[1:]
    held = modes.shape[1]
    anywhere = pl.BlockSpec(memory_space=pl.ANY)
    _, _, *piece = sums[0].shape
    return pl.pallas_call(
        functools.partial(add_kernel, sub),
        grid=(1,),
        in_specs=[pl.BlockSpec(memory_space=pltpu.SMEM)] * 2
        + [pl.BlockSpec((rows, held), lambda i: (i, 0)), whole(eigs.shape)]
        + pair_specs(pairs, offset)
        + [anywhere] * 2,
        out_specs=[anywhere] * 2,
        out_shape=[jax.ShapeDtypeStruct(x.shape, f32) for x in sums],
        scratch_shapes=[
            pltpu.VMEM((slots, sums[0].shape[0], *piece), f32),
            pltpu.SemaphoreType.DMA((slots,)),
        ],
        input_output_aliases={6: 0, 7: 1},
        compiler_params=params(16),
        cost_estimate=cost(1, rows, held, slots, width),
    )(*scalars, modes, eigs, *pairs, *sums)


def unpack_kernel(info, early_mine, early_theirs, mine, theirs, stiff_ref, mass_ref, out_stiff, out_mass):
    side = info[0]
    row = lax.broadcasted_iota(jnp.int32, (ROWT, ROWT), 0)
    col = lax.broadcasted_iota(jnp.int32, (ROWT, ROWT), 1)
    a, b = mine[...], theirs[...]
    packed = jnp.concatenate(
        [early_mine[...] + early_theirs[...], jnp.where(side == 0, a, b), jnp.where(side == 0, b, a)], 0
    )
    for which, (iface_ref, out_ref) in enumerate(((stiff_ref, out_stiff), (mass_ref, out_mass))):
        sign = -1.0 if which == 0 else 1.0
        rows = packed[which * ROWT : (which + 1) * ROWT]
        corner, square = rows[:, :LANES], rows[:, LANES:]
        diagonal = packed[2 * ROWT : 2 * ROWT + 1, which * LANES : (which + 1) * LANES]
        flipped = square.T

        @pl.when(side == 0)
        def _():
            first = jnp.where(row > col, square, jnp.where(row == col, diagonal, flipped))
            out_ref[0, :, :LANES] = iface_ref[0, :, :LANES] + sign * first
            out_ref[0, :, LANES:] = iface_ref[0, :, LANES:] + sign * corner.T

        @pl.when(side != 0)
        def _():
            second = jnp.where(row <= col, square, flipped)
            out_ref[0, :, :LANES] = iface_ref[0, :, :LANES] + sign * corner
            out_ref[0, :, LANES:] = iface_ref[0, :, LANES:] + sign * second


def unpack(info, sums, iface_stiff, iface_mass):
    vmem = pl.BlockSpec(memory_space=pltpu.VMEM)
    return pl.pallas_call(
        unpack_kernel,
        in_specs=[pl.BlockSpec(memory_space=pltpu.SMEM)] + [vmem] * 6,
        out_specs=(vmem, vmem),
        out_shape=(jax.ShapeDtypeStruct(iface_stiff.shape, f32),) * 2,
        compiler_params=params(8),
    )(info, *sums, iface_stiff, iface_mass)


def paired(modes, eigvals, stiff, mass, blocks, adjacency, iface_stiff, iface_mass):
    subs, rows, held = modes.shape
    n_wide = lax.axis_size("wide")
    chips = n_wide // 2
    side, wide = lax.axis_index("narrow"), lax.axis_index("wide")
    info = jnp.stack([side, wide // 2, wide % 2]).astype(jnp.int32)
    flat = modes.reshape(subs * rows, held)

    def swap(x):
        return lax.ppermute(x, "narrow", [(0, 1), (1, 0)])

    def over_wide(x, mask):
        return lax.ppermute(x, "wide", [(i, i ^ mask) for i in range(n_wide)])

    def after(x, *others):
        return lax.optimization_barrier((x, *others))

    half = subs // 2
    cuts = [0, half, subs - 2, subs - 1, subs]
    pieces = [flat[a * rows : b * rows] for a, b in zip(cuts[:-1], cuts[1:], strict=True)]
    came = [swap(pieces[0])]
    local = functools.partial(local_sums, [info, blocks, adjacency], flat, eigvals, stiff, mass)
    *early, acc = local(0, half, 28, n_wide)
    sent, acc = after(eigvals, acc)
    eigs = swap(sent)
    *late, acc = local(half, subs - half, 28, n_wide, acc)
    sent, acc = after(pieces[1], acc)
    came.append(swap(sent))
    sent, came[0] = after(pieces[2], came[0])
    came.append(swap(sent))

    scalars = [info, adjacency]
    acc = arrived_sums(scalars, came[0], eigs, early, 0, 0, half, acc)
    sent, acc = after(pieces[3], acc)
    came.append(swap(sent))
    acc = arrived_sums(scalars, came[1], eigs, late, half, 0, cuts[2] - half, acc)
    sums = packed_sums(info, acc, (3, chips, PIECE, 2 * LANES))
    for k in (2, 3):
        sums = added_sums(scalars, came[k], eigs, late, cuts[k], cuts[k] - half, sums)
    send, keep = sums

    def over_chips(x):
        total = x[0]
        for shift in range(1, chips):
            total = total + over_wide(x[shift], 2 * shift)
        return total

    got = over_wide(send, 1)
    away = swap(keep[1] + got[1])
    first = over_chips(keep[0] + got[0])
    first_theirs = swap(first)
    second = over_chips(keep[2] + got[2] + away)
    second_theirs = swap(second)
    return unpack(info, (first, first_theirs, second, second_theirs), iface_stiff, iface_mass)


def grouped(modes, eigvals, stiff, mass, blocks, adjacency, iface_stiff, iface_mass):
    subs, rows, _ = modes.shape
    width = stiff.shape[4]
    n_wide = lax.axis_size("wide")
    info = jnp.stack([lax.axis_index("narrow")] * 3).astype(jnp.int32)
    modes = lax.all_gather(modes, "narrow", axis=2, tiled=True)
    eigvals = lax.all_gather(eigvals, "narrow", axis=1, tiled=True)
    flat = modes.reshape(subs * rows, modes.shape[2])
    _, _, acc = local_sums([info, blocks, adjacency], flat, eigvals, stiff, mass, 0, subs, 52, n_wide)
    half = acc[:, :, width:]
    part = jnp.concatenate([acc[:, :, :width], half + jnp.swapaxes(half, 1, 2)], 2)
    part = lax.psum_scatter(part, "wide", scatter_dimension=0, tiled=True)
    part = lax.psum_scatter(part, ("narrow", "sub"), scatter_dimension=1, tiled=True)
    return iface_stiff - part[:, :, :width], iface_mass + part[:, :, width:]


def solution(mesh):
    wide = mesh.shape["wide"]
    pairs = mesh.shape["narrow"] == 2 and mesh.shape["sub"] == 1 and wide > 1 and wide & (wide - 1) == 0
    return jax.shard_map(
        paired if pairs else grouped,
        mesh=mesh,
        in_specs=(
            P(("parts", "wide"), None, ("narrow", "sub")),
            P(("parts", "wide"), ("narrow", "sub")),
            P(("parts", "wide"), "narrow", None, None, None),
            P(("parts", "wide"), "narrow", None, None, None),
            P(("parts", "wide"), "narrow", None),
            P(("parts", "wide"), None),
            P(("parts", "wide"), ("narrow", "sub"), None),
            P(("parts", "wide"), ("narrow", "sub"), None),
        ),
        out_specs=(
            P(("parts", "wide"), ("narrow", "sub"), None),
            P(("parts", "wide"), ("narrow", "sub"), None),
        ),
        check_vma=False,
    )
```

time: 874 us -> 86 us (0.10)
  waiting for transfers between devices: 614 us -> 26.4 us
  matrix products: 116 us -> 0 us
  local copies, waits for them, and re-layouts: 90.7 us -> 7.13 us
  Pallas kernels: 0 us -> 29.6 us
  between operations: 14.1 us -> 0.82 us
  other arithmetic: 11 us -> 0.29 us
    all_to_all x3 -> x0, waiting for transfers between devices: 545 us -> none  [the longest x1 364 us: per_device(): lax.all_to_all(send_blocks, 'wide', split_axis=1, concat_axis=1, tiled=True)]
    dot_general x7 -> x0, matrix products: 116 us -> none  [the longest x1 22.2 us: per_device(): jnp.einsum('rc,rd->cd', recv_stiff, weight_one * recv_stiff, precision=hi...]
    all_gather x1 -> x0, waiting for transfers between devices: 60.2 us -> none  [per_device(): lax.all_gather(modes, 'narrow', axis=2, tiled=True)]
    reshape x4 -> x0, local copies, waits for them, and re-layouts: 32 us -> none  [the longest x1 17.4 us: per_device(): send_blocks = send_blocks.reshape(2, n_wide, capacity, mode_part, width)]
    pallas_call x0 -> x8, Pallas kernels: none -> 29.6 us  [the longest x2 12.3 us: local_sums(): pl.pallas_call(functools.partial(local_kernel, start, acc is not None), g...]
    ppermute x0 -> x15, waiting for transfers between devices: none -> 26.4 us  [the longest x8 18.9 us: swap(): return lax.ppermute(x, 'narrow', [(0, 1), (1, 0)])]
    ppermute x0 -> x15, starting transfers between devices: none -> 21.5 us  [the longest x8 12.5 us: swap(): return lax.ppermute(x, 'narrow', [(0, 1), (1, 0)])]
    all_to_all x3 -> x0, starting transfers between devices: 20.4 us -> none  [the longest x1 9.8 us: per_device(): lax.all_to_all(partial_blocks, 'narrow', split_axis=3, concat_axis=2, til...]
  transfers between devices with their start and end apart: 6 -> 15, of which waited for: 4 -> 8; matrix products, arithmetic and copies ran while one was open for 12% -> 1% of each run, Pallas kernels for 0% -> 29%
where the time goes in v2:
time: 86 us; the launch traced here: 85.8 us
  Pallas kernels  29.6 us (34%)
  waiting for transfers between devices  26.4 us (31%)
  starting transfers between devices  21.5 us (25%)
  local copies, waits for them, and re-layouts  7.13 us (8%)
    ppermute x8, waiting for transfers between devices, swap(): return lax.ppermute(x, 'narrow', [(0, 1), (1, 0)])  18.9 us
    ppermute x8, starting transfers between devices, swap(): return lax.ppermute(x, 'narrow', [(0, 1), (1, 0)])  12.5 us
    pallas_call x2, Pallas kernels, local_sums(): pl.pallas_call(functools.partial(local_kernel, start, acc is not None), g...  12.3 us
    ppermute x7, starting transfers between devices, over_wide(): return lax.ppermute(x, 'wide', [(i, i ^ mask) for i in range(n_wide)])  9.01 us
    pallas_call x2, Pallas kernels, arrived_sums(): pl.pallas_call(functools.partial(sum_kernel, start), grid=(count,), in_sp...  8.98 us
    ppermute x7, waiting for transfers between devices, over_wide(): return lax.ppermute(x, 'wide', [(i, i ^ mask) for i in range(n_wide)])  7.57 us
    pallas_call x2, Pallas kernels, added_sums(): pl.pallas_call(functools.partial(add_kernel, sub), grid=(1,), in_specs=[p...  5.48 us
    unnamed x18, local copies, waits for them, and re-layouts  4.58 us
  transfers between devices with their start and end apart: 15, of which 8 were waited for; matrix products, arithmetic and copies ran while one was open for 1% of the time, Pallas kernels for 29%

profile of v2, /device:TPU:0, one launch (start us, length us, event | category | flops | bytes accessed | tf_op | source)
XLA Modules:
  0.0 85.8 jit_solution(486268276205075019)
XLA Ops:
  0.7 2.4 %slice.74 = f32[4,256,256]{2,1,0:T(8,128)} slice(f32[8,256,256]{2,1,0:T(8,128)} %param.8), slice={[0:4], [0:256], [0:256]} | slice | bytes 2097152 | tf_op jit(solution)/shard_map/slice | solution.py:340
  3.1 2.9 %collective-permute-start = (f32[1024,256]{1,0:T(8,128)}, f32[1024,256]{1,0:T(8,128)S(1)}, u32[]{:S(2)}, u32[]{:S(2)}) collective-permute-start(f32[1024,256]{1,0:T(8,128)} %bitcast.5), channel_id=1, source_target_pairs={{0,1},{1,0},{2,3},{3,2},{4,5},{5,4},{6,7},{7,6},{8,9},{9,8},{10,11... | collective-permute-start | bytes 3145736 | tf_op jit(solution)/shard_map/ppermute | solution.py:330
  6.1 0.1 copy.21.adjacency
  6.1 0.1 copy.14.blocks
  6.2 0.1 pad_add_fusion.info
  6.3 2.2 %copy-done.1 = f32[8,2,2,128,256]{4,3,2,1,0:T(8,128)S(1)} copy-done((f32[8,2,2,128,256]{4,3,2,1,0:T(8,128)S(1)}, f32[8,2,2,128,256]{4,3,2,1,0:T(8,128)}, u32[]{:S(2)}) %copy-start.1) | copy-done | bytes 4194328
  8.5 2.2 %copy-done.2 = f32[8,2,2,128,256]{4,3,2,1,0:T(8,128)S(1)} copy-done((f32[8,2,2,128,256]{4,3,2,1,0:T(8,128)S(1)}, f32[8,2,2,128,256]{4,3,2,1,0:T(8,128)}, u32[]{:S(2)}) %copy-start.2) | copy-done | bytes 4194328
  10.7 6.1 %shard_map.95 = (bf16[4,2,2,256,256]{4,3,2,1,0:T(8,128)(2,1)S(1)}, bf16[4,2,2,256,256]{4,3,2,1,0:T(8,128)(2,1)S(1)}, f32[8,256,512]{2,1,0:T(8,128)S(1)}) custom-call(s32[3]{0:T(128)S(1)} %pad_add_fusion.info, s32[8,2,2]{2,1,0:T(2,128)S(1)} %copy.14.blocks, s32[8,4]{1,0:T(8,128)S(1)} %copy.21.adjacency, f32[2048,256]{1,0:T(8,128)S(1)} %bitcast.44, ...), custom_call_target="tpu_custom_call" | custom-call | flops 3221225472 | bytes 12582912 | tf_op jit(solution)/shard_map/pallas_call | solution.py:116
  16.8 0.1 collective-permute-start.1
  17.0 6.2 %shard_map.96 = (bf16[4,2,2,256,256]{4,3,2,1,0:T(8,128)(2,1)S(1)}, bf16[4,2,2,256,256]{4,3,2,1,0:T(8,128)(2,1)S(1)}, f32[8,256,512]{2,1,0:T(8,128)S(1)}) custom-call(s32[3]{0:T(128)S(1)} %pad_add_fusion.info, s32[8,2,2]{2,1,0:T(2,128)S(1)} %copy.14.blocks, s32[8,4]{1,0:T(8,128)S(1)} %copy.21.adjacency, f32[2048,256]{1,0:T(8,128)S(1)} %bitcast.45, ...), custom_call_target="tpu_custom_call" | custom-call | flops 3221225472 | bytes 12582912 | tf_op jit(solution)/shard_map/pallas_call | solution.py:116
  23.1 2.1 %collective-permute-start.4 = (f32[512,256]{1,0:T(8,128)S(1)}, f32[512,256]{1,0:T(8,128)S(1)}, u32[]{:S(2)}, u32[]{:S(2)}) collective-permute-start(f32[512,256]{1,0:T(8,128)S(1)} %bitcast.46), channel_id=1, source_target_pairs={{0,1},{1,0},{2,3},{3,2},{4,5},{5,4},{6,7},{7,6},{8,9},{9,8},{10,11... | collective-permute-start | bytes 1572872 | tf_op jit(solution)/shard_map/ppermute | solution.py:330
  25.2 5.0 %collective-permute-done.modes_ref = f32[1024,256]{1,0:T(8,128)S(1)} collective-permute-done((f32[1024,256]{1,0:T(8,128)}, f32[1024,256]{1,0:T(8,128)S(1)}, u32[]{:S(2)}, u32[]{:S(2)}) %collective-permute-start) | collective-permute-done | bytes 1048608 | tf_op jit(solution)/shard_map/ppermute | solution.py:330
  30.2 2.1 %collective-permute-start.3 = (f32[256,256]{1,0:T(8,128)S(1)}, f32[256,256]{1,0:T(8,128)S(1)}, u32[]{:S(2)}, u32[]{:S(2)}) collective-permute-start(f32[256,256]{1,0:T(8,128)S(1)} %get-tuple-element.33), channel_id=1, source_target_pairs={{0,1},{1,0},{2,3},{3,2},{4,5},{5,4},{6,7},{7,6},{8,9},{9,8},{10,11... | collective-permute-start | bytes 786440 | tf_op jit(solution)/shard_map/ppermute | solution.py:330
  32.3 0.0 collective-permute-done.1.eig_ref
  32.3 5.7 %shard_map.97.acc_in = f32[8,256,512]{2,1,0:T(8,128)S(1)} custom-call(s32[3]{0:T(128)S(1)} %pad_add_fusion.info, s32[8,4]{1,0:T(8,128)S(1)} %copy.21.adjacency, f32[1024,256]{1,0:T(8,128)S(1)} %collective-permute-done.modes_ref, f32[8,256]{1,0:T(8,128)S(1)} %collective-permute-done.1.eig_ref, bf16[4,2,2,256,256]{4,3,2,1,0:T(8,128)(2,1)S(1)} %get-tuple-element.25.s_ref, ...), custom_call_target="tpu_custom_call" | custom-call | flops 3221225472 | bytes 12582912 | tf_op jit(solution)/shard_map/pallas_call | solution.py:155
  38.0 0.2 collective-permute-start.2
  38.2 3.4 %collective-permute-done.4.modes_ref = f32[512,256]{1,0:T(8,128)S(1)} collective-permute-done((f32[512,256]{1,0:T(8,128)S(1)}, f32[512,256]{1,0:T(8,128)S(1)}, u32[]{:S(2)}, u32[]{:S(2)}) %collective-permute-start.4) | collective-permute-done | bytes 524320 | tf_op jit(solution)/shard_map/ppermute | solution.py:330
  41.7 3.3 %shard_map.98.acc_ref = f32[8,256,512]{2,1,0:T(8,128)S(1)} custom-call(s32[3]{0:T(128)S(1)} %pad_add_fusion.info, s32[8,4]{1,0:T(8,128)S(1)} %copy.21.adjacency, f32[512,256]{1,0:T(8,128)S(1)} %collective-permute-done.4.modes_ref, f32[8,256]{1,0:T(8,128)S(1)} %collective-permute-done.1.eig_ref, bf16[4,2,2,256,256]{4,3,2,1,0:T(8,128)(2,1)S(1)} %get-tuple-element.31.s_ref, ...), custom_call_target="tpu_custom_call" | custom-call | flops 1610612736 | bytes 6291456 | tf_op jit(solution)/shard_map/pallas_call | solution.py:155
  45.0 1.2 %shard_map.99 = (f32[3,4,88,256]{3,2,1,0:T(8,128)S(1)}, f32[3,4,88,256]{3,2,1,0:T(8,128)S(1)}) custom-call(s32[3]{0:T(128)S(1)} %pad_add_fusion.info, f32[8,256,512]{2,1,0:T(8,128)S(1)} %shard_map.98.acc_ref), custom_call_target="tpu_custom_call" | custom-call | flops 8000000 | bytes 1048576 | tf_op jit(solution)/shard_map/pallas_call | solution.py:209
  46.1 1.1 %collective-permute-done.3.modes_ref = f32[256,256]{1,0:T(8,128)S(1)} collective-permute-done((f32[256,256]{1,0:T(8,128)S(1)}, f32[256,256]{1,0:T(8,128)S(1)}, u32[]{:S(2)}, u32[]{:S(2)}) %collective-permute-start.3) | collective-permute-done | bytes 262176 | tf_op jit(solution)/shard_map/ppermute | solution.py:330
  47.3 2.7 %shard_map.100 = (f32[3,4,88,256]{3,2,1,0:T(8,128)S(1)}, f32[3,4,88,256]{3,2,1,0:T(8,128)S(1)}) custom-call(s32[3]{0:T(128)S(1)} %pad_add_fusion.info, s32[8,4]{1,0:T(8,128)S(1)} %copy.21.adjacency, f32[256,256]{1,0:T(8,128)S(1)} %collective-permute-done.3.modes_ref, ...), custom_call_target="tpu_custom_call", output_to_operand_aliasing={{0}: (6, {}), {1}: (7, {})} | custom-call | flops 805306368 | bytes 3145728 | tf_op jit(solution)/shard_map/pallas_call | solution.py:263
  50.0 2.0 %collective-permute-done.2.modes_ref = f32[256,256]{1,0:T(8,128)S(1)} collective-permute-done((f32[256,256]{1,0:T(8,128)S(1)}, f32[256,256]{1,0:T(8,128)S(1)}, u32[]{:S(2)}, u32[]{:S(2)}) %collective-permute-start.2) | collective-permute-done | bytes 262176 | tf_op jit(solution)/shard_map/ppermute | solution.py:330
  52.1 2.7 %shard_map.101 = (f32[3,4,88,256]{3,2,1,0:T(8,128)S(1)}, f32[3,4,88,256]{3,2,1,0:T(8,128)S(1)}) custom-call(s32[3]{0:T(128)S(1)} %pad_add_fusion.info, s32[8,4]{1,0:T(8,128)S(1)} %copy.21.adjacency, f32[256,256]{1,0:T(8,128)S(1)} %collective-permute-done.2.modes_ref, ...), custom_call_target="tpu_custom_call", output_to_operand_aliasing={{0}: (6, {}), {1}: (7, {})} | custom-call | flops 805306368 | bytes 3145728 | tf_op jit(solution)/shard_map/pallas_call | solution.py:263
  54.8 0.1 collective-permute-start.5
  54.9 2.7 %collective-permute-done.5 = f32[3,4,88,256]{3,2,1,0:T(8,128)S(1)} collective-permute-done((f32[3,4,88,256]{3,2,1,0:T(8,128)S(1)}, f32[3,4,88,256]{3,2,1,0:T(8,128)S(1)}, u32[]{:S(2)}, u32[]{:S(2)}) %collective-permute-start.5) | collective-permute-done | bytes 1081376 | tf_op jit(solution)/shard_map/ppermute | solution.py:333
  57.6 0.1 fusion
  57.7 0.0 copy-start.3
  57.7 0.0 copy-start.4
  57.7 1.8 %collective-permute-start.10 = (f32[4,88,256]{2,1,0:T(8,128)S(1)}, f32[4,88,256]{2,1,0:T(8,128)S(1)}, u32[]{:S(2)}, u32[]{:S(2)}) collective-permute-start(f32[4,88,256]{2,1,0:T(8,128)S(1)} %get-tuple-element.42), channel_id=1, source_target_pairs={{0,1},{1,0},{2,3},{3,2},{4,5},{5,4},{6,7},{7,6},{8,9},{9,8},{10,11... | collective-permute-start | bytes 1081352 | tf_op jit(solution)/shard_map/ppermute | solution.py:330
  59.5 1.6 %collective-permute-start.6 = (f32[88,256]{1,0:T(8,128)S(1)}, f32[88,256]{1,0:T(8,128)S(1)}, u32[]{:S(2)}, u32[]{:S(2)}) collective-permute-start(f32[88,256]{1,0:T(8,128)S(1)} %get-tuple-element.49), channel_id=1, source_target_pairs={{0,4},{2,6},{4,0},{6,2},{8,12},{10,14},{12,8},{14,10},{1,5},{3,7},... | collective-permute-start | bytes 270344 | tf_op jit(solution)/shard_map/ppermute | solution.py:333
  61.2 2.6 %collective-permute-start.7 = (f32[88,256]{1,0:T(8,128)S(1)}, f32[88,256]{1,0:T(8,128)S(1)}, u32[]{:S(2)}, u32[]{:S(2)}) collective-permute-start(f32[88,256]{1,0:T(8,128)S(1)} %get-tuple-element.51), channel_id=1, source_target_pairs={{0,8},{2,10},{4,12},{6,14},{8,0},{10,2},{12,4},{14,6},{1,9},{3,11}... | collective-permute-start | bytes 270344 | tf_op jit(solution)/shard_map/ppermute | solution.py:333
  63.8 0.2 collective-permute-start.8
  64.0 4.2 %collective-permute-done.10 = f32[4,88,256]{2,1,0:T(8,128)S(1)} collective-permute-done((f32[4,88,256]{2,1,0:T(8,128)S(1)}, f32[4,88,256]{2,1,0:T(8,128)S(1)}, u32[]{:S(2)}, u32[]{:S(2)}) %collective-permute-start.10) | collective-permute-done | bytes 360480 | tf_op jit(solution)/shard_map/ppermute | solution.py:330
  68.2 0.1 fusion.2
  68.3 1.9 %collective-permute-start.11 = (f32[88,256]{1,0:T(8,128)S(1)}, f32[88,256]{1,0:T(8,128)S(1)}, u32[]{:S(2)}, u32[]{:S(2)}) collective-permute-start(f32[88,256]{1,0:T(8,128)S(1)} %get-tuple-element.46), channel_id=1, source_target_pairs={{0,4},{2,6},{4,0},{6,2},{8,12},{10,14},{12,8},{14,10},{1,5},{3,7},... | collective-permute-start | bytes 270344 | tf_op jit(solution)/shard_map/ppermute | solution.py:333
  70.2 2.6 %collective-permute-start.12 = (f32[88,256]{1,0:T(8,128)S(1)}, f32[88,256]{1,0:T(8,128)S(1)}, u32[]{:S(2)}, u32[]{:S(2)}) collective-permute-start(f32[88,256]{1,0:T(8,128)S(1)} %get-tuple-element.48), channel_id=1, source_target_pairs={{0,8},{2,10},{4,12},{6,14},{8,0},{10,2},{12,4},{14,6},{1,9},{3,11}... | collective-permute-start | bytes 270344 | tf_op jit(solution)/shard_map/ppermute | solution.py:333
  72.8 0.0 collective-permute-done.6
  72.8 0.0 collective-permute-start.13
  72.8 0.0 collective-permute-done.7
  72.8 0.0 collective-permute-done.8
  72.9 1.8 %collective-permute-start.9 = (f32[88,256]{1,0:T(8,128)S(1)}, f32[88,256]{1,0:T(8,128)S(1)}, u32[]{:S(2)}, u32[]{:S(2)}) collective-permute-start(f32[88,256]{1,0:T(8,128)S(1)} %fusion.8.early_mine), channel_id=1, source_target_pairs={{0,1},{1,0},{2,3},{3,2},{4,5},{5,4},{6,7},{7,6},{8,9},{9,8},{10,11... | collective-permute-start | bytes 270344 | tf_op jit(solution)/shard_map/ppermute | solution.py:330
  74.6 0.0 collective-permute-done.11
  74.6 4.9 %collective-permute-done.12 = f32[88,256]{1,0:T(8,128)S(1)} collective-permute-done((f32[88,256]{1,0:T(8,128)S(1)}, f32[88,256]{1,0:T(8,128)S(1)}, u32[]{:S(2)}, u32[]{:S(2)}) %collective-permute-start.12) | collective-permute-done | bytes 90144 | tf_op jit(solution)/shard_map/ppermute | solution.py:333
  79.5 0.0 collective-permute-done.13
  79.5 1.6 %collective-permute-start.14 = (f32[88,256]{1,0:T(8,128)S(1)}, f32[88,256]{1,0:T(8,128)S(1)}, u32[]{:S(2)}, u32[]{:S(2)}) collective-permute-start(f32[88,256]{1,0:T(8,128)S(1)} %fusion.5.mine), channel_id=1, source_target_pairs={{0,1},{1,0},{2,3},{3,2},{4,5},{5,4},{6,7},{7,6},{8,9},{9,8},{10,11... | collective-permute-start | bytes 270344 | tf_op jit(solution)/shard_map/ppermute | solution.py:330
  81.1 0.0 collective-permute-done.9.early_theirs
  81.1 3.0 %collective-permute-done.14.theirs = f32[88,256]{1,0:T(8,128)S(1)} collective-permute-done((f32[88,256]{1,0:T(8,128)S(1)}, f32[88,256]{1,0:T(8,128)S(1)}, u32[]{:S(2)}, u32[]{:S(2)}) %collective-permute-start.14) | collective-permute-done | bytes 90144 | tf_op jit(solution)/shard_map/ppermute | solution.py:330
  84.1 1.6 %shard_map.102 = (f32[1,128,256]{2,1,0:T(8,128)}, f32[1,128,256]{2,1,0:T(8,128)}) custom-call(s32[3]{0:T(128)S(1)} %pad_add_fusion.info, f32[88,256]{1,0:T(8,128)S(1)} %fusion.8.early_mine, f32[88,256]{1,0:T(8,128)S(1)} %collective-permute-done.9.early_theirs, f32[88,256]{1,0:T(8,128)S(1)} %fusion.5.mine, f32[88,256]{1,0:T(8,128)S(1)} %collective-permute-done.14.theirs, ...), custom_call_target="tpu_custom_call" | custom-call | tf_op jit(solution)/shard_map/pallas_call | solution.py:312
  (18 shorter events, 0.2 us)
Async XLA Ops:
  0.6 5.7 %copy-start = (f32[8,256,256]{2,1,0:T(8,128)S(1)}, f32[8,256,256]{2,1,0:T(8,128)}, u32[]{:S(2)}) copy-start(f32[8,256,256]{2,1,0:T(8,128)} %param.8) | copy-start | bytes 6291460
  0.6 5.4 %copy-start.6 = (s32[8,4]{0,1:T(4,128)S(1)}, s32[8,4]{0,1:T(4,128)}, u32[]{:S(2)}) copy-start(s32[8,4]{0,1:T(4,128)} %param.13) | copy-start | bytes 388
  0.7 5.5 %copy-start.7 = (s32[8,2,2]{0,2,1:T(2,128)S(1)}, s32[8,2,2]{0,2,1:T(2,128)}, u32[]{:S(2)}) copy-start(s32[8,2,2]{0,2,1:T(2,128)} %param.12) | copy-start | bytes 388
  0.7 5.7 %copy-start.5 = (f32[8,256]{1,0:T(8,128)S(1)}, f32[8,256]{1,0:T(8,128)}, u32[]{:S(2)}) copy-start(f32[8,256]{1,0:T(8,128)} %eig_ref.3) | copy-start | bytes 24580
  3.1 27.1 %collective-permute-start = (f32[1024,256]{1,0:T(8,128)}, f32[1024,256]{1,0:T(8,128)S(1)}, u32[]{:S(2)}, u32[]{:S(2)}) collective-permute-start(f32[1024,256]{1,0:T(8,128)} %bitcast.5), channel_id=1, source_target_pairs={{0,1},{1,0},{2,3},{3,2},{4,5},{5,4},{6,7},{7,6},{8,9},{9,8},{10,11... | collective-permute-start | bytes 3145736 | tf_op jit(solution)/shard_map/ppermute | solution.py:330
  6.3 2.2 %copy-start.1 = (f32[8,2,2,128,256]{4,3,2,1,0:T(8,128)S(1)}, f32[8,2,2,128,256]{4,3,2,1,0:T(8,128)}, u32[]{:S(2)}) copy-start(f32[8,2,2,128,256]{4,3,2,1,0:T(8,128)} %stiff_ref.4) | copy-start | bytes 12582916
  8.5 2.2 %copy-start.2 = (f32[8,2,2,128,256]{4,3,2,1,0:T(8,128)S(1)}, f32[8,2,2,128,256]{4,3,2,1,0:T(8,128)}, u32[]{:S(2)}) copy-start(f32[8,2,2,128,256]{4,3,2,1,0:T(8,128)} %mass_ref.4) | copy-start | bytes 12582916
  16.8 15.5 %collective-permute-start.1 = (f32[8,256]{1,0:T(8,128)S(1)}, f32[8,256]{1,0:T(8,128)S(1)}, u32[]{:S(2)}, u32[]{:S(2)}) collective-permute-start(f32[8,256]{1,0:T(8,128)S(1)} %copy-done.5), channel_id=1, source_target_pairs={{0,1},{1,0},{2,3},{3,2},{4,5},{5,4},{6,7},{7,6},{8,9},{9,8},{10,11... | collective-permute-start | bytes 24584 | tf_op jit(solution)/shard_map/ppermute | solution.py:330
  23.1 18.5 %collective-permute-start.4 = (f32[512,256]{1,0:T(8,128)S(1)}, f32[512,256]{1,0:T(8,128)S(1)}, u32[]{:S(2)}, u32[]{:S(2)}) collective-permute-start(f32[512,256]{1,0:T(8,128)S(1)} %bitcast.46), channel_id=1, source_target_pairs={{0,1},{1,0},{2,3},{3,2},{4,5},{5,4},{6,7},{7,6},{8,9},{9,8},{10,11... | collective-permute-start | bytes 1572872 | tf_op jit(solution)/shard_map/ppermute | solution.py:330
  30.2 17.0 %collective-permute-start.3 = (f32[256,256]{1,0:T(8,128)S(1)}, f32[256,256]{1,0:T(8,128)S(1)}, u32[]{:S(2)}, u32[]{:S(2)}) collective-permute-start(f32[256,256]{1,0:T(8,128)S(1)} %get-tuple-element.33), channel_id=1, source_target_pairs={{0,1},{1,0},{2,3},{3,2},{4,5},{5,4},{6,7},{7,6},{8,9},{9,8},{10,11... | collective-permute-start | bytes 786440 | tf_op jit(solution)/shard_map/ppermute | solution.py:330
  38.0 14.1 %collective-permute-start.2 = (f32[256,256]{1,0:T(8,128)S(1)}, f32[256,256]{1,0:T(8,128)S(1)}, u32[]{:S(2)}, u32[]{:S(2)}) collective-permute-start(f32[256,256]{1,0:T(8,128)S(1)} %get-tuple-element.30), channel_id=1, source_target_pairs={{0,1},{1,0},{2,3},{3,2},{4,5},{5,4},{6,7},{7,6},{8,9},{9,8},{10,11... | collective-permute-start | bytes 786440 | tf_op jit(solution)/shard_map/ppermute | solution.py:330
  54.8 2.8 %collective-permute-start.5 = (f32[3,4,88,256]{3,2,1,0:T(8,128)S(1)}, f32[3,4,88,256]{3,2,1,0:T(8,128)S(1)}, u32[]{:S(2)}, u32[]{:S(2)}) collective-permute-start(f32[3,4,88,256]{3,2,1,0:T(8,128)S(1)} %get-tuple-element.41), channel_id=1, source_target_pairs={{0,2},{2,0},{4,6},{6,4},{8,10},{10,8},{12,14},{14,12},{1,3},{3,1},... | collective-permute-start | bytes 3244040 | tf_op jit(solution)/shard_map/ppermute | solution.py:333
  57.7 26.4 %copy-start.3 = (f32[1,128,256]{2,1,0:T(8,128)S(1)}, f32[1,128,256]{2,1,0:T(8,128)}, u32[]{:S(2)}) copy-start(f32[1,128,256]{2,1,0:T(8,128)} %stiff_ref.5) | copy-start | bytes 393220
  57.7 26.4 %copy-start.4 = (f32[1,128,256]{2,1,0:T(8,128)S(1)}, f32[1,128,256]{2,1,0:T(8,128)}, u32[]{:S(2)}) copy-start(f32[1,128,256]{2,1,0:T(8,128)} %mass_ref.5) | copy-start | bytes 393220
  57.7 10.5 %collective-permute-start.10 = (f32[4,88,256]{2,1,0:T(8,128)S(1)}, f32[4,88,256]{2,1,0:T(8,128)S(1)}, u32[]{:S(2)}, u32[]{:S(2)}) collective-permute-start(f32[4,88,256]{2,1,0:T(8,128)S(1)} %get-tuple-element.42), channel_id=1, source_target_pairs={{0,1},{1,0},{2,3},{3,2},{4,5},{5,4},{6,7},{7,6},{8,9},{9,8},{10,11... | collective-permute-start | bytes 1081352 | tf_op jit(solution)/shard_map/ppermute | solution.py:330
  59.5 13.3 %collective-permute-start.6 = (f32[88,256]{1,0:T(8,128)S(1)}, f32[88,256]{1,0:T(8,128)S(1)}, u32[]{:S(2)}, u32[]{:S(2)}) collective-permute-start(f32[88,256]{1,0:T(8,128)S(1)} %get-tuple-element.49), channel_id=1, source_target_pairs={{0,4},{2,6},{4,0},{6,2},{8,12},{10,14},{12,8},{14,10},{1,5},{3,7},... | collective-permute-start | bytes 270344 | tf_op jit(solution)/shard_map/ppermute | solution.py:333
  61.2 11.6 %collective-permute-start.7 = (f32[88,256]{1,0:T(8,128)S(1)}, f32[88,256]{1,0:T(8,128)S(1)}, u32[]{:S(2)}, u32[]{:S(2)}) collective-permute-start(f32[88,256]{1,0:T(8,128)S(1)} %get-tuple-element.51), channel_id=1, source_target_pairs={{0,8},{2,10},{4,12},{6,14},{8,0},{10,2},{12,4},{14,6},{1,9},{3,11}... | collective-permute-start | bytes 270344 | tf_op jit(solution)/shard_map/ppermute | solution.py:333
  63.8 9.1 %collective-permute-start.8 = (f32[88,256]{1,0:T(8,128)S(1)}, f32[88,256]{1,0:T(8,128)S(1)}, u32[]{:S(2)}, u32[]{:S(2)}) collective-permute-start(f32[88,256]{1,0:T(8,128)S(1)} %get-tuple-element.50), channel_id=1, source_target_pairs={{0,12},{2,14},{4,8},{6,10},{8,4},{10,6},{12,0},{14,2},{1,13},{3,15... | collective-permute-start | bytes 270344 | tf_op jit(solution)/shard_map/ppermute | solution.py:333
  68.3 6.3 %collective-permute-start.11 = (f32[88,256]{1,0:T(8,128)S(1)}, f32[88,256]{1,0:T(8,128)S(1)}, u32[]{:S(2)}, u32[]{:S(2)}) collective-permute-start(f32[88,256]{1,0:T(8,128)S(1)} %get-tuple-element.46), channel_id=1, source_target_pairs={{0,4},{2,6},{4,0},{6,2},{8,12},{10,14},{12,8},{14,10},{1,5},{3,7},... | collective-permute-start | bytes 270344 | tf_op jit(solution)/shard_map/ppermute | solution.py:333
  70.2 9.3 %collective-permute-start.12 = (f32[88,256]{1,0:T(8,128)S(1)}, f32[88,256]{1,0:T(8,128)S(1)}, u32[]{:S(2)}, u32[]{:S(2)}) collective-permute-start(f32[88,256]{1,0:T(8,128)S(1)} %get-tuple-element.48), channel_id=1, source_target_pairs={{0,8},{2,10},{4,12},{6,14},{8,0},{10,2},{12,4},{14,6},{1,9},{3,11}... | collective-permute-start | bytes 270344 | tf_op jit(solution)/shard_map/ppermute | solution.py:333
  72.8 6.7 %collective-permute-start.13 = (f32[88,256]{1,0:T(8,128)S(1)}, f32[88,256]{1,0:T(8,128)S(1)}, u32[]{:S(2)}, u32[]{:S(2)}) collective-permute-start(f32[88,256]{1,0:T(8,128)S(1)} %get-tuple-element.47), channel_id=1, source_target_pairs={{0,12},{2,14},{4,8},{6,10},{8,4},{10,6},{12,0},{14,2},{1,13},{3,15... | collective-permute-start | bytes 270344 | tf_op jit(solution)/shard_map/ppermute | solution.py:333
  72.9 8.2 %collective-permute-start.9 = (f32[88,256]{1,0:T(8,128)S(1)}, f32[88,256]{1,0:T(8,128)S(1)}, u32[]{:S(2)}, u32[]{:S(2)}) collective-permute-start(f32[88,256]{1,0:T(8,128)S(1)} %fusion.8.early_mine), channel_id=1, source_target_pairs={{0,1},{1,0},{2,3},{3,2},{4,5},{5,4},{6,7},{7,6},{8,9},{9,8},{10,11... | collective-permute-start | bytes 270344 | tf_op jit(solution)/shard_map/ppermute | solution.py:330
  79.5 4.6 %collective-permute-start.14 = (f32[88,256]{1,0:T(8,128)S(1)}, f32[88,256]{1,0:T(8,128)S(1)}, u32[]{:S(2)}, u32[]{:S(2)}) collective-permute-start(f32[88,256]{1,0:T(8,128)S(1)} %fusion.5.mine), channel_id=1, source_target_pairs={{0,1},{1,0},{2,3},{3,2},{4,5},{5,4},{6,7},{7,6},{8,9},{9,8},{10,11... | collective-permute-start | bytes 270344 | tf_op jit(solution)/shard_map/ppermute | solution.py:330

commit v3 on v2

--- a/solution.py
+++ b/solution.py
@@ -10,7 +10,8 @@
 ROWT = 128
 LANES = 128
 GROUP = 8
-PIECE = (2 * ROWT + GROUP) // 3
+TRIANGLE = ROWT // 2 + GROUP
+PACKED = ROWT + 2 * TRIANGLE
 MIB = 1024 * 1024
 
 f32 = jnp.float32
@@ -166,29 +167,52 @@
     )(*scalars, modes, eigs, *pairs, acc)
 
 
+def folded(square):
+    half = ROWT // 2
+    row = lax.broadcasted_iota(jnp.int32, (half, ROWT), 0)
+    col = lax.broadcasted_iota(jnp.int32, (half, ROWT), 1)
+    top, bottom = square[:half], square[half:]
+    diagonal = jnp.sum(jnp.where(row == col, top, 0.0), axis=0, keepdims=True)
+    return jnp.where(col <= row + half, bottom, pltpu.roll(top, half, 1)), diagonal
+
+
+def unfolded(part, diagonal):
+    half = ROWT // 2
+    row = lax.broadcasted_iota(jnp.int32, (half, ROWT), 0)
+    col = lax.broadcasted_iota(jnp.int32, (half, ROWT), 1)
+    bottom = jnp.where(col < row + half, part, 0.0)
+    top = jnp.where((col > row) & (col < half), pltpu.roll(part, half, 1), 0.0)
+    single = jnp.concatenate([top, bottom], 0)
+    diagonals = [jnp.where(row == col, diagonal, 0.0), jnp.where(col == row + half, part, 0.0)]
+    return single + single.T + jnp.concatenate(diagonals, 0)
+
+
 def pack(sums):
-    row = lax.broadcasted_iota(jnp.int32, (ROWT, ROWT), 0)
-    col = lax.broadcasted_iota(jnp.int32, (ROWT, ROWT), 1)
-    packed, diagonals = [], []
+    corners, firsts, seconds = [], [], []
     for which in range(2):
         base = which * 2 * ROWT
         first = sums(slice(0, ROWT), slice(base, base + ROWT))
         second = sums(slice(ROWT, 2 * ROWT), slice(base + ROWT, base + 2 * ROWT))
         corner = sums(slice(ROWT, 2 * ROWT), slice(base, base + ROWT))
-        square = jnp.where(row > col, first, second)
-        diagonal = jnp.sum(jnp.where(row == col, first, 0.0), axis=0, keepdims=True)
         if which == 1:
             corner = corner + sums(slice(0, ROWT), slice(base + ROWT, base + 2 * ROWT)).T
-            square = square + jnp.where(row < col, first, second).T
-            diagonal = diagonal + diagonal
-        packed.append(jnp.concatenate([corner, square], 1))
-        diagonals.append(diagonal)
-    packed.append(jnp.broadcast_to(jnp.concatenate(diagonals, 1), (GROUP, 2 * LANES)))
-    return jnp.concatenate(packed, 0)
+            first, second = first + first.T, second + second.T
+        corners.append(corner)
+        firsts.append(folded(first))
+        seconds.append(folded(second))
+    triangles = []
+    for squares in (firsts, seconds):
+        parts, diagonals = (jnp.concatenate(x, 1) for x in zip(*squares, strict=True))
+        triangles.append(
+            jnp.concatenate([parts, jnp.broadcast_to(diagonals, (GROUP, 2 * ROWT))], 0)
+        )
+    return jnp.concatenate(corners, 1), *triangles
 
 
 def places(side):
-    return ((0, 0), (1, 2 - side), (2, 1 + side))
+    first = pl.ds(pl.multiple_of(ROWT + (1 - side) * TRIANGLE, GROUP), TRIANGLE)
+    second = pl.ds(pl.multiple_of(ROWT + side * TRIANGLE, GROUP), TRIANGLE)
+    return pl.ds(0, ROWT), first, second
 
 
 def pack_kernel(info, acc_ref, send_ref, keep_ref):
@@ -197,12 +221,12 @@
     def one(shift, carry):
         target = lax.bitwise_xor(chip, shift) * 2
         for owner, out_ref in ((target + 1 - core, send_ref), (target + core, keep_ref)):
-            packed = pack(lambda r, c, o=owner: acc_ref[o, r, c])
-            for piece, place in places(side):
-                out_ref[place, shift] = packed[piece * PIECE : (piece + 1) * PIECE]
+            parts = pack(lambda r, c, o=owner: acc_ref[o, r, c])
+            for part, rows in zip(parts, places(side), strict=True):
+                out_ref[shift, rows, :] = part
         return carry
 
-    lax.fori_loop(0, send_ref.shape[1], one, 0)
+    lax.fori_loop(0, send_ref.shape[0], one, 0)
 
 
 def packed_sums(info, acc, shape):
@@ -227,7 +251,7 @@
         shift = lax.bitwise_xor(owner // 2, chip)
         mine = lax.rem(owner, 2) == core
         for here, ref in ((mine, keep_ref), (jnp.logical_not(mine), send_ref)):
-            ends = (ref.at[:, shift], held.at[slot])
+            ends = (ref.at[shift], held.at[slot])
             source, target = ends if inward else ends[::-1]
             yield here, pltpu.make_async_copy(source, target, sems.at[slot])
 
@@ -246,10 +270,10 @@
     inverse = 1.0 / eig_ref[sub : sub + 1, :]
     sums = contributions(modes_ref[...], inverse, pairs_of(s_ref), pairs_of(m_ref))
     for slot, update in enumerate(sums):
-        packed = pack(lambda r, c, u=update: u[r, c])
+        parts = pack(lambda r, c, u=update: u[r, c])
         run(slot, True, True)
-        for piece, place in places(side):
-            held[slot, place] += packed[piece * PIECE : (piece + 1) * PIECE]
+        for part, rows in zip(parts, places(side), strict=True):
+            held[slot, rows, :] += part
         run(slot, False, False)
     for slot in range(slots):
         run(slot, False, True)
@@ -259,7 +283,6 @@
     slots, _, rows, width = pairs[0].shape[1:]
     held = modes.shape[1]
     anywhere = pl.BlockSpec(memory_space=pl.ANY)
-    _, _, *piece = sums[0].shape
     return pl.pallas_call(
         functools.partial(add_kernel, sub),
         grid=(1,),
@@ -270,7 +293,7 @@
         out_specs=[anywhere] * 2,
         out_shape=[jax.ShapeDtypeStruct(x.shape, f32) for x in sums],
         scratch_shapes=[
-            pltpu.VMEM((slots, sums[0].shape[0], *piece), f32),
+            pltpu.VMEM((slots, *sums[0].shape[1:]), f32),
             pltpu.SemaphoreType.DMA((slots,)),
         ],
         input_output_aliases={6: 0, 7: 1},
@@ -279,39 +302,32 @@
     )(*scalars, modes, eigs, *pairs, *sums)
 
 
-def unpack_kernel(info, early_mine, early_theirs, mine, theirs, stiff_ref, mass_ref, out_stiff, out_mass):
+def unpack_kernel(info, mine, theirs, triangle_ref, stiff_ref, mass_ref, out_stiff, out_mass):
     side = info[0]
-    row = lax.broadcasted_iota(jnp.int32, (ROWT, ROWT), 0)
-    col = lax.broadcasted_iota(jnp.int32, (ROWT, ROWT), 1)
-    a, b = mine[...], theirs[...]
-    packed = jnp.concatenate(
-        [early_mine[...] + early_theirs[...], jnp.where(side == 0, a, b), jnp.where(side == 0, b, a)], 0
-    )
+    half = ROWT // 2
     for which, (iface_ref, out_ref) in enumerate(((stiff_ref, out_stiff), (mass_ref, out_mass))):
         sign = -1.0 if which == 0 else 1.0
-        rows = packed[which * ROWT : (which + 1) * ROWT]
-        corner, square = rows[:, :LANES], rows[:, LANES:]
-        diagonal = packed[2 * ROWT : 2 * ROWT + 1, which * LANES : (which + 1) * LANES]
-        flipped = square.T
+        lanes = slice(which * ROWT, (which + 1) * ROWT)
+        corner = sign * (mine[:, lanes] + theirs[:, lanes])
+        square = sign * unfolded(triangle_ref[:half, lanes], triangle_ref[half : half + 1, lanes])
+        low, mid = slice(0, ROWT), slice(ROWT, 2 * ROWT)
 
         @pl.when(side == 0)
         def _():
-            first = jnp.where(row > col, square, jnp.where(row == col, diagonal, flipped))
-            out_ref[0, :, :LANES] = iface_ref[0, :, :LANES] + sign * first
-            out_ref[0, :, LANES:] = iface_ref[0, :, LANES:] + sign * corner.T
+            out_ref[0, :, low] = iface_ref[0, :, low] + square
+            out_ref[0, :, mid] = iface_ref[0, :, mid] + corner.T
 
         @pl.when(side != 0)
         def _():
-            second = jnp.where(row <= col, square, flipped)
-            out_ref[0, :, :LANES] = iface_ref[0, :, :LANES] + sign * corner
-            out_ref[0, :, LANES:] = iface_ref[0, :, LANES:] + sign * second
+            out_ref[0, :, low] = iface_ref[0, :, low] + corner
+            out_ref[0, :, mid] = iface_ref[0, :, mid] + square
 
 
 def unpack(info, sums, iface_stiff, iface_mass):
     vmem = pl.BlockSpec(memory_space=pltpu.VMEM)
     return pl.pallas_call(
         unpack_kernel,
-        in_specs=[pl.BlockSpec(memory_space=pltpu.SMEM)] + [vmem] * 6,
+        in_specs=[pl.BlockSpec(memory_space=pltpu.SMEM)] + [vmem] * 5,
         out_specs=(vmem, vmem),
         out_shape=(jax.ShapeDtypeStruct(iface_stiff.shape, f32),) * 2,
         compiler_params=params(8),
@@ -338,12 +354,13 @@
     half = subs // 2
     cuts = [0, half, subs - 2, subs - 1, subs]
     pieces = [flat[a * rows : b * rows] for a, b in zip(cuts[:-1], cuts[1:], strict=True)]
+    pieces[0], flat, eigvals, stiff, mass = after(pieces[0], flat, eigvals, stiff, mass)
     came = [swap(pieces[0])]
     local = functools.partial(local_sums, [info, blocks, adjacency], flat, eigvals, stiff, mass)
-    *early, acc = local(0, half, 28, n_wide)
+    *early, acc = local(0, half, 48, n_wide)
     sent, acc = after(eigvals, acc)
     eigs = swap(sent)
-    *late, acc = local(half, subs - half, 28, n_wide, acc)
+    *late, acc = local(half, subs - half, 48, n_wide, acc)
     sent, acc = after(pieces[1], acc)
     came.append(swap(sent))
     sent, came[0] = after(pieces[2], came[0])
@@ -354,24 +371,25 @@
     sent, acc = after(pieces[3], acc)
     came.append(swap(sent))
     acc = arrived_sums(scalars, came[1], eigs, late, half, 0, cuts[2] - half, acc)
-    sums = packed_sums(info, acc, (3, chips, PIECE, 2 * LANES))
+    sums = packed_sums(info, acc, (chips, PACKED, 2 * ROWT))
     for k in (2, 3):
         sums = added_sums(scalars, came[k], eigs, late, cuts[k], cuts[k] - half, sums)
     send, keep = sums
 
     def over_chips(x):
-        total = x[0]
-        for shift in range(1, chips):
-            total = total + over_wide(x[shift], 2 * shift)
-        return total
-
+        parts = [over_wide(x[shift], 2 * shift) for shift in range(chips - 1, 0, -1)]
+        return sum(parts, x[0])
+
+    away, home = slice(ROWT, ROWT + TRIANGLE), slice(ROWT + TRIANGLE, PACKED)
     got = over_wide(send, 1)
-    away = swap(keep[1] + got[1])
-    first = over_chips(keep[0] + got[0])
-    first_theirs = swap(first)
-    second = over_chips(keep[2] + got[2] + away)
-    second_theirs = swap(second)
-    return unpack(info, (first, first_theirs, second, second_theirs), iface_stiff, iface_mass)
+    corners = keep[:, :ROWT] + got[:, :ROWT]
+    corner = over_chips(corners)
+    sent, corners = after(keep[:, away] + got[:, away], corners)
+    came_away = swap(sent)
+    corner_theirs = swap(corner)
+    came_away, corner = after(came_away, corner)
+    triangle = over_chips(keep[:, home] + got[:, home] + came_away)
+    return unpack(info, (corner, corner_theirs, triangle), iface_stiff, iface_mass)
 
 
 def grouped(modes, eigvals, stiff, mass, blocks, adjacency, iface_stiff, iface_mass):

time: 86 us -> 83.3 us (0.969)
  Pallas kernels: 29.6 us -> 36.3 us
  waiting for transfers between devices: 26.4 us -> 20.2 us
  starting transfers between devices: 21.5 us -> 19.4 us
  local copies, waits for them, and re-layouts: 7.13 us -> 5.88 us
    ppermute x8 -> x7, waiting for transfers between devices: 18.9 us -> 5.91 us  [swap(): return lax.ppermute(x, 'narrow', [(0, 1), (1, 0)])]
    ppermute x7, waiting for transfers between devices: 7.57 us -> 14.3 us  [over_wide(): return lax.ppermute(x, 'wide', [(i, i ^ mask) for i in range(n_wide)])]
    pallas_call x2, Pallas kernels: 12.3 us -> 18.8 us  [local_sums(): pl.pallas_call(functools.partial(local_kernel, start, acc is not None), g...]
    unnamed x18 -> x14, local copies, waits for them, and re-layouts: 4.58 us -> 2.39 us
    ppermute x8 -> x7, starting transfers between devices: 12.5 us -> 10.4 us  [swap(): return lax.ppermute(x, 'narrow', [(0, 1), (1, 0)])]
    slice x3, local copies, waits for them, and re-layouts: 2.51 us -> 3.45 us  [paired(): flat[a * rows:b * rows]]
  transfers between devices with their start and end apart: 15 -> 14, of which waited for: 8 -> 10; matrix products, arithmetic and copies ran while one was open for 1% -> 3% of each run, Pallas kernels for 29% -> 39%
where the time goes in v3:
time: 83.3 us; the launch traced here: 82.9 us
  Pallas kernels  36.3 us (44%)
  waiting for transfers between devices  20.2 us (24%)
  starting transfers between devices  19.4 us (23%)
  local copies, waits for them, and re-layouts  5.88 us (7%)
    pallas_call x2, Pallas kernels, local_sums(): pl.pallas_call(functools.partial(local_kernel, start, acc is not None), g...  18.8 us
    ppermute x7, waiting for transfers between devices, over_wide(): return lax.ppermute(x, 'wide', [(i, i ^ mask) for i in range(n_wide)])  14.3 us
    ppermute x7, starting transfers between devices, swap(): return lax.ppermute(x, 'narrow', [(0, 1), (1, 0)])  10.4 us
    ppermute x7, starting transfers between devices, over_wide(): return lax.ppermute(x, 'wide', [(i, i ^ mask) for i in range(n_wide)])  9.07 us
    pallas_call x2, Pallas kernels, arrived_sums(): pl.pallas_call(functools.partial(sum_kernel, start), grid=(count,), in_sp...  9.04 us
    ppermute x7, waiting for transfers between devices, swap(): return lax.ppermute(x, 'narrow', [(0, 1), (1, 0)])  5.91 us
    pallas_call x2, Pallas kernels, added_sums(): pl.pallas_call(functools.partial(add_kernel, sub), grid=(1,), in_specs=[p...  5.2 us
    slice x3, local copies, waits for them, and re-layouts, paired(): flat[a * rows:b * rows]  3.45 us
  transfers between devices with their start and end apart: 14, of which 10 were waited for; matrix products, arithmetic and copies ran while one was open for 3% of the time, Pallas kernels for 39%

profile of v3, /device:TPU:0, one launch (start us, length us, event | category | flops | bytes accessed | tf_op | source)
XLA Modules:
  0.0 82.9 jit_solution(18123170423038437004)
XLA Ops:
  0.7 1.3 %slice.70 = f32[4,256,256]{2,1,0:T(8,128)S(1)} slice(f32[8,256,256]{2,1,0:T(8,128)} %param.8), slice={[0:4], [0:256], [0:256]} | slice | bytes 2097152 | tf_op jit(solution)/shard_map/slice | solution.py:356
  2.0 3.0 %collective-permute-start = (f32[1024,256]{1,0:T(8,128)S(1)}, f32[1024,256]{1,0:T(8,128)S(1)}, u32[]{:S(2)}, u32[]{:S(2)}) collective-permute-start(f32[1024,256]{1,0:T(8,128)S(1)} %bitcast.40), channel_id=1, source_target_pairs={{0,1},{1,0},{2,3},{3,2},{4,5},{5,4},{6,7},{7,6},{8,9},{9,8},{10,11... | collective-permute-start | bytes 3145736 | tf_op jit(solution)/shard_map/ppermute | solution.py:346
  5.0 0.1 copy.21.adjacency
  5.1 0.0 copy-done.5
  5.1 0.1 copy.14.blocks
  5.2 0.1 pad_add_fusion.info
  5.2 8.5 %shard_map.95 = (bf16[4,2,2,256,256]{4,3,2,1,0:T(8,128)(2,1)S(1)}, bf16[4,2,2,256,256]{4,3,2,1,0:T(8,128)(2,1)S(1)}, f32[8,256,512]{2,1,0:T(8,128)}) custom-call(s32[3]{0:T(128)S(1)} %pad_add_fusion.info, s32[8,2,2]{2,1,0:T(2,128)S(1)} %copy.14.blocks, s32[8,4]{1,0:T(8,128)S(1)} %copy.21.adjacency, f32[2048,256]{1,0:T(8,128)} %bitcast.38, ...), custom_call_target="tpu_custom_call" | custom-call | flops 3221225472 | bytes 12582912 | tf_op jit(solution)/shard_map/pallas_call | solution.py:117
  13.8 0.0 collective-permute-start.1
  13.8 1.1 %slice.72 = f32[2,256,256]{2,1,0:T(8,128)S(1)} slice(f32[8,256,256]{2,1,0:T(8,128)} %param.8), slice={[4:6], [0:256], [0:256]} | slice | bytes 1048576 | tf_op jit(solution)/shard_map/slice | solution.py:356
  14.9 10.2 %shard_map.96 = (bf16[4,2,2,256,256]{4,3,2,1,0:T(8,128)(2,1)S(1)}, bf16[4,2,2,256,256]{4,3,2,1,0:T(8,128)(2,1)S(1)}, f32[8,256,512]{2,1,0:T(8,128)}) custom-call(s32[3]{0:T(128)S(1)} %pad_add_fusion.info, s32[8,2,2]{2,1,0:T(2,128)S(1)} %copy.14.blocks, s32[8,4]{1,0:T(8,128)S(1)} %copy.21.adjacency, f32[2048,256]{1,0:T(8,128)} %bitcast.39, ...), custom_call_target="tpu_custom_call" | custom-call | flops 3221225472 | bytes 12582912 | tf_op jit(solution)/shard_map/pallas_call | solution.py:117
  25.1 2.0 %collective-permute-start.4 = (f32[512,256]{1,0:T(8,128)S(1)}, f32[512,256]{1,0:T(8,128)S(1)}, u32[]{:S(2)}, u32[]{:S(2)}) collective-permute-start(f32[512,256]{1,0:T(8,128)S(1)} %bitcast.41), channel_id=1, source_target_pairs={{0,1},{1,0},{2,3},{3,2},{4,5},{5,4},{6,7},{7,6},{8,9},{9,8},{10,11... | collective-permute-start | bytes 1572872 | tf_op jit(solution)/shard_map/ppermute | solution.py:346
  27.1 1.1 %slice_bitcast_fusion = (f32[256,256]{1,0:T(8,128)S(1)}, f32[256,256]{1,0:T(8,128)S(1)}) fusion(f32[8,256,256]{2,1,0:T(8,128)} %param.8), kind=kLoop, calls=%fused_computation.4 | loop fusion | bytes 1048576 | tf_op jit(solution)/shard_map/slice | solution.py:356
  28.2 0.8 collective-permute-done.modes_ref
  29.0 1.9 %collective-permute-start.3 = (f32[256,256]{1,0:T(8,128)S(1)}, f32[256,256]{1,0:T(8,128)S(1)}, u32[]{:S(2)}, u32[]{:S(2)}) collective-permute-start(f32[256,256]{1,0:T(8,128)S(1)} %get-tuple-element.46), channel_id=1, source_target_pairs={{0,1},{1,0},{2,3},{3,2},{4,5},{5,4},{6,7},{7,6},{8,9},{9,8},{10,11... | collective-permute-start | bytes 786440 | tf_op jit(solution)/shard_map/ppermute | solution.py:346
  30.9 0.0 collective-permute-done.1.eig_ref
  30.9 2.2 %copy-done = f32[8,256,512]{2,1,0:T(8,128)S(1)} copy-done((f32[8,256,512]{2,1,0:T(8,128)S(1)}, f32[8,256,512]{2,1,0:T(8,128)}, u32[]{:S(2)}) %copy-start) | copy-done | bytes 4194328
  33.1 5.7 %shard_map.97.acc_in = f32[8,256,512]{2,1,0:T(8,128)S(1)} custom-call(s32[3]{0:T(128)S(1)} %pad_add_fusion.info, s32[8,4]{1,0:T(8,128)S(1)} %copy.21.adjacency, f32[1024,256]{1,0:T(8,128)S(1)} %collective-permute-done.modes_ref, f32[8,256]{1,0:T(8,128)S(1)} %collective-permute-done.1.eig_ref, bf16[4,2,2,256,256]{4,3,2,1,0:T(8,128)(2,1)S(1)} %get-tuple-element.38.s_ref, ...), custom_call_target="tpu_custom_call" | custom-call | flops 3221225472 | bytes 12582912 | tf_op jit(solution)/shard_map/pallas_call | solution.py:156
  38.8 0.2 collective-permute-start.2
  39.1 1.3 %collective-permute-done.4.modes_ref = f32[512,256]{1,0:T(8,128)S(1)} collective-permute-done((f32[512,256]{1,0:T(8,128)S(1)}, f32[512,256]{1,0:T(8,128)S(1)}, u32[]{:S(2)}, u32[]{:S(2)}) %collective-permute-start.4) | collective-permute-done | bytes 524320 | tf_op jit(solution)/shard_map/ppermute | solution.py:346
  40.4 3.3 %shard_map.98.acc_ref = f32[8,256,512]{2,1,0:T(8,128)S(1)} custom-call(s32[3]{0:T(128)S(1)} %pad_add_fusion.info, s32[8,4]{1,0:T(8,128)S(1)} %copy.21.adjacency, f32[512,256]{1,0:T(8,128)S(1)} %collective-permute-done.4.modes_ref, f32[8,256]{1,0:T(8,128)S(1)} %collective-permute-done.1.eig_ref, bf16[4,2,2,256,256]{4,3,2,1,0:T(8,128)(2,1)S(1)} %get-tuple-element.44.s_ref, ...), custom_call_target="tpu_custom_call" | custom-call | flops 1610612736 | bytes 6291456 | tf_op jit(solution)/shard_map/pallas_call | solution.py:156
  43.7 1.6 %shard_map.99 = (f32[4,272,256]{2,1,0:T(8,128)S(1)}, f32[4,272,256]{2,1,0:T(8,128)S(1)}) custom-call(s32[3]{0:T(128)S(1)} %pad_add_fusion.info, f32[8,256,512]{2,1,0:T(8,128)S(1)} %shard_map.98.acc_ref), custom_call_target="tpu_custom_call" | custom-call | flops 8000000 | bytes 1048576 | tf_op jit(solution)/shard_map/pallas_call | solution.py:233
  45.3 0.7 collective-permute-done.3.modes_ref
  46.0 2.6 %shard_map.100 = (f32[4,272,256]{2,1,0:T(8,128)S(1)}, f32[4,272,256]{2,1,0:T(8,128)S(1)}) custom-call(s32[3]{0:T(128)S(1)} %pad_add_fusion.info, s32[8,4]{1,0:T(8,128)S(1)} %copy.21.adjacency, f32[256,256]{1,0:T(8,128)S(1)} %collective-permute-done.3.modes_ref, ...), custom_call_target="tpu_custom_call", output_to_operand_aliasing={{0}: (6, {}), {1}: (7, {})} | custom-call | flops 805306368 | bytes 3145728 | tf_op jit(solution)/shard_map/pallas_call | solution.py:286
  48.6 2.2 %collective-permute-done.2.modes_ref = f32[256,256]{1,0:T(8,128)S(1)} collective-permute-done((f32[256,256]{1,0:T(8,128)S(1)}, f32[256,256]{1,0:T(8,128)S(1)}, u32[]{:S(2)}, u32[]{:S(2)}) %collective-permute-start.2) | collective-permute-done | bytes 262176 | tf_op jit(solution)/shard_map/ppermute | solution.py:346
  50.8 2.6 %shard_map.101 = (f32[4,272,256]{2,1,0:T(8,128)S(1)}, f32[4,272,256]{2,1,0:T(8,128)S(1)}) custom-call(s32[3]{0:T(128)S(1)} %pad_add_fusion.info, s32[8,4]{1,0:T(8,128)S(1)} %copy.21.adjacency, f32[256,256]{1,0:T(8,128)S(1)} %collective-permute-done.2.modes_ref, ...), custom_call_target="tpu_custom_call", output_to_operand_aliasing={{0}: (6, {}), {1}: (7, {})} | custom-call | flops 805306368 | bytes 3145728 | tf_op jit(solution)/shard_map/pallas_call | solution.py:286
  53.4 0.1 collective-permute-start.5
  53.5 2.7 %collective-permute-done.5 = f32[4,272,256]{2,1,0:T(8,128)S(1)} collective-permute-done((f32[4,272,256]{2,1,0:T(8,128)S(1)}, f32[4,272,256]{2,1,0:T(8,128)S(1)}, u32[]{:S(2)}, u32[]{:S(2)}) %collective-permute-start.5) | collective-permute-done | bytes 1114144 | tf_op jit(solution)/shard_map/ppermute | solution.py:349
  56.2 0.1 slice_add_fusion
  56.3 3.9 %collective-permute-start.7 = (f32[128,256]{1,0:T(8,128)S(1)}, f32[128,256]{1,0:T(8,128)S(1)}, u32[]{:S(2)}, u32[]{:S(2)}) collective-permute-start(f32[128,256]{1,0:T(8,128)S(1)} %get-tuple-element.60), channel_id=1, source_target_pairs={{0,12},{2,14},{4,8},{6,10},{8,4},{10,6},{12,0},{14,2},{1,13},{3,15... | collective-permute-start | bytes 393224 | tf_op jit(solution)/shard_map/ppermute | solution.py:349
  60.2 0.0 collective-permute-start.8
  60.2 0.6 collective-permute-start.9
  60.9 1.7 %collective-permute-start.6 = (f32[4,72,256]{2,1,0:T(8,128)S(1)}, f32[4,72,256]{2,1,0:T(8,128)S(1)}, u32[]{:S(2)}, u32[]{:S(2)}) collective-permute-start(f32[4,72,256]{2,1,0:T(8,128)S(1)} %slice_add_fusion.2), channel_id=1, source_target_pairs={{0,1},{1,0},{2,3},{3,2},{4,5},{5,4},{6,7},{7,6},{8,9},{9,8},{10,11... | collective-permute-start | bytes 884744 | tf_op jit(solution)/shard_map/ppermute | solution.py:346
  62.6 2.0 %collective-permute-done.7 = f32[128,256]{1,0:T(8,128)S(1)} collective-permute-done((f32[128,256]{1,0:T(8,128)S(1)}, f32[128,256]{1,0:T(8,128)S(1)}, u32[]{:S(2)}, u32[]{:S(2)}) %collective-permute-start.7) | collective-permute-done | bytes 131104 | tf_op jit(solution)/shard_map/ppermute | solution.py:349
  64.6 7.0 %collective-permute-done.8 = f32[128,256]{1,0:T(8,128)S(1)} collective-permute-done((f32[128,256]{1,0:T(8,128)S(1)}, f32[128,256]{1,0:T(8,128)S(1)}, u32[]{:S(2)}, u32[]{:S(2)}) %collective-permute-start.8) | collective-permute-done | bytes 131104 | tf_op jit(solution)/shard_map/ppermute | solution.py:349
  71.6 0.0 collective-permute-done.9
  71.7 0.0 copy-start.1
  71.7 0.0 copy-start.2
  71.7 0.0 collective-permute-done.6
  71.7 0.1 fusion
  71.8 2.6 %collective-permute-start.11 = (f32[72,256]{1,0:T(8,128)S(1)}, f32[72,256]{1,0:T(8,128)S(1)}, u32[]{:S(2)}, u32[]{:S(2)}) collective-permute-start(f32[72,256]{1,0:T(8,128)S(1)} %get-tuple-element.63), channel_id=1, source_target_pairs={{0,12},{2,14},{4,8},{6,10},{8,4},{10,6},{12,0},{14,2},{1,13},{3,15... | collective-permute-start | bytes 221192 | tf_op jit(solution)/shard_map/ppermute | solution.py:349
  74.4 0.0 collective-permute-start.12
  74.4 1.9 %collective-permute-start.13 = (f32[72,256]{1,0:T(8,128)S(1)}, f32[72,256]{1,0:T(8,128)S(1)}, u32[]{:S(2)}, u32[]{:S(2)}) collective-permute-start(f32[72,256]{1,0:T(8,128)S(1)} %get-tuple-element.64), channel_id=1, source_target_pairs={{0,4},{2,6},{4,0},{6,2},{8,12},{10,14},{12,8},{14,10},{1,5},{3,7},... | collective-permute-start | bytes 221192 | tf_op jit(solution)/shard_map/ppermute | solution.py:349
  76.2 1.5 %collective-permute-start.10 = (f32[128,256]{1,0:T(8,128)S(1)}, f32[128,256]{1,0:T(8,128)S(1)}, u32[]{:S(2)}, u32[]{:S(2)}) collective-permute-start(f32[128,256]{1,0:T(8,128)S(1)} %fusion.3.mine), channel_id=1, source_target_pairs={{0,1},{1,0},{2,3},{3,2},{4,5},{5,4},{6,7},{7,6},{8,9},{9,8},{10,11... | collective-permute-start | bytes 393224 | tf_op jit(solution)/shard_map/ppermute | solution.py:346
  77.7 0.3 collective-permute-done.11
  78.0 2.3 %collective-permute-done.12 = f32[72,256]{1,0:T(8,128)S(1)} collective-permute-done((f32[72,256]{1,0:T(8,128)S(1)}, f32[72,256]{1,0:T(8,128)S(1)}, u32[]{:S(2)}, u32[]{:S(2)}) %collective-permute-start.12) | collective-permute-done | bytes 73760 | tf_op jit(solution)/shard_map/ppermute | solution.py:349
  80.3 0.0 collective-permute-done.13
  80.3 0.9 %collective-permute-done.10.theirs = f32[128,256]{1,0:T(8,128)S(1)} collective-permute-done((f32[128,256]{1,0:T(8,128)S(1)}, f32[128,256]{1,0:T(8,128)S(1)}, u32[]{:S(2)}, u32[]{:S(2)}) %collective-permute-start.10) | collective-permute-done | bytes 131104 | tf_op jit(solution)/shard_map/ppermute | solution.py:346
  81.2 1.7 %shard_map.102 = (f32[1,128,256]{2,1,0:T(8,128)}, f32[1,128,256]{2,1,0:T(8,128)}) custom-call(s32[3]{0:T(128)S(1)} %pad_add_fusion.info, f32[128,256]{1,0:T(8,128)S(1)} %fusion.3.mine, f32[128,256]{1,0:T(8,128)S(1)} %collective-permute-done.10.theirs, f32[72,256]{1,0:T(8,128)S(1)} %fusion.6.triangle_ref, f32[1,128,256]{2,1,0:T(8,128)S(1)} %copy-done.1, ...), custom_call_target="tpu_custom_call" | custom-call | tf_op jit(solution)/shard_map/pallas_call | solution.py:328
  (13 shorter events, 0.2 us)
Async XLA Ops:
  0.6 4.6 %copy-start.3 = (f32[8,256]{1,0:T(8,128)S(1)}, f32[8,256]{1,0:T(8,128)}, u32[]{:S(2)}) copy-start(f32[8,256]{1,0:T(8,128)} %eig_ref.1) | copy-start | bytes 24580
  0.6 4.3 %copy-start.4 = (s32[8,4]{0,1:T(4,128)S(1)}, s32[8,4]{0,1:T(4,128)}, u32[]{:S(2)}) copy-start(s32[8,4]{0,1:T(4,128)} %param.13) | copy-start | bytes 388
  0.7 4.4 %copy-start.5 = (s32[8,2,2]{0,2,1:T(2,128)S(1)}, s32[8,2,2]{0,2,1:T(2,128)}, u32[]{:S(2)}) copy-start(s32[8,2,2]{0,2,1:T(2,128)} %param.12) | copy-start | bytes 388
  2.0 27.0 %collective-permute-start = (f32[1024,256]{1,0:T(8,128)S(1)}, f32[1024,256]{1,0:T(8,128)S(1)}, u32[]{:S(2)}, u32[]{:S(2)}) collective-permute-start(f32[1024,256]{1,0:T(8,128)S(1)} %bitcast.40), channel_id=1, source_target_pairs={{0,1},{1,0},{2,3},{3,2},{4,5},{5,4},{6,7},{7,6},{8,9},{9,8},{10,11... | collective-permute-start | bytes 3145736 | tf_op jit(solution)/shard_map/ppermute | solution.py:346
  13.8 17.1 %collective-permute-start.1 = (f32[8,256]{1,0:T(8,128)S(1)}, f32[8,256]{1,0:T(8,128)S(1)}, u32[]{:S(2)}, u32[]{:S(2)}) collective-permute-start(f32[8,256]{1,0:T(8,128)S(1)} %copy-done.3), channel_id=1, source_target_pairs={{0,1},{1,0},{2,3},{3,2},{4,5},{5,4},{6,7},{7,6},{8,9},{9,8},{10,11... | collective-permute-start | bytes 24584 | tf_op jit(solution)/shard_map/ppermute | solution.py:346
  25.1 15.3 %collective-permute-start.4 = (f32[512,256]{1,0:T(8,128)S(1)}, f32[512,256]{1,0:T(8,128)S(1)}, u32[]{:S(2)}, u32[]{:S(2)}) collective-permute-start(f32[512,256]{1,0:T(8,128)S(1)} %bitcast.41), channel_id=1, source_target_pairs={{0,1},{1,0},{2,3},{3,2},{4,5},{5,4},{6,7},{7,6},{8,9},{9,8},{10,11... | collective-permute-start | bytes 1572872 | tf_op jit(solution)/shard_map/ppermute | solution.py:346
  29.0 17.0 %collective-permute-start.3 = (f32[256,256]{1,0:T(8,128)S(1)}, f32[256,256]{1,0:T(8,128)S(1)}, u32[]{:S(2)}, u32[]{:S(2)}) collective-permute-start(f32[256,256]{1,0:T(8,128)S(1)} %get-tuple-element.46), channel_id=1, source_target_pairs={{0,1},{1,0},{2,3},{3,2},{4,5},{5,4},{6,7},{7,6},{8,9},{9,8},{10,11... | collective-permute-start | bytes 786440 | tf_op jit(solution)/shard_map/ppermute | solution.py:346
  30.9 2.2 %copy-start = (f32[8,256,512]{2,1,0:T(8,128)S(1)}, f32[8,256,512]{2,1,0:T(8,128)}, u32[]{:S(2)}) copy-start(f32[8,256,512]{2,1,0:T(8,128)} %get-tuple-element.42.acc_in) | copy-start | bytes 12582916
  38.8 12.0 %collective-permute-start.2 = (f32[256,256]{1,0:T(8,128)S(1)}, f32[256,256]{1,0:T(8,128)S(1)}, u32[]{:S(2)}, u32[]{:S(2)}) collective-permute-start(f32[256,256]{1,0:T(8,128)S(1)} %get-tuple-element.43), channel_id=1, source_target_pairs={{0,1},{1,0},{2,3},{3,2},{4,5},{5,4},{6,7},{7,6},{8,9},{9,8},{10,11... | collective-permute-start | bytes 786440 | tf_op jit(solution)/shard_map/ppermute | solution.py:346
  53.4 2.8 %collective-permute-start.5 = (f32[4,272,256]{2,1,0:T(8,128)S(1)}, f32[4,272,256]{2,1,0:T(8,128)S(1)}, u32[]{:S(2)}, u32[]{:S(2)}) collective-permute-start(f32[4,272,256]{2,1,0:T(8,128)S(1)} %get-tuple-element.54), channel_id=1, source_target_pairs={{0,2},{2,0},{4,6},{6,4},{8,10},{10,8},{12,14},{14,12},{1,3},{3,1},... | collective-permute-start | bytes 3342344 | tf_op jit(solution)/shard_map/ppermute | solution.py:349
  56.3 8.3 %collective-permute-start.7 = (f32[128,256]{1,0:T(8,128)S(1)}, f32[128,256]{1,0:T(8,128)S(1)}, u32[]{:S(2)}, u32[]{:S(2)}) collective-permute-start(f32[128,256]{1,0:T(8,128)S(1)} %get-tuple-element.60), channel_id=1, source_target_pairs={{0,12},{2,14},{4,8},{6,10},{8,4},{10,6},{12,0},{14,2},{1,13},{3,15... | collective-permute-start | bytes 393224 | tf_op jit(solution)/shard_map/ppermute | solution.py:349
  60.2 11.4 %collective-permute-start.8 = (f32[128,256]{1,0:T(8,128)S(1)}, f32[128,256]{1,0:T(8,128)S(1)}, u32[]{:S(2)}, u32[]{:S(2)}) collective-permute-start(f32[128,256]{1,0:T(8,128)S(1)} %get-tuple-element.62), channel_id=1, source_target_pairs={{0,8},{2,10},{4,12},{6,14},{8,0},{10,2},{12,4},{14,6},{1,9},{3,11}... | collective-permute-start | bytes 393224 | tf_op jit(solution)/shard_map/ppermute | solution.py:349
  60.2 11.4 %collective-permute-start.9 = (f32[128,256]{1,0:T(8,128)S(1)}, f32[128,256]{1,0:T(8,128)S(1)}, u32[]{:S(2)}, u32[]{:S(2)}) collective-permute-start(f32[128,256]{1,0:T(8,128)S(1)} %get-tuple-element.61), channel_id=1, source_target_pairs={{0,4},{2,6},{4,0},{6,2},{8,12},{10,14},{12,8},{14,10},{1,5},{3,7},... | collective-permute-start | bytes 393224 | tf_op jit(solution)/shard_map/ppermute | solution.py:349
  60.9 10.8 %collective-permute-start.6 = (f32[4,72,256]{2,1,0:T(8,128)S(1)}, f32[4,72,256]{2,1,0:T(8,128)S(1)}, u32[]{:S(2)}, u32[]{:S(2)}) collective-permute-start(f32[4,72,256]{2,1,0:T(8,128)S(1)} %slice_add_fusion.2), channel_id=1, source_target_pairs={{0,1},{1,0},{2,3},{3,2},{4,5},{5,4},{6,7},{7,6},{8,9},{9,8},{10,11... | collective-permute-start | bytes 884744 | tf_op jit(solution)/shard_map/ppermute | solution.py:346
  71.7 9.5 %copy-start.1 = (f32[1,128,256]{2,1,0:T(8,128)S(1)}, f32[1,128,256]{2,1,0:T(8,128)}, u32[]{:S(2)}) copy-start(f32[1,128,256]{2,1,0:T(8,128)} %stiff_ref.3) | copy-start | bytes 393220
  71.7 9.5 %copy-start.2 = (f32[1,128,256]{2,1,0:T(8,128)S(1)}, f32[1,128,256]{2,1,0:T(8,128)}, u32[]{:S(2)}) copy-start(f32[1,128,256]{2,1,0:T(8,128)} %mass_ref.3) | copy-start | bytes 393220
  71.8 6.2 %collective-permute-start.11 = (f32[72,256]{1,0:T(8,128)S(1)}, f32[72,256]{1,0:T(8,128)S(1)}, u32[]{:S(2)}, u32[]{:S(2)}) collective-permute-start(f32[72,256]{1,0:T(8,128)S(1)} %get-tuple-element.63), channel_id=1, source_target_pairs={{0,12},{2,14},{4,8},{6,10},{8,4},{10,6},{12,0},{14,2},{1,13},{3,15... | collective-permute-start | bytes 221192 | tf_op jit(solution)/shard_map/ppermute | solution.py:349
  74.4 5.9 %collective-permute-start.12 = (f32[72,256]{1,0:T(8,128)S(1)}, f32[72,256]{1,0:T(8,128)S(1)}, u32[]{:S(2)}, u32[]{:S(2)}) collective-permute-start(f32[72,256]{1,0:T(8,128)S(1)} %get-tuple-element.65), channel_id=1, source_target_pairs={{0,8},{2,10},{4,12},{6,14},{8,0},{10,2},{12,4},{14,6},{1,9},{3,11}... | collective-permute-start | bytes 221192 | tf_op jit(solution)/shard_map/ppermute | solution.py:349
  74.4 5.9 %collective-permute-start.13 = (f32[72,256]{1,0:T(8,128)S(1)}, f32[72,256]{1,0:T(8,128)S(1)}, u32[]{:S(2)}, u32[]{:S(2)}) collective-permute-start(f32[72,256]{1,0:T(8,128)S(1)} %get-tuple-element.64), channel_id=1, source_target_pairs={{0,4},{2,6},{4,0},{6,2},{8,12},{10,14},{12,8},{14,10},{1,5},{3,7},... | collective-permute-start | bytes 221192 | tf_op jit(solution)/shard_map/ppermute | solution.py:349
  76.2 5.0 %collective-permute-start.10 = (f32[128,256]{1,0:T(8,128)S(1)}, f32[128,256]{1,0:T(8,128)S(1)}, u32[]{:S(2)}, u32[]{:S(2)}) collective-permute-start(f32[128,256]{1,0:T(8,128)S(1)} %fusion.3.mine), channel_id=1, source_target_pairs={{0,1},{1,0},{2,3},{3,2},{4,5},{5,4},{6,7},{7,6},{8,9},{9,8},{10,11... | collective-permute-start | bytes 393224 | tf_op jit(solution)/shard_map/ppermute | solution.py:346

commit v4 on v3

--- a/solution.py
+++ b/solution.py
@@ -11,7 +11,6 @@
 LANES = 128
 GROUP = 8
 TRIANGLE = ROWT // 2 + GROUP
-PACKED = ROWT + 2 * TRIANGLE
 MIB = 1024 * 1024
 
 f32 = jnp.float32
@@ -123,7 +122,7 @@
         out_specs=[pair_spec, pair_spec, whole(shape)],
         out_shape=[pair, pair, jax.ShapeDtypeStruct(shape, f32)],
         compiler_params=params(limit),
-        cost_estimate=cost(count, rows, held, slots, width),
+        cost_estimate=pl.CostEstimate(flops=1000, bytes_accessed=1000, transcendentals=0),
     )(*scalars, flat, eigvals, stiff, mass, *given)
 
 
@@ -162,7 +161,7 @@
         + [once(acc.shape)],
         out_specs=whole(acc.shape),
         out_shape=jax.ShapeDtypeStruct(acc.shape, f32),
-        compiler_params=params(24),
+        compiler_params=params(48),
         cost_estimate=cost(count, rows, held, slots, width),
     )(*scalars, modes, eigs, *pairs, acc)
 
@@ -210,128 +209,98 @@
 
 
 def places(side):
-    first = pl.ds(pl.multiple_of(ROWT + (1 - side) * TRIANGLE, GROUP), TRIANGLE)
-    second = pl.ds(pl.multiple_of(ROWT + side * TRIANGLE, GROUP), TRIANGLE)
-    return pl.ds(0, ROWT), first, second
-
-
-def pack_kernel(info, acc_ref, send_ref, keep_ref):
+    first = pl.ds(pl.multiple_of((1 - side) * TRIANGLE, GROUP), TRIANGLE)
+    second = pl.ds(pl.multiple_of(side * TRIANGLE, GROUP), TRIANGLE)
+    return first, second
+
+
+def pack_kernel(info, acc_ref, send_corner, send_triangle, keep_corner, keep_triangle):
     side, chip, core = info[0], info[1], info[2]
 
     def one(shift, carry):
         target = lax.bitwise_xor(chip, shift) * 2
-        for owner, out_ref in ((target + 1 - core, send_ref), (target + core, keep_ref)):
-            parts = pack(lambda r, c, o=owner: acc_ref[o, r, c])
-            for part, rows in zip(parts, places(side), strict=True):
-                out_ref[shift, rows, :] = part
+        for owner, corner_ref, triangle_ref in (
+            (target + 1 - core, send_corner, send_triangle),
+            (target + core, keep_corner, keep_triangle),
+        ):
+            corner, *triangles = pack(lambda r, c, o=owner: acc_ref[o, r, c])
+            corner_ref[shift] = corner
+            for triangle, rows in zip(triangles, places(side), strict=True):
+                triangle_ref[shift, rows, :] = triangle
         return carry
 
-    lax.fori_loop(0, send_ref.shape[0], one, 0)
-
-
-def packed_sums(info, acc, shape):
+    lax.fori_loop(0, send_corner.shape[0], one, 0)
+
+
+def packed_sums(info, acc, shapes):
     return pl.pallas_call(
         pack_kernel,
         in_specs=[pl.BlockSpec(memory_space=pltpu.SMEM), pl.BlockSpec(memory_space=pltpu.VMEM)],
-        out_specs=[pl.BlockSpec(memory_space=pltpu.VMEM)] * 2,
-        out_shape=[jax.ShapeDtypeStruct(shape, f32)] * 2,
+        out_specs=[pl.BlockSpec(memory_space=pltpu.VMEM)] * 4,
+        out_shape=[jax.ShapeDtypeStruct(shape, f32) for shape in shapes * 2],
         compiler_params=params(16),
         cost_estimate=pl.CostEstimate(flops=8_000_000, bytes_accessed=MIB, transcendentals=0),
     )(info, acc)
 
 
-def add_kernel(
-    sub, info, adjacency, modes_ref, eig_ref, s_ref, m_ref, send_in, keep_in, send_ref, keep_ref, held, sems
-):
-    side, chip, core = info[0], info[1], info[2]
-    slots = s_ref.shape[1]
-
-    def copies(slot, inward):
-        owner = adjacency[sub, side * slots + slot]
-        shift = lax.bitwise_xor(owner // 2, chip)
-        mine = lax.rem(owner, 2) == core
-        for here, ref in ((mine, keep_ref), (jnp.logical_not(mine), send_ref)):
-            ends = (ref.at[shift], held.at[slot])
-            source, target = ends if inward else ends[::-1]
-            yield here, pltpu.make_async_copy(source, target, sems.at[slot])
-
-    def run(slot, inward, wait):
-        for here, copy in copies(slot, inward):
-
-            @pl.when(here)
-            def _(copy=copy):
-                if wait:
-                    copy.wait()
-                else:
-                    copy.start()
-
-    for slot in range(slots):
-        run(slot, True, False)
-    inverse = 1.0 / eig_ref[sub : sub + 1, :]
+def add_kernel(sub, lanes, modes_ref, eig_ref, s_ref, m_ref, owner_ref, side_ref, *refs):
+    chips, slots = refs[0].shape[0], s_ref.shape[1]
+    inverse = 1.0 / eig_ref[sub : sub + 1, lanes]
     sums = contributions(modes_ref[...], inverse, pairs_of(s_ref), pairs_of(m_ref))
-    for slot, update in enumerate(sums):
-        parts = pack(lambda r, c, u=update: u[r, c])
-        run(slot, True, True)
-        for part, rows in zip(parts, places(side), strict=True):
-            held[slot, rows, :] += part
-        run(slot, False, False)
-    for slot in range(slots):
-        run(slot, False, True)
-
-
-def added_sums(scalars, modes, eigs, pairs, sub, offset, sums):
+    zero_side = side_ref[0:1, :] == 0.0
+    corners, triangles = [], []
+    for update in sums:
+        corner, first, second = pack(lambda r, c, u=update: u[r, c])
+        away, home = jnp.where(zero_side, second, first), jnp.where(zero_side, first, second)
+        corners.append(corner)
+        triangles.append(jnp.concatenate([away, home], 0))
+    for k, packed in enumerate((corners, triangles, corners, triangles)):
+        in_ref, out_ref = refs[k], refs[4 + k]
+        for shift in range(chips):
+            total = in_ref[shift]
+            for slot in range(slots):
+                row = slot * 2 * chips + k // 2 * chips + shift
+                total = total + jnp.where(owner_ref[row : row + 1, :] > 0.0, packed[slot], 0.0)
+            out_ref[shift] = total
+
+
+def added_sums(modes, eigs, pairs, sub, offset, first, owners, side, sums):
     slots, _, rows, width = pairs[0].shape[1:]
     held = modes.shape[1]
-    anywhere = pl.BlockSpec(memory_space=pl.ANY)
+    vmem = pl.BlockSpec(memory_space=pltpu.VMEM)
     return pl.pallas_call(
-        functools.partial(add_kernel, sub),
+        functools.partial(add_kernel, sub, slice(first, first + held)),
         grid=(1,),
-        in_specs=[pl.BlockSpec(memory_space=pltpu.SMEM)] * 2
-        + [pl.BlockSpec((rows, held), lambda i: (i, 0)), whole(eigs.shape)]
-        + pair_specs(pairs, offset)
-        + [anywhere] * 2,
-        out_specs=[anywhere] * 2,
+        in_specs=[vmem] * 2 + pair_specs(pairs, offset) + [vmem] * 6,
+        out_specs=[vmem] * 4,
         out_shape=[jax.ShapeDtypeStruct(x.shape, f32) for x in sums],
-        scratch_shapes=[
-            pltpu.VMEM((slots, *sums[0].shape[1:]), f32),
-            pltpu.SemaphoreType.DMA((slots,)),
-        ],
-        input_output_aliases={6: 0, 7: 1},
         compiler_params=params(16),
         cost_estimate=cost(1, rows, held, slots, width),
-    )(*scalars, modes, eigs, *pairs, *sums)
-
-
-def unpack_kernel(info, mine, theirs, triangle_ref, stiff_ref, mass_ref, out_stiff, out_mass):
-    side = info[0]
+    )(modes, eigs, *pairs, owners, side, *sums)
+
+
+def unpack_kernel(side_ref, mine, theirs, triangle_ref, stiff_ref, mass_ref, out_stiff, out_mass):
     half = ROWT // 2
+    zero_side = side_ref[0:1, :LANES] == 0.0
+    low, mid = slice(0, ROWT), slice(ROWT, 2 * ROWT)
     for which, (iface_ref, out_ref) in enumerate(((stiff_ref, out_stiff), (mass_ref, out_mass))):
         sign = -1.0 if which == 0 else 1.0
         lanes = slice(which * ROWT, (which + 1) * ROWT)
         corner = sign * (mine[:, lanes] + theirs[:, lanes])
         square = sign * unfolded(triangle_ref[:half, lanes], triangle_ref[half : half + 1, lanes])
-        low, mid = slice(0, ROWT), slice(ROWT, 2 * ROWT)
-
-        @pl.when(side == 0)
-        def _():
-            out_ref[0, :, low] = iface_ref[0, :, low] + square
-            out_ref[0, :, mid] = iface_ref[0, :, mid] + corner.T
-
-        @pl.when(side != 0)
-        def _():
-            out_ref[0, :, low] = iface_ref[0, :, low] + corner
-            out_ref[0, :, mid] = iface_ref[0, :, mid] + square
-
-
-def unpack(info, sums, iface_stiff, iface_mass):
+        out_ref[0, :, low] = iface_ref[0, :, low] + jnp.where(zero_side, square, corner)
+        out_ref[0, :, mid] = iface_ref[0, :, mid] + jnp.where(zero_side, corner.T, square)
+
+
+def unpack(side, sums, iface_stiff, iface_mass):
     vmem = pl.BlockSpec(memory_space=pltpu.VMEM)
     return pl.pallas_call(
         unpack_kernel,
-        in_specs=[pl.BlockSpec(memory_space=pltpu.SMEM)] + [vmem] * 5,
+        in_specs=[vmem] * 6,
         out_specs=(vmem, vmem),
         out_shape=(jax.ShapeDtypeStruct(iface_stiff.shape, f32),) * 2,
         compiler_params=params(8),
-    )(info, *sums, iface_stiff, iface_mass)
+    )(side, *sums, iface_stiff, iface_mass)
 
 
 def paired(modes, eigvals, stiff, mass, blocks, adjacency, iface_stiff, iface_mass):
@@ -352,44 +321,60 @@
         return lax.optimization_barrier((x, *others))
 
     half = subs // 2
-    cuts = [0, half, subs - 2, subs - 1, subs]
+    cuts = [0, half, subs - 2, subs - 1]
     pieces = [flat[a * rows : b * rows] for a, b in zip(cuts[:-1], cuts[1:], strict=True)]
+    middle = held // 2 if False and held % (2 * LANES) == 0 else held
+    last = flat[(subs - 1) * rows :]
+    pieces += [last[:, lane : lane + middle] for lane in range(0, held, middle)]
     pieces[0], flat, eigvals, stiff, mass = after(pieces[0], flat, eigvals, stiff, mass)
     came = [swap(pieces[0])]
     local = functools.partial(local_sums, [info, blocks, adjacency], flat, eigvals, stiff, mass)
-    *early, acc = local(0, half, 48, n_wide)
-    sent, acc = after(eigvals, acc)
-    eigs = swap(sent)
-    *late, acc = local(half, subs - half, 48, n_wide, acc)
-    sent, acc = after(pieces[1], acc)
+    *pairs, acc = local(0, subs, 52, n_wide)
+    sent, own, acc = after(pieces[1], eigvals, acc)
+    eigs = swap(own)
     came.append(swap(sent))
-    sent, came[0] = after(pieces[2], came[0])
+    slots = stiff.shape[1]
+    chip, core = wide // 2, wide % 2
+    targets = (chip ^ jnp.arange(chips)) * 2
+    targets = jnp.concatenate([targets + 1 - core, targets + core])
+    mine = lax.dynamic_slice_in_dim(adjacency, side * slots, slots, 1)[cuts[2] :]
+    owners = (mine[:, :, None] == targets).astype(f32).reshape(-1, slots * 2 * chips, 1)
+    owners = jnp.broadcast_to(owners, (*owners.shape[:2], 2 * ROWT))
+    side_rows = jnp.full((GROUP, 2 * ROWT), side, f32)
+    sent, came[0], owners, side_rows = after(pieces[2], came[0], owners, side_rows)
     came.append(swap(sent))
 
     scalars = [info, adjacency]
-    acc = arrived_sums(scalars, came[0], eigs, early, 0, 0, half, acc)
+    lasts = [x[cuts[2] :] for x in pairs]
+    acc = arrived_sums(scalars, came[0], eigs, pairs, 0, 0, half, acc)
     sent, acc = after(pieces[3], acc)
     came.append(swap(sent))
-    acc = arrived_sums(scalars, came[1], eigs, late, half, 0, cuts[2] - half, acc)
-    sums = packed_sums(info, acc, (chips, PACKED, 2 * ROWT))
-    for k in (2, 3):
-        sums = added_sums(scalars, came[k], eigs, late, cuts[k], cuts[k] - half, sums)
-    send, keep = sums
+    acc = arrived_sums(scalars, came[1], eigs, pairs, half, half, cuts[2] - half, acc)
+    for piece in pieces[4:]:
+        sent, acc = after(piece, acc)
+        came.append(swap(sent))
+    sums = packed_sums(info, acc, [(chips, ROWT, 2 * ROWT), (chips, 2 * TRIANGLE, 2 * ROWT)])
+    singles = [(subs - 2, 0)] + [(subs - 1, lane) for lane in range(0, held, middle)]
+    for (sub, lane), modes_ in zip(singles, came[2:], strict=True):
+        sums = added_sums(
+            modes_, eigs, lasts, sub, sub - cuts[2], lane, owners[sub - cuts[2]], side_rows, sums
+        )
+    send_corner, send_triangle, keep_corner, keep_triangle = sums
 
     def over_chips(x):
         parts = [over_wide(x[shift], 2 * shift) for shift in range(chips - 1, 0, -1)]
         return sum(parts, x[0])
 
-    away, home = slice(ROWT, ROWT + TRIANGLE), slice(ROWT + TRIANGLE, PACKED)
-    got = over_wide(send, 1)
-    corners = keep[:, :ROWT] + got[:, :ROWT]
+    away, home = slice(0, TRIANGLE), slice(TRIANGLE, 2 * TRIANGLE)
+    corners = keep_corner + over_wide(send_corner, 1)
+    got = over_wide(send_triangle, 1)
     corner = over_chips(corners)
-    sent, corners = after(keep[:, away] + got[:, away], corners)
+    sent, corners = after(keep_triangle[:, away] + got[:, away], corners)
     came_away = swap(sent)
     corner_theirs = swap(corner)
     came_away, corner = after(came_away, corner)
-    triangle = over_chips(keep[:, home] + got[:, home] + came_away)
-    return unpack(info, (corner, corner_theirs, triangle), iface_stiff, iface_mass)
+    triangle = over_chips(keep_triangle[:, home] + got[:, home] + came_away)
+    return unpack(side_rows, (corner, corner_theirs, triangle), iface_stiff, iface_mass)
 
 
 def grouped(modes, eigvals, stiff, mass, blocks, adjacency, iface_stiff, iface_mass):

time: 83.3 us -> 80.6 us (0.968)
  local copies, waits for them, and re-layouts: 5.88 us -> 10.9 us
  waiting for transfers between devices: 20.2 us -> 15.4 us
  Pallas kernels: 36.3 us -> 32.7 us
    slice x0 -> x5, local copies, waits for them, and re-layouts: none -> 4.57 us  [the longest x2 2.63 us: paired(): lasts = [x[cuts[2]:] for x in pairs]]
    pallas_call x2 -> x1, Pallas kernels: 18.8 us -> 14.4 us  [local_sums(): pl.pallas_call(functools.partial(local_kernel, start, acc is not None), g...]
    pallas_call x2, Pallas kernels: 9.04 us -> 12.9 us  [arrived_sums(): pl.pallas_call(functools.partial(sum_kernel, start), grid=(count,), in_sp...]
    pallas_call x3, Pallas kernels: 6.92 us -> 3.78 us  [the longest x2 2.9 us: added_sums(): pl.pallas_call(functools.partial(add_kernel, sub, slice(first, first + he...]
    ppermute x7, waiting for transfers between devices: 5.91 us -> 2.77 us  [swap(): return lax.ppermute(x, 'narrow', [(0, 1), (1, 0)])]
    ppermute x7 -> x8, waiting for transfers between devices: 14.3 us -> 12.6 us  [over_wide(): return lax.ppermute(x, 'wide', [(i, i ^ mask) for i in range(n_wide)])]
    unnamed x14 -> x12, local copies, waits for them, and re-layouts: 2.39 us -> 3.52 us
    slice x3 -> x2, local copies, waits for them, and re-layouts: 3.45 us -> 2.39 us  [paired(): flat[a * rows:b * rows]]
  transfers between devices with their start and end apart: 14 -> 15, of which waited for: 10 -> 8; matrix products, arithmetic and copies ran while one was open for 3% -> 10% of each run, Pallas kernels for 39% -> 38%
where the time goes in v4:
time: 80.6 us; the launch traced here: 80 us
  Pallas kernels  32.7 us (41%)
  starting transfers between devices  19.9 us (25%)
  waiting for transfers between devices  15.4 us (19%)
  local copies, waits for them, and re-layouts  10.9 us (14%)
  between operations  0.81 us (1%)
    pallas_call x1, Pallas kernels, local_sums(): pl.pallas_call(functools.partial(local_kernel, start, acc is not None), g...  14.4 us
    pallas_call x2, Pallas kernels, arrived_sums(): pl.pallas_call(functools.partial(sum_kernel, start), grid=(count,), in_sp...  12.9 us
    ppermute x8, waiting for transfers between devices, over_wide(): return lax.ppermute(x, 'wide', [(i, i ^ mask) for i in range(n_wide)])  12.6 us
    ppermute x7, starting transfers between devices, swap(): return lax.ppermute(x, 'narrow', [(0, 1), (1, 0)])  10.3 us
    ppermute x8, starting transfers between devices, over_wide(): return lax.ppermute(x, 'wide', [(i, i ^ mask) for i in range(n_wide)])  9.57 us
    unnamed x12, local copies, waits for them, and re-layouts  3.52 us
    pallas_call x2, Pallas kernels, added_sums(): pl.pallas_call(functools.partial(add_kernel, sub, slice(first, first + he...  2.9 us
    ppermute x7, waiting for transfers between devices, swap(): return lax.ppermute(x, 'narrow', [(0, 1), (1, 0)])  2.77 us
  transfers between devices with their start and end apart: 15, of which 8 were waited for; matrix products, arithmetic and copies ran while one was open for 10% of the time, Pallas kernels for 38%

profile of v4, /device:TPU:0, one launch (start us, length us, event | category | flops | bytes accessed | tf_op | source)
XLA Modules:
  0.0 80.0 jit_solution(14017677632726830996)
XLA Ops:
  0.6 1.3 %slice.77 = f32[4,256,256]{2,1,0:T(8,128)S(1)} slice(f32[8,256,256]{2,1,0:T(8,128)} %param.8), slice={[0:4], [0:256], [0:256]} | slice | bytes 2097152 | tf_op jit(solution)/shard_map/slice | solution.py:325
  1.9 3.0 %collective-permute-start = (f32[1024,256]{1,0:T(8,128)S(1)}, f32[1024,256]{1,0:T(8,128)S(1)}, u32[]{:S(2)}, u32[]{:S(2)}) collective-permute-start(f32[1024,256]{1,0:T(8,128)S(1)} %bitcast.43), channel_id=1, source_target_pairs={{0,1},{1,0},{2,3},{3,2},{4,5},{5,4},{6,7},{7,6},{8,9},{9,8},{10,11... | collective-permute-start | bytes 3145736 | tf_op jit(solution)/shard_map/ppermute | solution.py:315
  4.9 0.8 copy.13.adjacency
  5.7 0.8 copy.11.blocks
  6.5 0.1 pad_add_fusion.1.info
  6.5 14.4 %shard_map.95 = (bf16[8,2,2,256,256]{4,3,2,1,0:T(8,128)(2,1)}, bf16[8,2,2,256,256]{4,3,2,1,0:T(8,128)(2,1)}, f32[8,256,512]{2,1,0:T(8,128)}) custom-call(s32[3]{0:T(128)S(1)} %pad_add_fusion.1.info, s32[8,2,2]{2,1,0:T(2,128)S(1)} %copy.11.blocks, s32[8,4]{1,0:T(8,128)S(1)} %copy.13.adjacency, f32[2048,256]{1,0:T(8,128)} %bitcast.42, f32[8,256]{1,0:T(8,128)} %eig_ref, ...), custom_call_target="tpu_custom_call" | custom-call | flops 1000 | bytes 1000 | tf_op jit(solution)/shard_map/pallas_call | solution.py:116
  20.9 1.1 %slice.82 = f32[2,256,256]{2,1,0:T(8,128)S(1)} slice(f32[8,256,256]{2,1,0:T(8,128)} %param.8), slice={[4:6], [0:256], [0:256]} | slice | bytes 1048576 | tf_op jit(solution)/shard_map/slice | solution.py:325
  22.0 0.1 collective-permute-start.1
  22.1 2.0 %collective-permute-start.4 = (f32[512,256]{1,0:T(8,128)S(1)}, f32[512,256]{1,0:T(8,128)S(1)}, u32[]{:S(2)}, u32[]{:S(2)}) collective-permute-start(f32[512,256]{1,0:T(8,128)S(1)} %bitcast.44), channel_id=1, source_target_pairs={{0,1},{1,0},{2,3},{3,2},{4,5},{5,4},{6,7},{7,6},{8,9},{9,8},{10,11... | collective-permute-start | bytes 1572872 | tf_op jit(solution)/shard_map/ppermute | solution.py:315
  24.1 0.1 slice.79
  24.2 0.1 copy.10
  24.3 0.1 eq.26
  24.4 0.1 eq.27
  24.5 0.1 pad_add_fusion
  24.5 0.1 eq.29
  24.6 1.8 %slice_bitcast_fusion = (f32[256,256]{1,0:T(8,128)S(1)}, f32[256,256]{1,0:T(8,128)}) fusion(f32[8,256,256]{2,1,0:T(8,128)} %param.8), kind=kLoop, calls=%fused_computation.3 | loop fusion | bytes 1048576 | tf_op jit(solution)/shard_map/slice | solution.py:327
  26.4 1.3 %slice.85.m_ref = bf16[2,2,2,256,256]{4,3,2,1,0:T(8,128)(2,1)S(1)} slice(bf16[8,2,2,256,256]{4,3,2,1,0:T(8,128)(2,1)} %get-tuple-element.44.m_ref), slice={[6:8], [0:2], [0:2], [0:256], [0:256]} | slice | bytes 2097152 | tf_op jit(solution)/shard_map/slice | solution.py:348
  27.8 1.3 %slice.84.s_ref = bf16[2,2,2,256,256]{4,3,2,1,0:T(8,128)(2,1)S(1)} slice(bf16[8,2,2,256,256]{4,3,2,1,0:T(8,128)(2,1)} %get-tuple-element.43.s_ref), slice={[6:8], [0:2], [0:2], [0:256], [0:256]} | slice | bytes 2097152 | tf_op jit(solution)/shard_map/slice | solution.py:348
  29.1 0.0 collective-permute-done.modes_ref
  29.1 0.1 broadcast_in_dim.4
  29.2 1.9 %collective-permute-start.3 = (f32[256,256]{1,0:T(8,128)S(1)}, f32[256,256]{1,0:T(8,128)S(1)}, u32[]{:S(2)}, u32[]{:S(2)}) collective-permute-start(f32[256,256]{1,0:T(8,128)S(1)} %copy-done.3), channel_id=1, source_target_pairs={{0,1},{1,0},{2,3},{3,2},{4,5},{5,4},{6,7},{7,6},{8,9},{9,8},{10,11... | collective-permute-start | bytes 786440 | tf_op jit(solution)/shard_map/ppermute | solution.py:315
  31.1 7.7 %shard_map.96.acc_in = f32[8,256,512]{2,1,0:T(8,128)S(1)} custom-call(s32[3]{0:T(128)S(1)} %pad_add_fusion.1.info, s32[8,4]{1,0:T(8,128)S(1)} %copy.13.adjacency, f32[1024,256]{1,0:T(8,128)S(1)} %collective-permute-done.modes_ref, f32[8,256]{1,0:T(8,128)S(1)} %collective-permute-done.1.eig_ref, bf16[8,2,2,256,256]{4,3,2,1,0:T(8,128)(2,1)} %get-tuple-element.43.s_ref, ...), custom_call_target="tpu_custom_call" | custom-call | flops 3221225472 | bytes 12582912 | tf_op jit(solution)/shard_map/pallas_call | solution.py:155
  38.8 2.0 %copy-done = f32[8,256,512]{2,1,0:T(8,128)} copy-done((f32[8,256,512]{2,1,0:T(8,128)}, f32[8,256,512]{2,1,0:T(8,128)S(1)}, u32[]{:S(2)}) %copy-start) | copy-done | bytes 4194328
  40.8 0.1 collective-permute-start.2
  40.9 0.0 collective-permute-done.4.modes_ref
  40.9 5.2 %shard_map.97.acc_ref = f32[8,256,512]{2,1,0:T(8,128)S(1)} custom-call(s32[3]{0:T(128)S(1)} %pad_add_fusion.1.info, s32[8,4]{1,0:T(8,128)S(1)} %copy.13.adjacency, f32[512,256]{1,0:T(8,128)S(1)} %collective-permute-done.4.modes_ref, f32[8,256]{1,0:T(8,128)S(1)} %collective-permute-done.1.eig_ref, bf16[8,2,2,256,256]{4,3,2,1,0:T(8,128)(2,1)} %get-tuple-element.43.s_ref, ...), custom_call_target="tpu_custom_call" | custom-call | flops 1610612736 | bytes 6291456 | tf_op jit(solution)/shard_map/pallas_call | solution.py:155
  46.1 1.6 %shard_map.98 = (f32[4,128,256]{2,1,0:T(8,128)S(1)}, f32[4,144,256]{2,1,0:T(8,128)S(1)}, f32[4,128,256]{2,1,0:T(8,128)S(1)}, f32[4,144,256]{2,1,0:T(8,128)S(1)}) custom-call(s32[3]{0:T(128)S(1)} %pad_add_fusion.1.info, f32[8,256,512]{2,1,0:T(8,128)S(1)} %shard_map.97.acc_ref), custom_call_target="tpu_custom_call" | custom-call | flops 8000000 | bytes 1048576 | tf_op jit(solution)/shard_map/pallas_call | solution.py:236
  47.8 1.5 %shard_map.99 = (f32[4,128,256]{2,1,0:T(8,128)S(1)}, f32[4,144,256]{2,1,0:T(8,128)S(1)}, f32[4,128,256]{2,1,0:T(8,128)S(1)}, f32[4,144,256]{2,1,0:T(8,128)S(1)}) custom-call(f32[256,256]{1,0:T(8,128)S(1)} %collective-permute-done.3.modes_ref, f32[8,256]{1,0:T(8,128)S(1)} %collective-permute-done.1.eig_ref, bf16[2,2,2,256,256]{4,3,2,1,0:T(8,128)(2,1)S(1)} %slice.84.s_ref, ...), custom_call_target="tpu_custom_call" | custom-call | flops 805306368 | bytes 3145728 | tf_op jit(solution)/shard_map/pallas_call | solution.py:271
  49.2 1.5 %collective-permute-done.2.modes_ref = f32[256,256]{1,0:T(8,128)S(1)} collective-permute-done((f32[256,256]{1,0:T(8,128)S(1)}, f32[256,256]{1,0:T(8,128)S(1)}, u32[]{:S(2)}, u32[]{:S(2)}) %collective-permute-start.2) | collective-permute-done | bytes 262176 | tf_op jit(solution)/shard_map/ppermute | solution.py:315
  50.8 1.4 %shard_map.100 = (f32[4,128,256]{2,1,0:T(8,128)S(1)}, f32[4,144,256]{2,1,0:T(8,128)S(1)}, f32[4,128,256]{2,1,0:T(8,128)S(1)}, f32[4,144,256]{2,1,0:T(8,128)S(1)}) custom-call(f32[256,256]{1,0:T(8,128)S(1)} %collective-permute-done.2.modes_ref, f32[8,256]{1,0:T(8,128)S(1)} %collective-permute-done.1.eig_ref, bf16[2,2,2,256,256]{4,3,2,1,0:T(8,128)(2,1)S(1)} %slice.84.s_ref, ...), custom_call_target="tpu_custom_call" | custom-call | flops 805306368 | bytes 3145728 | tf_op jit(solution)/shard_map/pallas_call | solution.py:271
  52.2 0.1 collective-permute-start.6
  52.3 0.5 collective-permute-start.5
  52.8 1.4 %collective-permute-done.6 = f32[4,128,256]{2,1,0:T(8,128)S(1)} collective-permute-done((f32[4,128,256]{2,1,0:T(8,128)S(1)}, f32[4,128,256]{2,1,0:T(8,128)S(1)}, u32[]{:S(2)}, u32[]{:S(2)}) %collective-permute-start.6) | collective-permute-done | bytes 524320 | tf_op jit(solution)/shard_map/ppermute | solution.py:318
  54.2 0.1 add.51
  54.3 3.9 %collective-permute-start.8 = (f32[128,256]{1,0:T(8,128)S(1)}, f32[128,256]{1,0:T(8,128)S(1)}, u32[]{:S(2)}, u32[]{:S(2)}) collective-permute-start(f32[128,256]{1,0:T(8,128)S(1)} %get-tuple-element.68), channel_id=1, source_target_pairs={{0,12},{2,14},{4,8},{6,10},{8,4},{10,6},{12,0},{14,2},{1,13},{3,15... | collective-permute-start | bytes 393224 | tf_op jit(solution)/shard_map/ppermute | solution.py:318
  58.2 0.6 collective-permute-start.9
  58.9 1.7 %collective-permute-start.7 = (f32[4,72,256]{2,1,0:T(8,128)S(1)}, f32[4,72,256]{2,1,0:T(8,128)S(1)}, u32[]{:S(2)}, u32[]{:S(2)}) collective-permute-start(f32[4,72,256]{2,1,0:T(8,128)S(1)} %slice_add_fusion.1), channel_id=1, source_target_pairs={{0,1},{1,0},{2,3},{3,2},{4,5},{5,4},{6,7},{7,6},{8,9},{9,8},{10,11... | collective-permute-start | bytes 884744 | tf_op jit(solution)/shard_map/ppermute | solution.py:315
  60.6 1.9 %collective-permute-done.8 = f32[128,256]{1,0:T(8,128)S(1)} collective-permute-done((f32[128,256]{1,0:T(8,128)S(1)}, f32[128,256]{1,0:T(8,128)S(1)}, u32[]{:S(2)}, u32[]{:S(2)}) %collective-permute-start.8) | collective-permute-done | bytes 131104 | tf_op jit(solution)/shard_map/ppermute | solution.py:318
  62.5 3.4 %collective-permute-done.10 = f32[128,256]{1,0:T(8,128)S(1)} collective-permute-done((f32[128,256]{1,0:T(8,128)S(1)}, f32[128,256]{1,0:T(8,128)S(1)}, u32[]{:S(2)}, u32[]{:S(2)}) %collective-permute-start.10) | collective-permute-done | bytes 131104 | tf_op jit(solution)/shard_map/ppermute | solution.py:318
  65.9 3.7 %collective-permute-done.9 = f32[128,256]{1,0:T(8,128)S(1)} collective-permute-done((f32[128,256]{1,0:T(8,128)S(1)}, f32[128,256]{1,0:T(8,128)S(1)}, u32[]{:S(2)}, u32[]{:S(2)}) %collective-permute-start.9) | collective-permute-done | bytes 131104 | tf_op jit(solution)/shard_map/ppermute | solution.py:318
  69.6 0.1 fusion
  69.7 2.5 %collective-permute-start.12 = (f32[72,256]{1,0:T(8,128)S(1)}, f32[72,256]{1,0:T(8,128)S(1)}, u32[]{:S(2)}, u32[]{:S(2)}) collective-permute-start(f32[72,256]{1,0:T(8,128)S(1)} %get-tuple-element.71), channel_id=1, source_target_pairs={{0,12},{2,14},{4,8},{6,10},{8,4},{10,6},{12,0},{14,2},{1,13},{3,15... | collective-permute-start | bytes 221192 | tf_op jit(solution)/shard_map/ppermute | solution.py:318
  72.3 1.9 %collective-permute-start.13 = (f32[72,256]{1,0:T(8,128)S(1)}, f32[72,256]{1,0:T(8,128)S(1)}, u32[]{:S(2)}, u32[]{:S(2)}) collective-permute-start(f32[72,256]{1,0:T(8,128)S(1)} %get-tuple-element.73), channel_id=1, source_target_pairs={{0,8},{2,10},{4,12},{6,14},{8,0},{10,2},{12,4},{14,6},{1,9},{3,11}... | collective-permute-start | bytes 221192 | tf_op jit(solution)/shard_map/ppermute | solution.py:318
  74.2 1.5 %collective-permute-start.11 = (f32[128,256]{1,0:T(8,128)S(1)}, f32[128,256]{1,0:T(8,128)S(1)}, u32[]{:S(2)}, u32[]{:S(2)}) collective-permute-start(f32[128,256]{1,0:T(8,128)S(1)} %fusion.3.mine), channel_id=1, source_target_pairs={{0,1},{1,0},{2,3},{3,2},{4,5},{5,4},{6,7},{7,6},{8,9},{9,8},{10,11... | collective-permute-start | bytes 393224 | tf_op jit(solution)/shard_map/ppermute | solution.py:315
  75.7 1.1 %collective-permute-done.12 = f32[72,256]{1,0:T(8,128)S(1)} collective-permute-done((f32[72,256]{1,0:T(8,128)S(1)}, f32[72,256]{1,0:T(8,128)S(1)}, u32[]{:S(2)}, u32[]{:S(2)}) %collective-permute-start.12) | collective-permute-done | bytes 73760 | tf_op jit(solution)/shard_map/ppermute | solution.py:318
  76.8 1.1 %collective-permute-done.14 = f32[72,256]{1,0:T(8,128)S(1)} collective-permute-done((f32[72,256]{1,0:T(8,128)S(1)}, f32[72,256]{1,0:T(8,128)S(1)}, u32[]{:S(2)}, u32[]{:S(2)}) %collective-permute-start.14) | collective-permute-done | bytes 73760 | tf_op jit(solution)/shard_map/ppermute | solution.py:318
  77.9 1.2 %collective-permute-done.11.theirs = f32[128,256]{1,0:T(8,128)S(1)} collective-permute-done((f32[128,256]{1,0:T(8,128)S(1)}, f32[128,256]{1,0:T(8,128)S(1)}, u32[]{:S(2)}, u32[]{:S(2)}) %collective-permute-start.11) | collective-permute-done | bytes 131104 | tf_op jit(solution)/shard_map/ppermute | solution.py:315
  79.1 0.9 %shard_map.101 = (f32[1,128,256]{2,1,0:T(8,128)}, f32[1,128,256]{2,1,0:T(8,128)}) custom-call(f32[8,256]{1,0:T(8,128)S(1)} %broadcast_in_dim.5.side_ref, f32[128,256]{1,0:T(8,128)S(1)} %fusion.3.mine, f32[128,256]{1,0:T(8,128)S(1)} %collective-permute-done.11.theirs, f32[72,256]{1,0:T(8,128)S(1)} %fusion.6.triangle_ref, f32[1,128,256]{2,1,0:T(8,128)S(1)} %copy-done.1, ...), custom_call_target="tpu_custom_call" | custom-call | tf_op jit(solution)/shard_map/pallas_call | solution.py:297
  (27 shorter events, 0.2 us)
Async XLA Ops:
  1.9 27.1 %collective-permute-start = (f32[1024,256]{1,0:T(8,128)S(1)}, f32[1024,256]{1,0:T(8,128)S(1)}, u32[]{:S(2)}, u32[]{:S(2)}) collective-permute-start(f32[1024,256]{1,0:T(8,128)S(1)} %bitcast.43), channel_id=1, source_target_pairs={{0,1},{1,0},{2,3},{3,2},{4,5},{5,4},{6,7},{7,6},{8,9},{9,8},{10,11... | collective-permute-start | bytes 3145736 | tf_op jit(solution)/shard_map/ppermute | solution.py:315
  6.5 17.6 %copy-start.4 = (s32[8,4]{0,1:T(4,128)S(1)}, s32[8,4]{0,1:T(4,128)}, u32[]{:S(2)}) copy-start(s32[8,4]{0,1:T(4,128)} %param.13) | copy-start | bytes 388
  22.0 9.1 %collective-permute-start.1 = (f32[8,256]{1,0:T(8,128)}, f32[8,256]{1,0:T(8,128)S(1)}, u32[]{:S(2)}, u32[]{:S(2)}) collective-permute-start(f32[8,256]{1,0:T(8,128)} %eig_ref), channel_id=1, source_target_pairs={{0,1},{1,0},{2,3},{3,2},{4,5},{5,4},{6,7},{7,6},{8,9},{9,8},{10,11... | collective-permute-start | bytes 24584 | tf_op jit(solution)/shard_map/ppermute | solution.py:315
  22.1 18.8 %collective-permute-start.4 = (f32[512,256]{1,0:T(8,128)S(1)}, f32[512,256]{1,0:T(8,128)S(1)}, u32[]{:S(2)}, u32[]{:S(2)}) collective-permute-start(f32[512,256]{1,0:T(8,128)S(1)} %bitcast.44), channel_id=1, source_target_pairs={{0,1},{1,0},{2,3},{3,2},{4,5},{5,4},{6,7},{7,6},{8,9},{9,8},{10,11... | collective-permute-start | bytes 1572872 | tf_op jit(solution)/shard_map/ppermute | solution.py:315
  26.4 2.7 %copy-start.3 = (f32[256,256]{1,0:T(8,128)S(1)}, f32[256,256]{1,0:T(8,128)}, u32[]{:S(2)}) copy-start(f32[256,256]{1,0:T(8,128)} %get-tuple-element.48) | copy-start | bytes 786436
  29.2 18.6 %collective-permute-start.3 = (f32[256,256]{1,0:T(8,128)S(1)}, f32[256,256]{1,0:T(8,128)S(1)}, u32[]{:S(2)}, u32[]{:S(2)}) collective-permute-start(f32[256,256]{1,0:T(8,128)S(1)} %copy-done.3), channel_id=1, source_target_pairs={{0,1},{1,0},{2,3},{3,2},{4,5},{5,4},{6,7},{7,6},{8,9},{9,8},{10,11... | collective-permute-start | bytes 786440 | tf_op jit(solution)/shard_map/ppermute | solution.py:315
  38.8 2.0 %copy-start = (f32[8,256,512]{2,1,0:T(8,128)}, f32[8,256,512]{2,1,0:T(8,128)S(1)}, u32[]{:S(2)}) copy-start(f32[8,256,512]{2,1,0:T(8,128)S(1)} %shard_map.96.acc_in) | copy-start | bytes 12582916
  40.8 10.0 %collective-permute-start.2 = (f32[256,256]{1,0:T(8,128)S(1)}, f32[256,256]{1,0:T(8,128)S(1)}, u32[]{:S(2)}, u32[]{:S(2)}) collective-permute-start(f32[256,256]{1,0:T(8,128)S(1)} %get-tuple-element.46), channel_id=1, source_target_pairs={{0,1},{1,0},{2,3},{3,2},{4,5},{5,4},{6,7},{7,6},{8,9},{9,8},{10,11... | collective-permute-start | bytes 786440 | tf_op jit(solution)/shard_map/ppermute | solution.py:315
  50.8 28.4 %copy-start.1 = (f32[1,128,256]{2,1,0:T(8,128)S(1)}, f32[1,128,256]{2,1,0:T(8,128)}, u32[]{:S(2)}) copy-start(f32[1,128,256]{2,1,0:T(8,128)} %stiff_ref.2) | copy-start | bytes 393220
  50.8 28.4 %copy-start.2 = (f32[1,128,256]{2,1,0:T(8,128)S(1)}, f32[1,128,256]{2,1,0:T(8,128)}, u32[]{:S(2)}) copy-start(f32[1,128,256]{2,1,0:T(8,128)} %mass_ref.2) | copy-start | bytes 393220
  52.2 2.0 %collective-permute-start.6 = (f32[4,128,256]{2,1,0:T(8,128)S(1)}, f32[4,128,256]{2,1,0:T(8,128)S(1)}, u32[]{:S(2)}, u32[]{:S(2)}) collective-permute-start(f32[4,128,256]{2,1,0:T(8,128)S(1)} %get-tuple-element.62), channel_id=1, source_target_pairs={{0,2},{2,0},{4,6},{6,4},{8,10},{10,8},{12,14},{14,12},{1,3},{3,1},... | collective-permute-start | bytes 1572872 | tf_op jit(solution)/shard_map/ppermute | solution.py:318
  52.3 6.6 %collective-permute-start.5 = (f32[4,144,256]{2,1,0:T(8,128)S(1)}, f32[4,144,256]{2,1,0:T(8,128)S(1)}, u32[]{:S(2)}, u32[]{:S(2)}) collective-permute-start(f32[4,144,256]{2,1,0:T(8,128)S(1)} %get-tuple-element.60), channel_id=1, source_target_pairs={{0,2},{2,0},{4,6},{6,4},{8,10},{10,8},{12,14},{14,12},{1,3},{3,1},... | collective-permute-start | bytes 1769480 | tf_op jit(solution)/shard_map/ppermute | solution.py:318
  54.3 8.2 %collective-permute-start.8 = (f32[128,256]{1,0:T(8,128)S(1)}, f32[128,256]{1,0:T(8,128)S(1)}, u32[]{:S(2)}, u32[]{:S(2)}) collective-permute-start(f32[128,256]{1,0:T(8,128)S(1)} %get-tuple-element.68), channel_id=1, source_target_pairs={{0,12},{2,14},{4,8},{6,10},{8,4},{10,6},{12,0},{14,2},{1,13},{3,15... | collective-permute-start | bytes 393224 | tf_op jit(solution)/shard_map/ppermute | solution.py:318
  58.2 7.7 %collective-permute-start.10 = (f32[128,256]{1,0:T(8,128)S(1)}, f32[128,256]{1,0:T(8,128)S(1)}, u32[]{:S(2)}, u32[]{:S(2)}) collective-permute-start(f32[128,256]{1,0:T(8,128)S(1)} %get-tuple-element.69), channel_id=1, source_target_pairs={{0,4},{2,6},{4,0},{6,2},{8,12},{10,14},{12,8},{14,10},{1,5},{3,7},... | collective-permute-start | bytes 393224 | tf_op jit(solution)/shard_map/ppermute | solution.py:318
  58.2 11.4 %collective-permute-start.9 = (f32[128,256]{1,0:T(8,128)S(1)}, f32[128,256]{1,0:T(8,128)S(1)}, u32[]{:S(2)}, u32[]{:S(2)}) collective-permute-start(f32[128,256]{1,0:T(8,128)S(1)} %get-tuple-element.70), channel_id=1, source_target_pairs={{0,8},{2,10},{4,12},{6,14},{8,0},{10,2},{12,4},{14,6},{1,9},{3,11}... | collective-permute-start | bytes 393224 | tf_op jit(solution)/shard_map/ppermute | solution.py:318
  58.9 10.7 %collective-permute-start.7 = (f32[4,72,256]{2,1,0:T(8,128)S(1)}, f32[4,72,256]{2,1,0:T(8,128)S(1)}, u32[]{:S(2)}, u32[]{:S(2)}) collective-permute-start(f32[4,72,256]{2,1,0:T(8,128)S(1)} %slice_add_fusion.1), channel_id=1, source_target_pairs={{0,1},{1,0},{2,3},{3,2},{4,5},{5,4},{6,7},{7,6},{8,9},{9,8},{10,11... | collective-permute-start | bytes 884744 | tf_op jit(solution)/shard_map/ppermute | solution.py:315
  69.7 7.0 %collective-permute-start.12 = (f32[72,256]{1,0:T(8,128)S(1)}, f32[72,256]{1,0:T(8,128)S(1)}, u32[]{:S(2)}, u32[]{:S(2)}) collective-permute-start(f32[72,256]{1,0:T(8,128)S(1)} %get-tuple-element.71), channel_id=1, source_target_pairs={{0,12},{2,14},{4,8},{6,10},{8,4},{10,6},{12,0},{14,2},{1,13},{3,15... | collective-permute-start | bytes 221192 | tf_op jit(solution)/shard_map/ppermute | solution.py:318
  72.3 5.6 %collective-permute-start.14 = (f32[72,256]{1,0:T(8,128)S(1)}, f32[72,256]{1,0:T(8,128)S(1)}, u32[]{:S(2)}, u32[]{:S(2)}) collective-permute-start(f32[72,256]{1,0:T(8,128)S(1)} %get-tuple-element.72), channel_id=1, source_target_pairs={{0,4},{2,6},{4,0},{6,2},{8,12},{10,14},{12,8},{14,10},{1,5},{3,7},... | collective-permute-start | bytes 221192 | tf_op jit(solution)/shard_map/ppermute | solution.py:318
  72.3 5.6 %collective-permute-start.13 = (f32[72,256]{1,0:T(8,128)S(1)}, f32[72,256]{1,0:T(8,128)S(1)}, u32[]{:S(2)}, u32[]{:S(2)}) collective-permute-start(f32[72,256]{1,0:T(8,128)S(1)} %get-tuple-element.73), channel_id=1, source_target_pairs={{0,8},{2,10},{4,12},{6,14},{8,0},{10,2},{12,4},{14,6},{1,9},{3,11}... | collective-permute-start | bytes 221192 | tf_op jit(solution)/shard_map/ppermute | solution.py:318
  74.2 5.0 %collective-permute-start.11 = (f32[128,256]{1,0:T(8,128)S(1)}, f32[128,256]{1,0:T(8,128)S(1)}, u32[]{:S(2)}, u32[]{:S(2)}) collective-permute-start(f32[128,256]{1,0:T(8,128)S(1)} %fusion.3.mine), channel_id=1, source_target_pairs={{0,1},{1,0},{2,3},{3,2},{4,5},{5,4},{6,7},{7,6},{8,9},{9,8},{10,11... | collective-permute-start | bytes 393224 | tf_op jit(solution)/shard_map/ppermute | solution.py:315

commit v5 on v4

--- a/solution.py
+++ b/solution.py
@@ -361,19 +361,19 @@
         )
     send_corner, send_triangle, keep_corner, keep_triangle = sums
 
-    def over_chips(x):
-        parts = [over_wide(x[shift], 2 * shift) for shift in range(chips - 1, 0, -1)]
+    def over_chips(x, order):
+        parts = [over_wide(x[shift], 2 * shift) for shift in order]
         return sum(parts, x[0])
 
     away, home = slice(0, TRIANGLE), slice(TRIANGLE, 2 * TRIANGLE)
     corners = keep_corner + over_wide(send_corner, 1)
     got = over_wide(send_triangle, 1)
-    corner = over_chips(corners)
+    corner = over_chips(corners, (2, 3, 1))
     sent, corners = after(keep_triangle[:, away] + got[:, away], corners)
     came_away = swap(sent)
     corner_theirs = swap(corner)
     came_away, corner = after(came_away, corner)
-    triangle = over_chips(keep_triangle[:, home] + got[:, home] + came_away)
+    triangle = over_chips(keep_triangle[:, home] + got[:, home] + came_away, (3, 2, 1))
     return unpack(side_rows, (corner, corner_theirs, triangle), iface_stiff, iface_mass)
 
 

time: 80.6 us -> 80.3 us (level)
    ppermute x7, waiting for transfers between devices: 2.77 us -> 1.55 us  [swap(): return lax.ppermute(x, 'narrow', [(0, 1), (1, 0)])]
  transfers between devices with their start and end apart: 15 -> 15, of which waited for: 8 -> 7; matrix products, arithmetic and copies ran while one was open for 10% -> 10% of each run, Pallas kernels for 38% -> 38%
where the time goes in v5:
time: 80.3 us; the launch traced here: 79.7 us
  Pallas kernels  32.7 us (41%)
  starting transfers between devices  20.3 us (25%)
  waiting for transfers between devices  14.7 us (18%)
  local copies, waits for them, and re-layouts  10.9 us (14%)
  between operations  0.83 us (1%)
    pallas_call x1, Pallas kernels, local_sums(): pl.pallas_call(functools.partial(local_kernel, start, acc is not None), g...  14.4 us
    ppermute x8, waiting for transfers between devices, over_wide(): return lax.ppermute(x, 'wide', [(i, i ^ mask) for i in range(n_wide)])  13.1 us
    pallas_call x2, Pallas kernels, arrived_sums(): pl.pallas_call(functools.partial(sum_kernel, start), grid=(count,), in_sp...  12.9 us
    ppermute x7, starting transfers between devices, swap(): return lax.ppermute(x, 'narrow', [(0, 1), (1, 0)])  10.4 us
    ppermute x8, starting transfers between devices, over_wide(): return lax.ppermute(x, 'wide', [(i, i ^ mask) for i in range(n_wide)])  9.91 us
    unnamed x12, local copies, waits for them, and re-layouts  3.52 us
    pallas_call x2, Pallas kernels, added_sums(): pl.pallas_call(functools.partial(add_kernel, sub, slice(first, first + he...  2.9 us
    slice x2, local copies, waits for them, and re-layouts, paired(): lasts = [x[cuts[2]:] for x in pairs]  2.63 us
  transfers between devices with their start and end apart: 15, of which 7 were waited for; matrix products, arithmetic and copies ran while one was open for 10% of the time, Pallas kernels for 38%

profile of v5, /device:TPU:0, one launch (start us, length us, event | category | flops | bytes accessed | tf_op | source)
XLA Modules:
  0.0 79.7 jit_solution(6876489611537498271)
XLA Ops:
  0.6 1.3 %slice.77 = f32[4,256,256]{2,1,0:T(8,128)S(1)} slice(f32[8,256,256]{2,1,0:T(8,128)} %param.8), slice={[0:4], [0:256], [0:256]} | slice | bytes 2097152 | tf_op jit(solution)/shard_map/slice | solution.py:325
  1.9 3.0 %collective-permute-start = (f32[1024,256]{1,0:T(8,128)S(1)}, f32[1024,256]{1,0:T(8,128)S(1)}, u32[]{:S(2)}, u32[]{:S(2)}) collective-permute-start(f32[1024,256]{1,0:T(8,128)S(1)} %bitcast.43), channel_id=1, source_target_pairs={{0,1},{1,0},{2,3},{3,2},{4,5},{5,4},{6,7},{7,6},{8,9},{9,8},{10,11... | collective-permute-start | bytes 3145736 | tf_op jit(solution)/shard_map/ppermute | solution.py:315
  4.9 0.8 copy.13.adjacency
  5.7 0.8 copy.11.blocks
  6.5 0.1 pad_add_fusion.1.info
  6.5 14.4 %shard_map.95 = (bf16[8,2,2,256,256]{4,3,2,1,0:T(8,128)(2,1)}, bf16[8,2,2,256,256]{4,3,2,1,0:T(8,128)(2,1)}, f32[8,256,512]{2,1,0:T(8,128)}) custom-call(s32[3]{0:T(128)S(1)} %pad_add_fusion.1.info, s32[8,2,2]{2,1,0:T(2,128)S(1)} %copy.11.blocks, s32[8,4]{1,0:T(8,128)S(1)} %copy.13.adjacency, f32[2048,256]{1,0:T(8,128)} %bitcast.42, f32[8,256]{1,0:T(8,128)} %eig_ref, ...), custom_call_target="tpu_custom_call" | custom-call | flops 1000 | bytes 1000 | tf_op jit(solution)/shard_map/pallas_call | solution.py:116
  20.9 1.1 %slice.82 = f32[2,256,256]{2,1,0:T(8,128)S(1)} slice(f32[8,256,256]{2,1,0:T(8,128)} %param.8), slice={[4:6], [0:256], [0:256]} | slice | bytes 1048576 | tf_op jit(solution)/shard_map/slice | solution.py:325
  22.0 0.1 collective-permute-start.1
  22.1 2.0 %collective-permute-start.4 = (f32[512,256]{1,0:T(8,128)S(1)}, f32[512,256]{1,0:T(8,128)S(1)}, u32[]{:S(2)}, u32[]{:S(2)}) collective-permute-start(f32[512,256]{1,0:T(8,128)S(1)} %bitcast.44), channel_id=1, source_target_pairs={{0,1},{1,0},{2,3},{3,2},{4,5},{5,4},{6,7},{7,6},{8,9},{9,8},{10,11... | collective-permute-start | bytes 1572872 | tf_op jit(solution)/shard_map/ppermute | solution.py:315
  24.1 0.1 slice.79
  24.2 0.1 copy.10
  24.3 0.1 eq.26
  24.4 0.1 eq.27
  24.5 0.1 pad_add_fusion
  24.5 0.1 eq.29
  24.6 1.8 %slice_bitcast_fusion = (f32[256,256]{1,0:T(8,128)S(1)}, f32[256,256]{1,0:T(8,128)}) fusion(f32[8,256,256]{2,1,0:T(8,128)} %param.8), kind=kLoop, calls=%fused_computation.3 | loop fusion | bytes 1048576 | tf_op jit(solution)/shard_map/slice | solution.py:327
  26.4 1.3 %slice.85.m_ref = bf16[2,2,2,256,256]{4,3,2,1,0:T(8,128)(2,1)S(1)} slice(bf16[8,2,2,256,256]{4,3,2,1,0:T(8,128)(2,1)} %get-tuple-element.44.m_ref), slice={[6:8], [0:2], [0:2], [0:256], [0:256]} | slice | bytes 2097152 | tf_op jit(solution)/shard_map/slice | solution.py:348
  27.8 1.3 %slice.84.s_ref = bf16[2,2,2,256,256]{4,3,2,1,0:T(8,128)(2,1)S(1)} slice(bf16[8,2,2,256,256]{4,3,2,1,0:T(8,128)(2,1)} %get-tuple-element.43.s_ref), slice={[6:8], [0:2], [0:2], [0:256], [0:256]} | slice | bytes 2097152 | tf_op jit(solution)/shard_map/slice | solution.py:348
  29.1 0.1 broadcast_in_dim.4
  29.2 1.9 %collective-permute-start.3 = (f32[256,256]{1,0:T(8,128)S(1)}, f32[256,256]{1,0:T(8,128)S(1)}, u32[]{:S(2)}, u32[]{:S(2)}) collective-permute-start(f32[256,256]{1,0:T(8,128)S(1)} %copy-done.3), channel_id=1, source_target_pairs={{0,1},{1,0},{2,3},{3,2},{4,5},{5,4},{6,7},{7,6},{8,9},{9,8},{10,11... | collective-permute-start | bytes 786440 | tf_op jit(solution)/shard_map/ppermute | solution.py:315
  31.1 0.0 collective-permute-done.1.eig_ref
  31.1 7.7 %shard_map.96.acc_in = f32[8,256,512]{2,1,0:T(8,128)S(1)} custom-call(s32[3]{0:T(128)S(1)} %pad_add_fusion.1.info, s32[8,4]{1,0:T(8,128)S(1)} %copy.13.adjacency, f32[1024,256]{1,0:T(8,128)S(1)} %collective-permute-done.modes_ref, f32[8,256]{1,0:T(8,128)S(1)} %collective-permute-done.1.eig_ref, bf16[8,2,2,256,256]{4,3,2,1,0:T(8,128)(2,1)} %get-tuple-element.43.s_ref, ...), custom_call_target="tpu_custom_call" | custom-call | flops 3221225472 | bytes 12582912 | tf_op jit(solution)/shard_map/pallas_call | solution.py:155
  38.8 2.0 %copy-done = f32[8,256,512]{2,1,0:T(8,128)} copy-done((f32[8,256,512]{2,1,0:T(8,128)}, f32[8,256,512]{2,1,0:T(8,128)S(1)}, u32[]{:S(2)}) %copy-start) | copy-done | bytes 4194328
  40.8 0.1 collective-permute-start.2
  40.9 5.2 %shard_map.97.acc_ref = f32[8,256,512]{2,1,0:T(8,128)S(1)} custom-call(s32[3]{0:T(128)S(1)} %pad_add_fusion.1.info, s32[8,4]{1,0:T(8,128)S(1)} %copy.13.adjacency, f32[512,256]{1,0:T(8,128)S(1)} %collective-permute-done.4.modes_ref, f32[8,256]{1,0:T(8,128)S(1)} %collective-permute-done.1.eig_ref, bf16[8,2,2,256,256]{4,3,2,1,0:T(8,128)(2,1)} %get-tuple-element.43.s_ref, ...), custom_call_target="tpu_custom_call" | custom-call | flops 1610612736 | bytes 6291456 | tf_op jit(solution)/shard_map/pallas_call | solution.py:155
  46.1 1.6 %shard_map.98 = (f32[4,128,256]{2,1,0:T(8,128)S(1)}, f32[4,144,256]{2,1,0:T(8,128)S(1)}, f32[4,128,256]{2,1,0:T(8,128)S(1)}, f32[4,144,256]{2,1,0:T(8,128)S(1)}) custom-call(s32[3]{0:T(128)S(1)} %pad_add_fusion.1.info, f32[8,256,512]{2,1,0:T(8,128)S(1)} %shard_map.97.acc_ref), custom_call_target="tpu_custom_call" | custom-call | flops 8000000 | bytes 1048576 | tf_op jit(solution)/shard_map/pallas_call | solution.py:236
  47.8 1.5 %shard_map.99 = (f32[4,128,256]{2,1,0:T(8,128)S(1)}, f32[4,144,256]{2,1,0:T(8,128)S(1)}, f32[4,128,256]{2,1,0:T(8,128)S(1)}, f32[4,144,256]{2,1,0:T(8,128)S(1)}) custom-call(f32[256,256]{1,0:T(8,128)S(1)} %collective-permute-done.3.modes_ref, f32[8,256]{1,0:T(8,128)S(1)} %collective-permute-done.1.eig_ref, bf16[2,2,2,256,256]{4,3,2,1,0:T(8,128)(2,1)S(1)} %slice.84.s_ref, ...), custom_call_target="tpu_custom_call" | custom-call | flops 805306368 | bytes 3145728 | tf_op jit(solution)/shard_map/pallas_call | solution.py:271
  49.2 1.5 %collective-permute-done.2.modes_ref = f32[256,256]{1,0:T(8,128)S(1)} collective-permute-done((f32[256,256]{1,0:T(8,128)S(1)}, f32[256,256]{1,0:T(8,128)S(1)}, u32[]{:S(2)}, u32[]{:S(2)}) %collective-permute-start.2) | collective-permute-done | bytes 262176 | tf_op jit(solution)/shard_map/ppermute | solution.py:315
  50.8 1.4 %shard_map.100 = (f32[4,128,256]{2,1,0:T(8,128)S(1)}, f32[4,144,256]{2,1,0:T(8,128)S(1)}, f32[4,128,256]{2,1,0:T(8,128)S(1)}, f32[4,144,256]{2,1,0:T(8,128)S(1)}) custom-call(f32[256,256]{1,0:T(8,128)S(1)} %collective-permute-done.2.modes_ref, f32[8,256]{1,0:T(8,128)S(1)} %collective-permute-done.1.eig_ref, bf16[2,2,2,256,256]{4,3,2,1,0:T(8,128)(2,1)S(1)} %slice.84.s_ref, ...), custom_call_target="tpu_custom_call" | custom-call | flops 805306368 | bytes 3145728 | tf_op jit(solution)/shard_map/pallas_call | solution.py:271
  52.2 0.1 collective-permute-start.6
  52.3 0.5 collective-permute-start.5
  52.8 1.4 %collective-permute-done.6 = f32[4,128,256]{2,1,0:T(8,128)S(1)} collective-permute-done((f32[4,128,256]{2,1,0:T(8,128)S(1)}, f32[4,128,256]{2,1,0:T(8,128)S(1)}, u32[]{:S(2)}, u32[]{:S(2)}) %collective-permute-start.6) | collective-permute-done | bytes 524320 | tf_op jit(solution)/shard_map/ppermute | solution.py:318
  54.2 0.1 add.51
  54.3 2.9 %collective-permute-start.8 = (f32[128,256]{1,0:T(8,128)S(1)}, f32[128,256]{1,0:T(8,128)S(1)}, u32[]{:S(2)}, u32[]{:S(2)}) collective-permute-start(f32[128,256]{1,0:T(8,128)S(1)} %get-tuple-element.68), channel_id=1, source_target_pairs={{0,8},{2,10},{4,12},{6,14},{8,0},{10,2},{12,4},{14,6},{1,9},{3,11}... | collective-permute-start | bytes 393224 | tf_op jit(solution)/shard_map/ppermute | solution.py:318
  57.2 1.6 %collective-permute-start.10 = (f32[128,256]{1,0:T(8,128)S(1)}, f32[128,256]{1,0:T(8,128)S(1)}, u32[]{:S(2)}, u32[]{:S(2)}) collective-permute-start(f32[128,256]{1,0:T(8,128)S(1)} %get-tuple-element.69), channel_id=1, source_target_pairs={{0,4},{2,6},{4,0},{6,2},{8,12},{10,14},{12,8},{14,10},{1,5},{3,7},... | collective-permute-start | bytes 393224 | tf_op jit(solution)/shard_map/ppermute | solution.py:318
  58.8 0.0 collective-permute-start.9
  58.8 1.8 %collective-permute-start.7 = (f32[4,72,256]{2,1,0:T(8,128)S(1)}, f32[4,72,256]{2,1,0:T(8,128)S(1)}, u32[]{:S(2)}, u32[]{:S(2)}) collective-permute-start(f32[4,72,256]{2,1,0:T(8,128)S(1)} %slice_add_fusion.1), channel_id=1, source_target_pairs={{0,1},{1,0},{2,3},{3,2},{4,5},{5,4},{6,7},{7,6},{8,9},{9,8},{10,11... | collective-permute-start | bytes 884744 | tf_op jit(solution)/shard_map/ppermute | solution.py:315
  60.6 4.1 %collective-permute-done.8 = f32[128,256]{1,0:T(8,128)S(1)} collective-permute-done((f32[128,256]{1,0:T(8,128)S(1)}, f32[128,256]{1,0:T(8,128)S(1)}, u32[]{:S(2)}, u32[]{:S(2)}) %collective-permute-start.8) | collective-permute-done | bytes 131104 | tf_op jit(solution)/shard_map/ppermute | solution.py:318
  64.7 0.0 collective-permute-done.10
  64.7 3.2 %collective-permute-done.9 = f32[128,256]{1,0:T(8,128)S(1)} collective-permute-done((f32[128,256]{1,0:T(8,128)S(1)}, f32[128,256]{1,0:T(8,128)S(1)}, u32[]{:S(2)}, u32[]{:S(2)}) %collective-permute-start.9) | collective-permute-done | bytes 131104 | tf_op jit(solution)/shard_map/ppermute | solution.py:318
  67.9 0.1 fusion
  68.0 3.1 %collective-permute-start.12 = (f32[72,256]{1,0:T(8,128)S(1)}, f32[72,256]{1,0:T(8,128)S(1)}, u32[]{:S(2)}, u32[]{:S(2)}) collective-permute-start(f32[72,256]{1,0:T(8,128)S(1)} %get-tuple-element.71), channel_id=1, source_target_pairs={{0,12},{2,14},{4,8},{6,10},{8,4},{10,6},{12,0},{14,2},{1,13},{3,15... | collective-permute-start | bytes 221192 | tf_op jit(solution)/shard_map/ppermute | solution.py:318
  71.1 1.8 %collective-permute-start.14 = (f32[72,256]{1,0:T(8,128)S(1)}, f32[72,256]{1,0:T(8,128)S(1)}, u32[]{:S(2)}, u32[]{:S(2)}) collective-permute-start(f32[72,256]{1,0:T(8,128)S(1)} %get-tuple-element.72), channel_id=1, source_target_pairs={{0,4},{2,6},{4,0},{6,2},{8,12},{10,14},{12,8},{14,10},{1,5},{3,7},... | collective-permute-start | bytes 221192 | tf_op jit(solution)/shard_map/ppermute | solution.py:318
  72.8 1.5 %collective-permute-start.11 = (f32[128,256]{1,0:T(8,128)S(1)}, f32[128,256]{1,0:T(8,128)S(1)}, u32[]{:S(2)}, u32[]{:S(2)}) collective-permute-start(f32[128,256]{1,0:T(8,128)S(1)} %fusion.3.mine), channel_id=1, source_target_pairs={{0,1},{1,0},{2,3},{3,2},{4,5},{5,4},{6,7},{7,6},{8,9},{9,8},{10,11... | collective-permute-start | bytes 393224 | tf_op jit(solution)/shard_map/ppermute | solution.py:315
  74.3 0.1 collective-permute-done.12
  74.4 1.4 %collective-permute-done.14 = f32[72,256]{1,0:T(8,128)S(1)} collective-permute-done((f32[72,256]{1,0:T(8,128)S(1)}, f32[72,256]{1,0:T(8,128)S(1)}, u32[]{:S(2)}, u32[]{:S(2)}) %collective-permute-start.14) | collective-permute-done | bytes 73760 | tf_op jit(solution)/shard_map/ppermute | solution.py:318
  75.8 3.0 %collective-permute-done.13 = f32[72,256]{1,0:T(8,128)S(1)} collective-permute-done((f32[72,256]{1,0:T(8,128)S(1)}, f32[72,256]{1,0:T(8,128)S(1)}, u32[]{:S(2)}, u32[]{:S(2)}) %collective-permute-start.13) | collective-permute-done | bytes 73760 | tf_op jit(solution)/shard_map/ppermute | solution.py:318
  78.9 0.9 %shard_map.101 = (f32[1,128,256]{2,1,0:T(8,128)}, f32[1,128,256]{2,1,0:T(8,128)}) custom-call(f32[8,256]{1,0:T(8,128)S(1)} %broadcast_in_dim.5.side_ref, f32[128,256]{1,0:T(8,128)S(1)} %fusion.3.mine, f32[128,256]{1,0:T(8,128)S(1)} %collective-permute-done.11.theirs, f32[72,256]{1,0:T(8,128)S(1)} %fusion.6.triangle_ref, f32[1,128,256]{2,1,0:T(8,128)S(1)} %copy-done.1, ...), custom_call_target="tpu_custom_call" | custom-call | tf_op jit(solution)/shard_map/pallas_call | solution.py:297
  (27 shorter events, 0.2 us)
Async XLA Ops:
  1.9 27.1 %collective-permute-start = (f32[1024,256]{1,0:T(8,128)S(1)}, f32[1024,256]{1,0:T(8,128)S(1)}, u32[]{:S(2)}, u32[]{:S(2)}) collective-permute-start(f32[1024,256]{1,0:T(8,128)S(1)} %bitcast.43), channel_id=1, source_target_pairs={{0,1},{1,0},{2,3},{3,2},{4,5},{5,4},{6,7},{7,6},{8,9},{9,8},{10,11... | collective-permute-start | bytes 3145736 | tf_op jit(solution)/shard_map/ppermute | solution.py:315
  6.5 17.6 %copy-start.4 = (s32[8,4]{0,1:T(4,128)S(1)}, s32[8,4]{0,1:T(4,128)}, u32[]{:S(2)}) copy-start(s32[8,4]{0,1:T(4,128)} %param.13) | copy-start | bytes 388
  22.0 9.1 %collective-permute-start.1 = (f32[8,256]{1,0:T(8,128)}, f32[8,256]{1,0:T(8,128)S(1)}, u32[]{:S(2)}, u32[]{:S(2)}) collective-permute-start(f32[8,256]{1,0:T(8,128)} %eig_ref), channel_id=1, source_target_pairs={{0,1},{1,0},{2,3},{3,2},{4,5},{5,4},{6,7},{7,6},{8,9},{9,8},{10,11... | collective-permute-start | bytes 24584 | tf_op jit(solution)/shard_map/ppermute | solution.py:315
  22.1 18.8 %collective-permute-start.4 = (f32[512,256]{1,0:T(8,128)S(1)}, f32[512,256]{1,0:T(8,128)S(1)}, u32[]{:S(2)}, u32[]{:S(2)}) collective-permute-start(f32[512,256]{1,0:T(8,128)S(1)} %bitcast.44), channel_id=1, source_target_pairs={{0,1},{1,0},{2,3},{3,2},{4,5},{5,4},{6,7},{7,6},{8,9},{9,8},{10,11... | collective-permute-start | bytes 1572872 | tf_op jit(solution)/shard_map/ppermute | solution.py:315
  26.4 2.7 %copy-start.3 = (f32[256,256]{1,0:T(8,128)S(1)}, f32[256,256]{1,0:T(8,128)}, u32[]{:S(2)}) copy-start(f32[256,256]{1,0:T(8,128)} %get-tuple-element.48) | copy-start | bytes 786436
  29.2 18.6 %collective-permute-start.3 = (f32[256,256]{1,0:T(8,128)S(1)}, f32[256,256]{1,0:T(8,128)S(1)}, u32[]{:S(2)}, u32[]{:S(2)}) collective-permute-start(f32[256,256]{1,0:T(8,128)S(1)} %copy-done.3), channel_id=1, source_target_pairs={{0,1},{1,0},{2,3},{3,2},{4,5},{5,4},{6,7},{7,6},{8,9},{9,8},{10,11... | collective-permute-start | bytes 786440 | tf_op jit(solution)/shard_map/ppermute | solution.py:315
  38.8 2.0 %copy-start = (f32[8,256,512]{2,1,0:T(8,128)}, f32[8,256,512]{2,1,0:T(8,128)S(1)}, u32[]{:S(2)}) copy-start(f32[8,256,512]{2,1,0:T(8,128)S(1)} %shard_map.96.acc_in) | copy-start | bytes 12582916
  40.8 10.0 %collective-permute-start.2 = (f32[256,256]{1,0:T(8,128)S(1)}, f32[256,256]{1,0:T(8,128)S(1)}, u32[]{:S(2)}, u32[]{:S(2)}) collective-permute-start(f32[256,256]{1,0:T(8,128)S(1)} %get-tuple-element.46), channel_id=1, source_target_pairs={{0,1},{1,0},{2,3},{3,2},{4,5},{5,4},{6,7},{7,6},{8,9},{9,8},{10,11... | collective-permute-start | bytes 786440 | tf_op jit(solution)/shard_map/ppermute | solution.py:315
  50.8 28.1 %copy-start.1 = (f32[1,128,256]{2,1,0:T(8,128)S(1)}, f32[1,128,256]{2,1,0:T(8,128)}, u32[]{:S(2)}) copy-start(f32[1,128,256]{2,1,0:T(8,128)} %stiff_ref.2) | copy-start | bytes 393220
  50.8 28.1 %copy-start.2 = (f32[1,128,256]{2,1,0:T(8,128)S(1)}, f32[1,128,256]{2,1,0:T(8,128)}, u32[]{:S(2)}) copy-start(f32[1,128,256]{2,1,0:T(8,128)} %mass_ref.2) | copy-start | bytes 393220
  52.2 2.0 %collective-permute-start.6 = (f32[4,128,256]{2,1,0:T(8,128)S(1)}, f32[4,128,256]{2,1,0:T(8,128)S(1)}, u32[]{:S(2)}, u32[]{:S(2)}) collective-permute-start(f32[4,128,256]{2,1,0:T(8,128)S(1)} %get-tuple-element.62), channel_id=1, source_target_pairs={{0,2},{2,0},{4,6},{6,4},{8,10},{10,8},{12,14},{14,12},{1,3},{3,1},... | collective-permute-start | bytes 1572872 | tf_op jit(solution)/shard_map/ppermute | solution.py:318
  52.3 6.5 %collective-permute-start.5 = (f32[4,144,256]{2,1,0:T(8,128)S(1)}, f32[4,144,256]{2,1,0:T(8,128)S(1)}, u32[]{:S(2)}, u32[]{:S(2)}) collective-permute-start(f32[4,144,256]{2,1,0:T(8,128)S(1)} %get-tuple-element.60), channel_id=1, source_target_pairs={{0,2},{2,0},{4,6},{6,4},{8,10},{10,8},{12,14},{14,12},{1,3},{3,1},... | collective-permute-start | bytes 1769480 | tf_op jit(solution)/shard_map/ppermute | solution.py:318
  54.3 10.4 %collective-permute-start.8 = (f32[128,256]{1,0:T(8,128)S(1)}, f32[128,256]{1,0:T(8,128)S(1)}, u32[]{:S(2)}, u32[]{:S(2)}) collective-permute-start(f32[128,256]{1,0:T(8,128)S(1)} %get-tuple-element.68), channel_id=1, source_target_pairs={{0,8},{2,10},{4,12},{6,14},{8,0},{10,2},{12,4},{14,6},{1,9},{3,11}... | collective-permute-start | bytes 393224 | tf_op jit(solution)/shard_map/ppermute | solution.py:318
  57.2 7.5 %collective-permute-start.10 = (f32[128,256]{1,0:T(8,128)S(1)}, f32[128,256]{1,0:T(8,128)S(1)}, u32[]{:S(2)}, u32[]{:S(2)}) collective-permute-start(f32[128,256]{1,0:T(8,128)S(1)} %get-tuple-element.69), channel_id=1, source_target_pairs={{0,4},{2,6},{4,0},{6,2},{8,12},{10,14},{12,8},{14,10},{1,5},{3,7},... | collective-permute-start | bytes 393224 | tf_op jit(solution)/shard_map/ppermute | solution.py:318
  58.8 9.1 %collective-permute-start.9 = (f32[128,256]{1,0:T(8,128)S(1)}, f32[128,256]{1,0:T(8,128)S(1)}, u32[]{:S(2)}, u32[]{:S(2)}) collective-permute-start(f32[128,256]{1,0:T(8,128)S(1)} %get-tuple-element.70), channel_id=1, source_target_pairs={{0,12},{2,14},{4,8},{6,10},{8,4},{10,6},{12,0},{14,2},{1,13},{3,15... | collective-permute-start | bytes 393224 | tf_op jit(solution)/shard_map/ppermute | solution.py:318
  58.8 9.0 %collective-permute-start.7 = (f32[4,72,256]{2,1,0:T(8,128)S(1)}, f32[4,72,256]{2,1,0:T(8,128)S(1)}, u32[]{:S(2)}, u32[]{:S(2)}) collective-permute-start(f32[4,72,256]{2,1,0:T(8,128)S(1)} %slice_add_fusion.1), channel_id=1, source_target_pairs={{0,1},{1,0},{2,3},{3,2},{4,5},{5,4},{6,7},{7,6},{8,9},{9,8},{10,11... | collective-permute-start | bytes 884744 | tf_op jit(solution)/shard_map/ppermute | solution.py:315
  68.0 6.4 %collective-permute-start.12 = (f32[72,256]{1,0:T(8,128)S(1)}, f32[72,256]{1,0:T(8,128)S(1)}, u32[]{:S(2)}, u32[]{:S(2)}) collective-permute-start(f32[72,256]{1,0:T(8,128)S(1)} %get-tuple-element.71), channel_id=1, source_target_pairs={{0,12},{2,14},{4,8},{6,10},{8,4},{10,6},{12,0},{14,2},{1,13},{3,15... | collective-permute-start | bytes 221192 | tf_op jit(solution)/shard_map/ppermute | solution.py:318
  71.1 4.7 %collective-permute-start.14 = (f32[72,256]{1,0:T(8,128)S(1)}, f32[72,256]{1,0:T(8,128)S(1)}, u32[]{:S(2)}, u32[]{:S(2)}) collective-permute-start(f32[72,256]{1,0:T(8,128)S(1)} %get-tuple-element.72), channel_id=1, source_target_pairs={{0,4},{2,6},{4,0},{6,2},{8,12},{10,14},{12,8},{14,10},{1,5},{3,7},... | collective-permute-start | bytes 221192 | tf_op jit(solution)/shard_map/ppermute | solution.py:318
  72.8 6.0 %collective-permute-start.13 = (f32[72,256]{1,0:T(8,128)S(1)}, f32[72,256]{1,0:T(8,128)S(1)}, u32[]{:S(2)}, u32[]{:S(2)}) collective-permute-start(f32[72,256]{1,0:T(8,128)S(1)} %get-tuple-element.73), channel_id=1, source_target_pairs={{0,8},{2,10},{4,12},{6,14},{8,0},{10,2},{12,4},{14,6},{1,9},{3,11}... | collective-permute-start | bytes 221192 | tf_op jit(solution)/shard_map/ppermute | solution.py:318
  72.8 6.0 %collective-permute-start.11 = (f32[128,256]{1,0:T(8,128)S(1)}, f32[128,256]{1,0:T(8,128)S(1)}, u32[]{:S(2)}, u32[]{:S(2)}) collective-permute-start(f32[128,256]{1,0:T(8,128)S(1)} %fusion.3.mine), channel_id=1, source_target_pairs={{0,1},{1,0},{2,3},{3,2},{4,5},{5,4},{6,7},{7,6},{8,9},{9,8},{10,11... | collective-permute-start | bytes 393224 | tf_op jit(solution)/shard_map/ppermute | solution.py:315
